TPU v7x, 256 devices: a whole 4x4x8 slice. The times are simulated.
256 devices in a mesh: atom: 64 (over y, z, core), col: 4 (over x).
Axes of the slice: x: 4, y: 4, z: 8, core: 2. Of those that a mesh axis runs over, the one named last changes fastest.
Arguments:
- atom_single: bfloat16 [32768, 128], P('atom'), may hold values from -6 to 6
- positions: float32 [3, 32768], P(None, 'atom'), may hold values from -96 to 96
- noise_index: int32 [1], replicated, may hold values from 0 to 199
- token_counts: int32 [2048], P('atom'), may hold values from 1 to 256, as said below
- token_single: bfloat16 [2048, 768], P('atom'), may hold values from -6 to 6
- pair_repr: bfloat16 [2048, 2048, 128], P('atom', 'col')
- w_pos: float32 [3, 128], replicated, may hold values from -3.5 to 3.5
- atom_wq: bfloat16 [128, 128], replicated
- atom_wk: bfloat16 [128, 128], replicated
- atom_wv: bfloat16 [128, 128], replicated, may hold values from -0.5 to 0.5
- atom_wo: bfloat16 [128, 128], replicated, may hold values from -0.5 to 0.5
- w_pool: bfloat16 [128, 768], replicated, may hold values from -0.5 to 0.5
- trans_w1: bfloat16 [128, 512], replicated, may hold values from -0.5 to 0.5
- trans_w2: bfloat16 [256, 128], replicated, may hold values from -0.375 to 0.375
- w_bias: bfloat16 [128, 16], replicated, may hold values from -1.5 to 1.5
- token_wq: bfloat16 [768, 768], P(None, 'col')
- token_wk: bfloat16 [768, 768], P(None, 'col')
- token_wv: bfloat16 [768, 768], P(None, 'col'), may hold values from -0.21875 to 0.21875
- token_wo: bfloat16 [768, 768], P('col'), may hold values from -0.21875 to 0.21875
- w_back: bfloat16 [768, 128], replicated, may hold values from -0.21875 to 0.21875
Outputs:
- atom_out: bfloat16 [32768, 128], P('atom')
- pair_out: bfloat16 [2048, 2048, 128], P('atom', 'col')
Inputs may be any that keep to these rules, and one draw needn't show every extreme that they name: `token_counts`: tokens form aligned runs of 32; the counts of one run sum to at most 512, and to exactly 512 in at least one run; some token has exactly 256 atoms.
All inputs are finite; a program needn't handle non-finite values.
Results may differ from a plain program's by a relative error of at most 0.018.
Values may be sent and summed in bfloat16 or wider, within the bound.
No kernel may reach another device: no remote copies, remote signals or barrier semaphores. Data moves between devices by JAX's collectives and lax.ppermute only.
A program may use at most 64 MiB of HBM per device.

v0:
```python
import math

import jax
import jax.numpy as jnp
from jax import lax
from jax.sharding import PartitionSpec as P

H_A = 4
H_T = 16
WIN_Q = 32
WIN_K = 128
STEPS = 200


EPS = 1e-05
SIGMA_DATA = 16.0
SIGMA_MAX = 160.0
SIGMA_MIN = 0.0004
RHO = 7.0
MASKED = -1000000000.0


def padded(array, sides, width):
    for axis, dim in sides:
        devices, length = (lax.axis_size(axis), array.shape[dim])
        up = [(i, (i + 1) % devices) for i in range(devices - 1)]
        down = [(j, i) for i, j in up]
        last = lax.slice_in_dim(array, length - width, length, axis=dim)
        initial = lax.slice_in_dim(array, 0, width, axis=dim)
        before = lax.ppermute(last, axis, up)
        after = lax.ppermute(initial, axis, down)
        array = jnp.concatenate([before, array, after], axis=dim)
    return array


def normalize(values):
    average = jnp.mean(values, axis=-1, keepdims=True)
    centred = values - average
    variance = jnp.mean(centred * centred, axis=-1, keepdims=True)
    return centred * lax.rsqrt(variance + EPS)


def noise_scale(noise_index):
    level = noise_index[0].astype(jnp.float32)
    upper = SIGMA_MAX ** (1.0 / RHO)
    lower = SIGMA_MIN ** (1.0 / RHO)
    sigma_now = (upper + level / (STEPS - 1) * (lower - upper)) ** RHO
    return 1.0 / jnp.sqrt(sigma_now * sigma_now + SIGMA_DATA * SIGMA_DATA)


def pair_block(pair_rows, trans_w1, trans_w2, w_bias):
    row_count, col_count, channels = pair_rows.shape
    flattened = pair_rows.reshape(row_count * col_count, channels).astype(jnp.float32)
    normed_in = normalize(flattened).astype(jnp.bfloat16)
    gate_up = jnp.dot(normed_in, trans_w1, preferred_element_type=jnp.float32)
    half_width = gate_up.shape[1] // 2
    hidden = (jax.nn.silu(gate_up[:, :half_width]) * gate_up[:, half_width:]).astype(jnp.bfloat16)
    updated = flattened + jnp.dot(hidden, trans_w2, preferred_element_type=jnp.float32)
    normed_out = normalize(updated).astype(jnp.bfloat16)
    head_bias = lax.dot_general(
        w_bias, normed_out, (((0,), (1,)), ((), ())), preferred_element_type=jnp.float32
    )
    head_bias = head_bias.astype(jnp.bfloat16).reshape(-1, row_count, col_count)
    return (updated.astype(jnp.bfloat16).reshape(row_count, col_count, channels), head_bias)


def window_attention(queries, padded_kv, padded_live, head_count):
    length, feat_width = queries.shape
    windows = length // WIN_Q
    key_blocks = WIN_K // WIN_Q
    head_size = feat_width // head_count
    blocks = padded_kv.reshape(windows + key_blocks - 1, WIN_Q, 2 * feat_width)
    key_marks = padded_live.reshape(windows + key_blocks - 1, WIN_Q)
    key_rows = jnp.concatenate(
        [blocks[offset : offset + windows] for offset in range(key_blocks)], axis=1
    )
    alive_keys = jnp.concatenate(
        [key_marks[offset : offset + windows] for offset in range(key_blocks)], axis=1
    )
    query_part = queries.reshape(windows, WIN_Q, head_count, head_size)
    key_part = key_rows[:, :, :feat_width].reshape(windows, WIN_K, head_count, head_size)
    value_part = key_rows[:, :, feat_width:].reshape(windows, WIN_K, head_count, head_size)
    scores = jnp.einsum(
        "wqhd,wkhd->whqk", query_part, key_part, preferred_element_type=jnp.float32
    ) / math.sqrt(head_size)
    penalty = jnp.where(alive_keys > 0, jnp.float32(0.0), jnp.float32(MASKED))
    scores = scores + penalty[:, None, None, :]
    weights = jax.nn.softmax(scores, axis=-1).astype(jnp.bfloat16)
    mixture = jnp.einsum("whqk,wkhd->wqhd", weights, value_part, preferred_element_type=jnp.float32)
    return mixture.astype(jnp.bfloat16).reshape(length, feat_width)


def local(
    atom_single,
    positions,
    noise_index,
    token_counts,
    token_single,
    pair_repr,
    w_pos,
    atom_wq,
    atom_wk,
    atom_wv,
    atom_wo,
    w_pool,
    trans_w1,
    trans_w2,
    w_bias,
    token_wq,
    token_wk,
    token_wv,
    token_wo,
    w_back,
):
    highest = lax.Precision.HIGHEST
    tok_rows = token_counts.shape[0]
    slot_total = atom_single.shape[0]
    token_ends = jnp.cumsum(token_counts)
    slot_ids = jnp.arange(slot_total, dtype=jnp.int32)
    owner_token = jnp.sum((slot_ids[:, None] >= token_ends[None, :]).astype(jnp.int32), axis=1)
    alive_slot = slot_ids < token_ends[-1]
    onehot = (owner_token[:, None] == jnp.arange(tok_rows, dtype=jnp.int32)[None, :]).astype(
        jnp.float32
    )
    noise_gain = noise_scale(noise_index)
    lifted = lax.dot_general(
        positions * noise_gain, w_pos, (((0,), (0,)), ((), ())), precision=highest
    )
    initial = atom_single.astype(jnp.float32) + lifted
    normed = normalize(initial).astype(jnp.bfloat16)
    queries = jnp.dot(normed, atom_wq, preferred_element_type=jnp.float32).astype(jnp.bfloat16)
    keyvals = jnp.dot(
        normed, jnp.concatenate([atom_wk, atom_wv], axis=1), preferred_element_type=jnp.float32
    ).astype(jnp.bfloat16)
    margin = (WIN_K - WIN_Q) // 2
    padded_kv, padded_live = (
        padded(keyvals, (("atom", 0),), margin),
        padded(alive_slot.astype(jnp.bfloat16), (("atom", 0),), margin),
    )
    mixture = window_attention(queries, padded_kv, padded_live, H_A)
    atom_state = initial + jnp.dot(mixture, atom_wo, preferred_element_type=jnp.float32)
    features = jax.nn.relu(
        jnp.dot(atom_state.astype(jnp.bfloat16), w_pool, preferred_element_type=jnp.float32)
    )
    token_sums = lax.dot_general(onehot, features, (((0,), (0,)), ((), ())), precision=highest)
    pooled = token_sums / token_counts.astype(jnp.float32)[:, None]
    token_in = token_single.astype(jnp.float32) + pooled
    token_normed = normalize(token_in).astype(jnp.bfloat16)
    col_count = pair_repr.shape[1]
    rows_per = math.gcd(tok_rows, 8)

    def process(pair_rows):
        return pair_block(pair_rows, trans_w1, trans_w2, w_bias)

    pair_out, pair_bias = lax.map(
        process, pair_repr.reshape(tok_rows // rows_per, rows_per, col_count, pair_repr.shape[2])
    )
    pair_out = pair_out.reshape(tok_rows, col_count, pair_repr.shape[2])
    pair_bias = pair_bias.transpose(1, 0, 2, 3).reshape(H_T, tok_rows, col_count)
    head_bias = lax.all_to_all(pair_bias, "col", split_axis=0, concat_axis=2, tiled=True)
    local_heads = head_bias.shape[0]
    shard_width = token_wq.shape[1]
    head_size = shard_width // local_heads
    token_queries = jnp.dot(token_normed, token_wq, preferred_element_type=jnp.float32).astype(
        jnp.bfloat16
    )
    key_weights = jnp.concatenate([token_wk, token_wv], axis=1)
    token_kv = jnp.dot(
        lax.all_gather(token_normed, "atom", axis=0, tiled=True),
        key_weights,
        preferred_element_type=jnp.float32,
    ).astype(jnp.bfloat16)
    query_part = token_queries.reshape(tok_rows, local_heads, head_size)
    key_part = token_kv[:, :shard_width].reshape(-1, local_heads, head_size)
    value_part = token_kv[:, shard_width:].reshape(-1, local_heads, head_size)
    scores = jnp.einsum(
        "ihd,jhd->hij", query_part, key_part, preferred_element_type=jnp.float32
    ) / math.sqrt(head_size)
    scores = scores + head_bias.astype(jnp.float32)
    weights = jax.nn.softmax(scores, axis=-1).astype(jnp.bfloat16)
    token_mix = jnp.einsum("hij,jhd->ihd", weights, value_part, preferred_element_type=jnp.float32)
    token_mix = token_mix.astype(jnp.bfloat16).reshape(tok_rows, shard_width)
    partial_out = jnp.dot(token_mix, token_wo, preferred_element_type=jnp.float32)
    token_new = token_in + lax.psum(partial_out.astype(jnp.bfloat16), "col").astype(jnp.float32)
    returned = jnp.dot(token_new.astype(jnp.bfloat16), w_back, preferred_element_type=jnp.float32)
    spread = jnp.dot(onehot, returned, precision=highest)
    atom_out = jnp.where(alive_slot[:, None], atom_state + spread, jnp.float32(0.0))
    return (atom_out.astype(jnp.bfloat16), pair_out)


def solution(mesh):
    placed = (
        P("atom", None),
        P(None, "atom"),
        P(),
        P("atom"),
        P("atom", None),
        P("atom", "col", None),
        P(),
        P(),
        P(),
        P(),
        P(),
        P(),
        P(),
        P(),
        P(),
        P(None, "col"),
        P(None, "col"),
        P(None, "col"),
        P("col", None),
        P(),
    )
    return jax.shard_map(
        local,
        mesh=mesh,
        in_specs=placed,
        out_specs=(P("atom", None), P("atom", "col", None)),
        check_vma=False,
    )
```

profile of v0, /device:TPU:1, one launch (start us, length us, event | category | flops | bytes accessed | tf_op | source)
XLA Modules:
  0.0 148.3 jit_solution(4082003843184654483)
XLA Ops:
  11.3 4.9 %collective-permute-start = (bf16[48,256]{1,0:T(8,128)(2,1)S(1)}, bf16[48,256]{1,0:T(8,128)(2,1)S(1)}, u32[]{:S(2)}, u32[]{:S(2)}) collective-permute-start(bf16[48,256]{1,0:T(8,128)(2,1)S(1)} %get-tuple-element.78), channel_id=1, source_target_pairs={{0,4},{4,8},{8,12},{12,16},{16,20},{20,24},{24,28},{28,32},{32,36}... | collective-permute-start | bytes 73736 | tf_op jit(solution)/shard_map/ppermute | solution.py:30
  16.2 1.9 %collective-permute-start.1 = (bf16[48,256]{1,0:T(8,128)(2,1)S(1)}, bf16[48,256]{1,0:T(8,128)(2,1)S(1)}, u32[]{:S(2)}, u32[]{:S(2)}) collective-permute-start(bf16[48,256]{1,0:T(8,128)(2,1)S(1)} %get-tuple-element.79), channel_id=1, source_target_pairs={{4,0},{8,4},{12,8},{16,12},{20,16},{24,20},{28,24},{32,28},{36,32}... | collective-permute-start | bytes 73736 | tf_op jit(solution)/shard_map/ppermute | solution.py:31
  20.1 3.6 %collective-permute-start.2 = (bf16[48]{0:T(256)(128)(2,1)S(1)}, bf16[48]{0:T(256)(128)(2,1)S(1)}, u32[]{:S(2)}, u32[]{:S(2)}) collective-permute-start(bf16[48]{0:T(256)(128)(2,1)S(1)} %get-tuple-element.86), channel_id=1, source_target_pairs={{0,4},{4,8},{8,12},{12,16},{16,20},{20,24},{24,28},{28,32},{32,36}... | collective-permute-start | bytes 296 | tf_op jit(solution)/shard_map/ppermute | solution.py:30
  23.7 1.9 %collective-permute-start.3 = (bf16[48]{0:T(256)(128)(2,1)S(1)}, bf16[48]{0:T(256)(128)(2,1)S(1)}, u32[]{:S(2)}, u32[]{:S(2)}) collective-permute-start(bf16[48]{0:T(256)(128)(2,1)S(1)} %get-tuple-element.87), channel_id=1, source_target_pairs={{4,0},{8,4},{12,8},{16,12},{20,16},{24,20},{28,24},{32,28},{36,32}... | collective-permute-start | bytes 296 | tf_op jit(solution)/shard_map/ppermute | solution.py:31
  31.2 3.6 %fusion.19 = bf16[16,32,4,32]{1,3,2,0:T(8,128)(2,1)S(1)} fusion(bf16[16,128,4,32]{1,3,2,0:T(8,128)(2,1)S(1)} %bitcast.123, f32[16,4,32]{2,1,0:T(4,128)S(1)} %fusion.63, f32[16,4,32,128]{3,2,1,0:T(8,128)S(1)} %fusion.18), kind=kOutput, calls=%fused_computation.37 | convolution fusion | flops 17631360 | bytes 1712128 | tf_op jit(solution)/shard_map/whqk,wkhd->wqhd/dot_general | solution.py:89
  38.2 60.6 %while.12 = (s32[]{:T(128)}, bf16[4,8,512,128]{3,2,1,0:T(8,128)(2,1)}, bf16[4,16,8,512]{3,2,0,1:T(8,128)(2,1)}, bf16[4,8,512,128]{3,2,1,0:T(8,128)(2,1)}, bf16[1...) while((s32[]{:T(128)}, ...), condition=%wide.region_13.14_spmd, body=%wide.region_8.13_spmd.sunk | while | flops 838934528 | bytes 37934180 | solution.py:155
  38.2 1.6 %convert_reduce_fusion.3 = f32[8,512]{1,0:T(8,128)S(1)} fusion(bf16[4,8,512,128]{3,2,1,0:T(8,128)(2,1)} %get-tuple-element.168, s32[]{:T(128)} %get-tuple-element.157), kind=kLoop, calls=%fused_computation.10.clone.1 | loop fusion | flops 1044480 | bytes 1064964 | tf_op jit(solution)/shard_map/while/body/eval_jaxpr/reduce_sum | solution.py:37
  39.8 2.3 %multiply_reduce_fusion.6 = f32[8,512]{1,0:T(8,128)S(1)} fusion(f32[8,512]{1,0:T(8,128)S(1)} %get-tuple-element.143, bf16[4,8,512,128]{3,2,1,0:T(8,128)(2,1)} %get-tuple-element.168, s32[]{:T(128)} %get-tuple-element.157), kind=kLoop, calls=%fused_computation.9.clone.1 | loop fusion | flops 2093056 | bytes 1081348 | tf_op jit(solution)/shard_map/while/body/eval_jaxpr/reduce_sum | solution.py:39
  42.2 2.3 %fusion.105 = bf16[4096,128]{1,0:T(8,128)(2,1)S(1)} fusion(f32[4096]{0:T(1024)S(1)} %bitcast.116, f32[4096]{0:T(1024)S(1)} %bitcast.117, bf16[4,8,512,128]{3,2,1,0:T(8,128)(2,1)} %get-tuple-element.168, s32[]{:T(128)} %get-tuple-element.157), kind=kLoop, calls=%fused_computation.6.clone.1 | loop fusion | flops 2097152 | bytes 2129924 | tf_op jit(solution)/shard_map/while/body/eval_jaxpr/convert_element_type | solution.py:54
  47.1 1.6 %fusion.107 = (f32[4096]{0:T(1024)S(1)}, f32[4096,128]{1,0:T(8,128)S(1)}) fusion(f32[4096,128]{1,0:T(8,128)S(1)} %bitcast.109, bf16[256,128]{1,0:T(8,128)(2,1)S(1)} %get-tuple-element.170, f32[4096,512]{1,0:T(8,128)S(1)} %fusion.106), kind=kOutput, calls=%fused_computation.103.clone.1 | convolution fusion | flops 275771392 | bytes 12664832 | tf_op jit(solution)/shard_map/while/body/eval_jaxpr/dot_general | solution.py:58
  54.9 2.4 %multiply_reduce_fusion.6 = f32[8,512]{1,0:T(8,128)S(1)} fusion(f32[8,512]{1,0:T(8,128)S(1)} %get-tuple-element.143, bf16[4,8,512,128]{3,2,1,0:T(8,128)(2,1)} %get-tuple-element.168, s32[]{:T(128)} %get-tuple-element.157), kind=kLoop, calls=%fused_computation.9.clone.1 | loop fusion | flops 2093056 | bytes 1081348 | tf_op jit(solution)/shard_map/while/body/eval_jaxpr/reduce_sum | solution.py:39
  57.3 2.3 %fusion.105 = bf16[4096,128]{1,0:T(8,128)(2,1)S(1)} fusion(f32[4096]{0:T(1024)S(1)} %bitcast.116, f32[4096]{0:T(1024)S(1)} %bitcast.117, bf16[4,8,512,128]{3,2,1,0:T(8,128)(2,1)} %get-tuple-element.168, s32[]{:T(128)} %get-tuple-element.157), kind=kLoop, calls=%fused_computation.6.clone.1 | loop fusion | flops 2097152 | bytes 2129924 | tf_op jit(solution)/shard_map/while/body/eval_jaxpr/convert_element_type | solution.py:54
  62.2 1.6 %fusion.107 = (f32[4096]{0:T(1024)S(1)}, f32[4096,128]{1,0:T(8,128)S(1)}) fusion(f32[4096,128]{1,0:T(8,128)S(1)} %bitcast.109, bf16[256,128]{1,0:T(8,128)(2,1)S(1)} %get-tuple-element.170, f32[4096,512]{1,0:T(8,128)S(1)} %fusion.106), kind=kOutput, calls=%fused_computation.103.clone.1 | convolution fusion | flops 275771392 | bytes 12664832 | tf_op jit(solution)/shard_map/while/body/eval_jaxpr/dot_general | solution.py:58
  70.0 2.3 %multiply_reduce_fusion.6 = f32[8,512]{1,0:T(8,128)S(1)} fusion(f32[8,512]{1,0:T(8,128)S(1)} %get-tuple-element.143, bf16[4,8,512,128]{3,2,1,0:T(8,128)(2,1)} %get-tuple-element.168, s32[]{:T(128)} %get-tuple-element.157), kind=kLoop, calls=%fused_computation.9.clone.1 | loop fusion | flops 2093056 | bytes 1081348 | tf_op jit(solution)/shard_map/while/body/eval_jaxpr/reduce_sum | solution.py:39
  72.4 2.3 %fusion.105 = bf16[4096,128]{1,0:T(8,128)(2,1)S(1)} fusion(f32[4096]{0:T(1024)S(1)} %bitcast.116, f32[4096]{0:T(1024)S(1)} %bitcast.117, bf16[4,8,512,128]{3,2,1,0:T(8,128)(2,1)} %get-tuple-element.168, s32[]{:T(128)} %get-tuple-element.157), kind=kLoop, calls=%fused_computation.6.clone.1 | loop fusion | flops 2097152 | bytes 2129924 | tf_op jit(solution)/shard_map/while/body/eval_jaxpr/convert_element_type | solution.py:54
  77.3 1.6 %fusion.107 = (f32[4096]{0:T(1024)S(1)}, f32[4096,128]{1,0:T(8,128)S(1)}) fusion(f32[4096,128]{1,0:T(8,128)S(1)} %bitcast.109, bf16[256,128]{1,0:T(8,128)(2,1)S(1)} %get-tuple-element.170, f32[4096,512]{1,0:T(8,128)S(1)} %fusion.106), kind=kOutput, calls=%fused_computation.103.clone.1 | convolution fusion | flops 275771392 | bytes 12664832 | tf_op jit(solution)/shard_map/while/body/eval_jaxpr/dot_general | solution.py:58
  85.1 2.3 %multiply_reduce_fusion.6 = f32[8,512]{1,0:T(8,128)S(1)} fusion(f32[8,512]{1,0:T(8,128)S(1)} %get-tuple-element.143, bf16[4,8,512,128]{3,2,1,0:T(8,128)(2,1)} %get-tuple-element.168, s32[]{:T(128)} %get-tuple-element.157), kind=kLoop, calls=%fused_computation.9.clone.1 | loop fusion | flops 2093056 | bytes 1081348 | tf_op jit(solution)/shard_map/while/body/eval_jaxpr/reduce_sum | solution.py:39
  87.5 2.3 %fusion.105 = bf16[4096,128]{1,0:T(8,128)(2,1)S(1)} fusion(f32[4096]{0:T(1024)S(1)} %bitcast.116, f32[4096]{0:T(1024)S(1)} %bitcast.117, bf16[4,8,512,128]{3,2,1,0:T(8,128)(2,1)} %get-tuple-element.168, s32[]{:T(128)} %get-tuple-element.157), kind=kLoop, calls=%fused_computation.6.clone.1 | loop fusion | flops 2097152 | bytes 2129924 | tf_op jit(solution)/shard_map/while/body/eval_jaxpr/convert_element_type | solution.py:54
  92.5 1.6 %fusion.107 = (f32[4096]{0:T(1024)S(1)}, f32[4096,128]{1,0:T(8,128)S(1)}) fusion(f32[4096,128]{1,0:T(8,128)S(1)} %bitcast.109, bf16[256,128]{1,0:T(8,128)(2,1)S(1)} %get-tuple-element.170, f32[4096,512]{1,0:T(8,128)S(1)} %fusion.106), kind=kOutput, calls=%fused_computation.103.clone.1 | convolution fusion | flops 275771392 | bytes 12664832 | tf_op jit(solution)/shard_map/while/body/eval_jaxpr/dot_general | solution.py:58
  98.7 4.2 %all-to-all-start = ((bf16[16,32,512]{2,1,0:T(8,128)(2,1)}), bf16[16,32,512]{2,1,0:T(8,128)(2,1)S(1)}, u32[]{:S(2)}, u32[]{:S(2)}) async-start(bf16[16,32,512]{2,1,0:T(8,128)(2,1)} %bitcast.17), calls=%async_computation | async-start | bytes 1048576 | tf_op jit(solution)/shard_map/all_to_all | solution.py:160
  104.4 6.9 %all-to-all-done = bf16[16,32,512]{2,1,0:T(8,128)(2,1)S(1)} async-done(((bf16[16,32,512]{2,1,0:T(8,128)(2,1)}), bf16[16,32,512]{2,1,0:T(8,128)(2,1)S(1)}, u32[]{:S(2)}, u32[]{:S(2)}) %all-to-all-start) | async-done | bytes 524320 | tf_op jit(solution)/shard_map/all_to_all | solution.py:160
  111.6 9.5 %all-gather.2.cloned.1.call-done = bf16[2048,768]{1,0:T(8,128)(2,1)} async-done(((bf16[32,768]{1,0:T(8,128)(2,1)}), bf16[2048,768]{1,0:T(8,128)(2,1)}) %all-gather.2.cloned.1.call-update) | async-done | bytes 3145744 | tf_op jit(solution)/shard_map/all_gather | solution.py:169
  121.1 3.3 %convolution_convert_fusion.1 = bf16[2048,384]{0,1:T(8,128)(2,1)S(1)} fusion(bf16[2048,768]{1,0:T(8,128)(2,1)} %all-gather.2.cloned.1.call-done, bf16[768,192]{0,1:T(8,128)(2,1)S(1)} %copy-done.10, bf16[768,192]{0,1:T(8,128)(2,1)S(1)} %copy-done.11), kind=kOutput, calls=%fused_computation.25 | convolution fusion | flops 1209925632 | bytes 5308416 | tf_op jit(solution)/shard_map/dot_general | solution.py:168
  126.5 13.5 %psum.7 = bf16[32,768]{1,0:T(8,128)(2,1)S(1)} all-reduce(bf16[32,768]{1,0:T(8,128)(2,1)S(1)} %convolution_convert_fusion.5), channel_id=1, replica_groups=mesh['atom'=64,'col'=4] {'col'}, use_global_device_ids=true, to_apply=%region_16.17 | all-reduce | flops 24576 | bytes 98304 | tf_op jit(solution)/shard_map/psum | solution.py:184
  (144 shorter events, 52.6 us)
Async XLA Ops:
  7.2 119.2 %copy-start = (bf16[192,768]{1,0:T(8,128)(2,1)S(1)}, bf16[192,768]{1,0:T(8,128)(2,1)}, u32[]{:S(2)}) copy-start(bf16[192,768]{1,0:T(8,128)(2,1)} %param.40) | copy-start | bytes 884740
  7.2 113.9 %all-gather.2.cloned.1.call-start = ((), (), s32[]{:S(2)}) async-start(), calls=%async_computation.1 | async-start | bytes 3194880 | tf_op jit(solution)/shard_map/all_gather | solution.py:169
  11.3 17.9 %collective-permute-start = (bf16[48,256]{1,0:T(8,128)(2,1)S(1)}, bf16[48,256]{1,0:T(8,128)(2,1)S(1)}, u32[]{:S(2)}, u32[]{:S(2)}) collective-permute-start(bf16[48,256]{1,0:T(8,128)(2,1)S(1)} %get-tuple-element.78), channel_id=1, source_target_pairs={{0,4},{4,8},{8,12},{12,16},{16,20},{20,24},{24,28},{28,32},{32,36}... | collective-permute-start | bytes 73736 | tf_op jit(solution)/shard_map/ppermute | solution.py:30
  16.2 13.0 %collective-permute-start.1 = (bf16[48,256]{1,0:T(8,128)(2,1)S(1)}, bf16[48,256]{1,0:T(8,128)(2,1)S(1)}, u32[]{:S(2)}, u32[]{:S(2)}) collective-permute-start(bf16[48,256]{1,0:T(8,128)(2,1)S(1)} %get-tuple-element.79), channel_id=1, source_target_pairs={{4,0},{8,4},{12,8},{16,12},{20,16},{24,20},{28,24},{32,28},{36,32}... | collective-permute-start | bytes 73736 | tf_op jit(solution)/shard_map/ppermute | solution.py:31
  20.1 7.7 %collective-permute-start.2 = (bf16[48]{0:T(256)(128)(2,1)S(1)}, bf16[48]{0:T(256)(128)(2,1)S(1)}, u32[]{:S(2)}, u32[]{:S(2)}) collective-permute-start(bf16[48]{0:T(256)(128)(2,1)S(1)} %get-tuple-element.86), channel_id=1, source_target_pairs={{0,4},{4,8},{8,12},{12,16},{16,20},{20,24},{24,28},{28,32},{32,36}... | collective-permute-start | bytes 296 | tf_op jit(solution)/shard_map/ppermute | solution.py:30
  23.7 4.9 %collective-permute-start.3 = (bf16[48]{0:T(256)(128)(2,1)S(1)}, bf16[48]{0:T(256)(128)(2,1)S(1)}, u32[]{:S(2)}, u32[]{:S(2)}) collective-permute-start(bf16[48]{0:T(256)(128)(2,1)S(1)} %get-tuple-element.87), channel_id=1, source_target_pairs={{4,0},{8,4},{12,8},{16,12},{20,16},{24,20},{28,24},{32,28},{36,32}... | collective-permute-start | bytes 296 | tf_op jit(solution)/shard_map/ppermute | solution.py:31
  31.1 4.5 %copy-start.9 = (bf16[128,128]{1,0:T(8,128)(2,1)S(1)}, bf16[128,128]{1,0:T(8,128)(2,1)}, u32[]{:S(2)}) copy-start(bf16[128,128]{1,0:T(8,128)(2,1)} %param.32) | copy-start | bytes 98308
  34.8 1.1 copy-start.5
  34.8 1.5 %copy-start.8 = (bf16[32,768]{1,0:T(8,128)(2,1)S(1)}, bf16[32,768]{1,0:T(8,128)(2,1)}, u32[]{:S(2)}) copy-start(bf16[32,768]{1,0:T(8,128)(2,1)} %param.26) | copy-start | bytes 147460
  35.9 2.2 %copy-start.1 = (bf16[128,512]{1,0:T(8,128)(2,1)S(1)}, bf16[128,512]{1,0:T(8,128)(2,1)}, u32[]{:S(2)}) copy-start(bf16[128,512]{1,0:T(8,128)(2,1)} %param.34) | copy-start | bytes 393220
  35.9 2.2 %copy-start.7 = (bf16[128,16]{0,1:T(8,128)(2,1)S(1)}, bf16[128,16]{0,1:T(8,128)(2,1)}, u32[]{:S(2)}) copy-start(bf16[128,16]{0,1:T(8,128)(2,1)} %param.36) | copy-start | bytes 12292
  35.9 2.2 %copy-start.12 = (bf16[256,128]{1,0:T(8,128)(2,1)S(1)}, bf16[256,128]{1,0:T(8,128)(2,1)}, u32[]{:S(2)}) copy-start(bf16[256,128]{1,0:T(8,128)(2,1)} %param.35) | copy-start | bytes 196612
  38.1 65.4 %copy-start.2 = (bf16[32,768]{1,0:T(8,128)(2,1)S(1)}, bf16[32,768]{1,0:T(8,128)(2,1)}, u32[]{:S(2)}) copy-start(bf16[32,768]{1,0:T(8,128)(2,1)} %multiply_convert_fusion.3) | copy-start | bytes 147460
  38.1 65.4 %copy-start.3 = (bf16[768,192]{0,1:T(8,128)(2,1)S(1)}, bf16[768,192]{0,1:T(8,128)(2,1)}, u32[]{:S(2)}) copy-start(bf16[768,192]{0,1:T(8,128)(2,1)} %param.37) | copy-start | bytes 884740
  98.7 12.7 %all-to-all-start = ((bf16[16,32,512]{2,1,0:T(8,128)(2,1)}), bf16[16,32,512]{2,1,0:T(8,128)(2,1)S(1)}, u32[]{:S(2)}, u32[]{:S(2)}) async-start(bf16[16,32,512]{2,1,0:T(8,128)(2,1)} %bitcast.17), calls=%async_computation | async-start | bytes 1048576 | tf_op jit(solution)/shard_map/all_to_all | solution.py:160
  102.9 18.2 %copy-start.10 = (bf16[768,192]{0,1:T(8,128)(2,1)S(1)}, bf16[768,192]{0,1:T(8,128)(2,1)}, u32[]{:S(2)}) copy-start(bf16[768,192]{0,1:T(8,128)(2,1)} %param.39) | copy-start | bytes 884740
  102.9 18.2 %copy-start.11 = (bf16[768,192]{0,1:T(8,128)(2,1)S(1)}, bf16[768,192]{0,1:T(8,128)(2,1)}, u32[]{:S(2)}) copy-start(bf16[768,192]{0,1:T(8,128)(2,1)} %param.38) | copy-start | bytes 884740
  124.4 0.8 copy-start.6
  125.8 14.3 %copy-start.4 = (bf16[768,128]{1,0:T(8,128)(2,1)S(1)}, bf16[768,128]{1,0:T(8,128)(2,1)}, u32[]{:S(2)}) copy-start(bf16[768,128]{1,0:T(8,128)(2,1)} %param.41) | copy-start | bytes 589828
Sparse Core Ops, SparseCore 0:
  38.2 82.8 all-gather.1
where the time goes:
time: 151 us; the launch traced here: 148 us
  other arithmetic  40.2 us (27%)
  matrix products  30.7 us (20%)
  waiting for transfers between devices  17.3 us (11%)
  starting transfers between devices  16.6 us (11%)
  between operations  15.2 us (10%)
  local copies, waits for them, and re-layouts  14.4 us (10%)
  blocking collectives  13.5 us (9%)
    reduce_sum x10, other arithmetic, normalize(): variance = jnp.mean(centred * centred, axis=-1, keepdims=True)  14.8 us
    psum x1, blocking collectives, local(): lax.psum(partial_out.astype(jnp.bfloat16), 'col').astype(jnp.float32)  13.5 us
    all_gather x1, waiting for transfers between devices, local(): lax.all_gather(token_normed, 'atom', axis=0, tiled=True)  9.51 us
    convert_element_type x4, other arithmetic, pair_block(): normed_in = normalize(flattened).astype(jnp.bfloat16)  9.17 us
    ppermute x2, starting transfers between devices, padded(): before = lax.ppermute(last, axis, up)  8.57 us
    dynamic_update_slice x8, local copies, waits for them, and re-layouts, local(): lax.map(process, pair_repr.reshape(tok_rows // rows_per, rows_per, col_co...  6.95 us
    all_to_all x1, waiting for transfers between devices, local(): lax.all_to_all(pair_bias, 'col', split_axis=0, concat_axis=2, tiled=True)  6.94 us
    dot_general x4, matrix products, pair_block(): jnp.dot(hidden, trans_w2, preferred_element_type=jnp.float32)  6.46 us
  transfers between devices with their start and end apart: 6, of which 3 were waited for; matrix products, arithmetic and copies ran while one was open for 45% of the time, Pallas kernels for 0%

commit v1 on v0

v1 whole, which is shorter than its diff:
```python
import math

import jax
import jax.numpy as jnp
from jax import lax
from jax.experimental import pallas as pl
from jax.experimental.pallas import tpu as pltpu
from jax.sharding import PartitionSpec as P

H_A = 4
H_T = 16
WIN_Q = 32
WIN_K = 128
MARGIN = (WIN_K - WIN_Q) // 2
STEPS = 200
EPS = 1e-05
SIGMA_DATA = 16.0
SIGMA_MAX = 160.0
SIGMA_MIN = 0.0004
RHO = 7
MASKED = -1000000000.0

NY = 4
NZ = 8
NK = 2
NC = 4

ATOMS = 512
TOKS = 32
C_A = 128
C_S = 768
GROUP = 4
HEAD = 48
GW = GROUP * HEAD
ROWS = 8
COLS = 512

F32 = jnp.float32
BF = jnp.bfloat16
VMEM = pltpu.CompilerParams(vmem_limit_bytes=56 * 2**20)


def dot(a, b):
    return jnp.dot(a, b, preferred_element_type=F32)


def dot_nt(a, b):
    return lax.dot_general(a, b, (((1,), (1,)), ((), ())), preferred_element_type=F32)


def iota(shape, dim):
    return lax.broadcasted_iota(jnp.int32, shape, dim)


def hi_lo(v):
    hi = v.astype(BF)
    return hi, (v - hi.astype(F32)).astype(BF)


def three(v):
    hi = v.astype(BF)
    rest = v - hi.astype(F32)
    mid = rest.astype(BF)
    return hi, mid, (rest - mid.astype(F32)).astype(BF)


def normalize(values):
    average = jnp.mean(values, axis=-1, keepdims=True)
    centred = values - average
    variance = jnp.mean(centred * centred, axis=-1, keepdims=True)
    return centred * lax.rsqrt(variance + EPS)


def call(kernel, outs, *args, name, flops=0, smem=()):
    vm = pl.BlockSpec(memory_space=pltpu.VMEM)
    sm = pl.BlockSpec(memory_space=pltpu.SMEM)
    return pl.pallas_call(
        kernel,
        in_specs=[sm if i in smem else vm for i in range(len(args))],
        out_specs=[vm] * len(outs),
        out_shape=[jax.ShapeDtypeStruct(s, d) for s, d in outs],
        compiler_params=VMEM,
        cost_estimate=pl.CostEstimate(flops=flops, bytes_accessed=2**20, transcendentals=0),
        name=name,
    )(*args)


def atom_in_kernel(noise_ref, pos_ref, wpos_ref, single_ref, counts_ref, initial_ref, normed_ref, first_ref, last_ref):
    level = jnp.full((1, C_A), noise_ref[0], jnp.int32).astype(F32)
    upper = SIGMA_MAX ** (1.0 / RHO)
    lower = SIGMA_MIN ** (1.0 / RHO)
    root = upper + level / (STEPS - 1) * (lower - upper)
    square = root * root
    sigma = square * square * square * root
    gain = 1.0 / jnp.sqrt(sigma * sigma + SIGMA_DATA * SIGMA_DATA)
    lifted = lax.dot_general(
        pos_ref[...], wpos_ref[...] * gain, (((0,), (0,)), ((), ())),
        precision=lax.Precision.HIGHEST, preferred_element_type=F32,
    )
    initial = single_ref[...].astype(F32) + lifted
    initial_ref[...] = initial
    normed = normalize(initial).astype(BF)
    normed_ref[...] = normed
    total = jnp.sum(counts_ref[...], axis=1, keepdims=True)
    slots = iota((ATOMS, C_A), 0)
    live = jnp.where(slots < total, 1.0, 0.0).astype(BF)
    both = jnp.concatenate([normed, live], axis=1)
    first_ref[...] = both[:MARGIN]
    last_ref[...] = both[ATOMS - MARGIN :]


def spans(counts_ref):
    row = counts_ref[...].astype(F32)
    grid = jnp.broadcast_to(row, (TOKS, TOKS))
    r, c = iota((TOKS, TOKS), 0), iota((TOKS, TOKS), 1)
    count_col = jnp.sum(jnp.where(r == c, grid, 0.0), axis=1, keepdims=True)
    end_col = jnp.sum(jnp.where(c <= r, grid, 0.0), axis=1, keepdims=True)
    end_row = jnp.sum(jnp.where(r <= c, jnp.broadcast_to(count_col, (TOKS, TOKS)), 0.0), axis=0, keepdims=True)
    return row, count_col, end_row, end_col


def atom_mid_kernel(
    normed_ref, initial_ref, before_ref, after_ref, counts_ref,
    wq_ref, wk_ref, wv_ref, wo_ref, pool_ref, single_ref, twq_ref, twk_ref,
    state_ref, token_in_ref, token_normed_ref, t_ref,
):
    before = before_ref[...]
    after = after_ref[...]
    normed = normed_ref[...]
    _, count_col, _, end_col = spans(counts_ref)
    slots = iota((TOKS, ATOMS), 1).astype(F32)
    onehot = jnp.where((slots < end_col) & (slots >= end_col - count_col), 1.0, 0.0).astype(BF)
    total = jnp.sum(counts_ref[...], axis=1, keepdims=True)
    own_live = jnp.where(iota((ATOMS, C_A), 0) < total, 1.0, 0.0).astype(BF)
    wide = jnp.concatenate([before[:, :C_A], normed, after[:, :C_A]], axis=0)
    live = jnp.concatenate([before[:, C_A:], own_live, after[:, C_A:]], axis=0)
    queries = dot(normed, wq_ref[...]).astype(BF)
    keys = dot(wide, wk_ref[...]).astype(BF)
    values = dot(wide, wv_ref[...]).astype(BF)
    lane_head = iota((H_A * WIN_Q, C_A), 1) // (C_A // H_A)
    row_head = iota((H_A * WIN_Q, C_A), 0) // WIN_Q
    mine = lane_head == row_head
    eye = jnp.where(iota((WIN_K, WIN_K), 0) == iota((WIN_K, WIN_K), 1), 1.0, 0.0).astype(BF)
    scale = 1.0 / math.sqrt(C_A // H_A)
    mixes = []
    for w in range(ATOMS // WIN_Q):
        q = queries[w * WIN_Q : (w + 1) * WIN_Q]
        q4 = jnp.where(mine, jnp.concatenate([q] * H_A, axis=0).astype(F32), 0.0).astype(BF)
        lo = w * WIN_Q
        k = keys[lo : lo + WIN_K]
        v = values[lo : lo + WIN_K]
        alive = dot_nt(jnp.ones((8, C_A), BF), jnp.where(iota((WIN_K, C_A), 1) == 0, live[lo : lo + WIN_K].astype(F32), 0.0).astype(BF))
        scores = dot_nt(q4, k) * scale + jnp.where(alive[:1] > 0.5, 0.0, MASKED)
        top = jnp.max(scores, axis=1, keepdims=True)
        p = jnp.exp(scores - top)
        weight = (p / jnp.sum(p, axis=1, keepdims=True)).astype(BF)
        o = jnp.where(mine, dot(weight, v), 0.0)
        mixes.append(o[:32] + o[32:64] + o[64:96] + o[96:])
    mix = jnp.concatenate(mixes, axis=0).astype(BF)
    state = initial_ref[...] + dot(mix, wo_ref[...])
    state_ref[...] = state
    features = jnp.maximum(dot(state.astype(BF), pool_ref[...]), 0.0)
    f_hi, f_lo = hi_lo(features)
    sums = dot(onehot, f_hi) + dot(onehot, f_lo)
    token_in = single_ref[...].astype(F32) + sums / count_col
    token_in_ref[...] = token_in
    token_normed = normalize(token_in).astype(BF)
    token_normed_ref[...] = token_normed
    tq = dot(token_normed, twq_ref[...]).astype(BF).astype(F32)
    lanes = iota((ROWS, GW), 1) // HEAD
    pieces = [
        jnp.where(lanes == h, tq[ib * ROWS : (ib + 1) * ROWS], 0.0)
        for ib in range(TOKS // ROWS)
        for h in range(GROUP)
    ]
    spread = jnp.concatenate(pieces, axis=0).astype(BF)
    t_ref[...] = (dot_nt(spread, twk_ref[...]) * (1.0 / math.sqrt(HEAD))).astype(BF)


def pair_kernel(x_ref, w1_ref, w2_ref, wb_ref, *refs, fresh):
    if not fresh:
        refs = refs[2:]
    out_ref, bias_ref, cen_s, avg_s, w1_s, w2_s, wb_s, vb_s = refs
    pairs = ROWS // 2

    @pl.when(pl.program_id(0) == 0)
    def _():
        r, c = iota((256, 256), 0), iota((256, 256), 1)
        same = (r // 128) == (c // 128)
        avg_s[...] = jnp.where(same, 1.0 / 128, 0.0).astype(BF)
        cen_s[...] = (jnp.where(r == c, 1.0, 0.0) - jnp.where(same, 1.0 / 128, 0.0)).astype(BF)
        w1_s[:, :256] = w1_ref[:, :256] * jnp.asarray(0.5, BF)
        w1_s[:, 256:] = w1_ref[:, 256:]
        w2 = w2_ref[...]
        w2_s[:, :128] = w2
        wide = w2.astype(F32)
        w2_s[:, 128:] = (wide - jnp.mean(wide, axis=1, keepdims=True)).astype(BF)
        head, lane = iota((H_T, 128), 0), iota((H_T, 128), 1)
        spot = iota((128, 128), 1)
        for p in range(pairs):
            for k in range(2):
                g = k * pairs + p
                place = jnp.where(lane == head * ROWS + g, 1.0, 0.0).astype(BF)
                wb_s[p, 128 * k : 128 * k + 128, :] = dot(wb_ref[...], place).astype(BF)
                vb_s[p, 128 * k : 128 * k + 128, :] = jnp.where(spot % ROWS == g, 1.0 / 128, 0.0).astype(BF)

    m = pairs * COLS
    xs = [x_ref[:pairs].reshape(m, 128), x_ref[pairs:].reshape(m, 128)]
    c = dot(jnp.concatenate(xs, axis=1), cen_s[...])
    v = dot((c * c).astype(BF), avg_s[...])
    n = (c * lax.rsqrt(v + EPS)).astype(BF)
    kept, squares = [], []
    for k in range(2):
        g = dot(n[:, 128 * k : 128 * k + 128], w1_s[...])
        gate, up = g[:, :256], g[:, 256:]
        h = ((gate + gate * jnp.tanh(gate)) * up).astype(BF)
        u = dot(h, w2_s[...])
        out_ref[k * pairs : (k + 1) * pairs] = (
            (xs[k].astype(F32) + u[:, :128]).astype(BF).reshape(pairs, COLS, 128)
        )
        c2 = c[:, 128 * k : 128 * k + 128] + u[:, 128:]
        kept.append(c2.astype(BF))
        squares.append((c2 * c2).astype(BF))
    cc = jnp.concatenate(kept, axis=1)
    ss = jnp.concatenate(squares, axis=1)
    acc = jnp.zeros((COLS, 128), F32)
    var = jnp.zeros((COLS, 128), F32)
    for p in range(pairs):
        acc = acc + dot(cc[p * COLS : (p + 1) * COLS], wb_s[p])
        var = var + dot(ss[p * COLS : (p + 1) * COLS], vb_s[p])
    b = acc * lax.rsqrt(var + EPS)
    bias_ref[...] = b.T.astype(BF).reshape(NC, 1, GROUP * ROWS, COLS)


def pair_call(x, w1, w2, wb, prior, start, count):
    fresh = prior is None
    whole = lambda a: pl.BlockSpec(a.shape, lambda i: (0,) * a.ndim)
    anywhere = pl.BlockSpec(memory_space=pl.ANY)
    n = TOKS // ROWS
    return pl.pallas_call(
        lambda *refs: pair_kernel(*refs, fresh=fresh),
        grid=(count,),
        in_specs=[pl.BlockSpec((ROWS, COLS, 128), lambda i: (i + start, 0, 0)), whole(w1), whole(w2), whole(wb)]
        + ([] if fresh else [anywhere] * 2),
        out_specs=[
            pl.BlockSpec((ROWS, COLS, 128), lambda i: (i + start, 0, 0)),
            pl.BlockSpec((NC, 1, GROUP * ROWS, COLS), lambda i: (0, i + start, 0, 0)),
        ],
        out_shape=[
            jax.ShapeDtypeStruct(x.shape, BF),
            jax.ShapeDtypeStruct((NC, n, GROUP * ROWS, COLS), BF),
        ],
        scratch_shapes=[
            pltpu.VMEM((256, 256), BF),
            pltpu.VMEM((256, 256), BF),
            pltpu.VMEM((128, 512), BF),
            pltpu.VMEM((256, 256), BF),
            pltpu.VMEM((ROWS // 2, 256, 128), BF),
            pltpu.VMEM((ROWS // 2, 256, 128), BF),
        ],
        input_output_aliases={} if fresh else {4: 0, 5: 1},
        compiler_params=VMEM,
        cost_estimate=pl.CostEstimate(flops=count * 3 * 10**9, bytes_accessed=count * 2**21, transcendentals=0),
        name="pair",
    )(x, w1, w2, wb, *(() if fresh else prior))


def weights_kernel(wv_ref, wo_ref, back_ref, out_ref):
    out_ref[:C_S, :GW] = wv_ref[...]
    out_ref[:C_S, GW:] = jnp.zeros((C_S, 256 - GW), BF)
    hi, lo = hi_lo(dot(wo_ref[...], back_ref[...]))
    out_ref[C_S:, :C_A] = hi
    out_ref[C_S:, C_A:] = lo


def attention_kernel(
    place_ref, t0, t1, t2, t3, own_ref, other_ref, bias_ref, w0, w1, w2, w3, msg_ref, back_ref, xk_s, o_s
):
    col, core = place_ref[0], place_ref[1]
    xk_s[:, pl.ds(core, 1)] = own_ref[...].reshape(NZ, 1, TOKS, C_S)
    xk_s[:, pl.ds(1 - core, 1)] = other_ref[...].reshape(NZ, 1, TOKS, C_S)
    xk = xk_s[...].reshape(COLS, C_S)
    wide = GROUP * TOKS
    t = jnp.concatenate([t0[...], t1[...], t2[...], t3[...]], axis=0)
    scores = dot_nt(t, xk)
    groups = [(col + NC - s) % NC for s in range(NC)]
    scores = jnp.concatenate(
        [
            scores[s * wide : (s + 1) * wide] + bias_ref[pl.ds(groups[s], 1)].reshape(wide, COLS).astype(F32)
            for s in range(NC)
        ],
        axis=0,
    )
    top = jnp.max(scores, axis=1, keepdims=True)
    p = jnp.exp(scores - top)
    total = jnp.sum(p, axis=1, keepdims=True)
    mixed = (dot(p.astype(BF), xk) / total).astype(BF)
    blocks = TOKS // ROWS
    lane_head = iota((1, GROUP, 1, 256), 3) // HEAD
    row_head = iota((1, GROUP, 1, 256), 1)
    lane16 = iota((1, GROUP, 1, 128), 3) % H_T
    row16 = iota((1, GROUP, 1, 128), 1)
    tops = jnp.zeros((TOKS, 128), F32)
    totals = jnp.zeros((TOKS, 128), F32)
    for s, w in enumerate((w0, w1, w2, w3)):
        lo = s * wide
        o = dot(mixed[lo : lo + wide], w[:C_S, :]).reshape(blocks, GROUP, ROWS, 256)
        o = jnp.sum(jnp.where(lane_head == row_head, o, 0.0), axis=1).reshape(TOKS, 256)
        o_s[pl.ds(groups[s], 1)] = o.reshape(1, TOKS, 256)
        back_ref[pl.ds(groups[s], 1)] = w[C_S:, :].reshape(1, GW, 256)
        here = lane16 == row16 + groups[s] * GROUP
        for value, which in ((top, 0), (total, 1)):
            part = jnp.broadcast_to(value[lo : lo + wide], (wide, 128)).reshape(blocks, GROUP, ROWS, 128)
            part = jnp.sum(jnp.where(here, part, 0.0), axis=1).reshape(TOKS, 128)
            if which == 0:
                tops = tops + part
            else:
                totals = totals + part
    part_of = iota((TOKS, 128), 1) // H_T
    stats = jnp.zeros((TOKS, 128), F32)
    for i, piece in enumerate((*three(tops), *three(totals))):
        stats = jnp.where(part_of == i, piece.astype(F32), stats)
    msg_ref[...] = jnp.concatenate([o_s[g][:, :GW] for g in range(NC)] + [stats], axis=1).astype(BF)


def final_kernel(m0, m1, m2, m3, token_in_ref, state_ref, counts_ref, wback_ref, back_ref, out_ref):
    msgs = [m0[...], m1[...], m2[...], m3[...]]
    r, c = iota((128, 256), 0), iota((128, 256), 1)
    pick = ((r // H_T) // 3 == c // 128) & (r % H_T == c % H_T) & (r < 6 * H_T)
    stats = dot(jnp.concatenate([m[:, C_S:] for m in msgs], axis=0), jnp.where(pick, 1.0, 0.0).astype(BF))
    tops = [stats[i * TOKS : (i + 1) * TOKS, :128] for i in range(NC)]
    totals = [stats[i * TOKS : (i + 1) * TOKS, 128:] for i in range(NC)]
    top = jnp.maximum(jnp.maximum(tops[0], tops[1]), jnp.maximum(tops[2], tops[3]))
    shares = [l * jnp.exp(t - top) for l, t in zip(totals, tops)]
    whole = shares[0] + shares[1] + shares[2] + shares[3]
    r, c = iota((128, C_S), 0), iota((128, C_S), 1)
    expand = jnp.where((r % H_T == c // HEAD) & (r < 2 * H_T), 1.0, 0.0).astype(BF)
    part_of = iota((TOKS, 128), 1) // H_T
    coefs = []
    for share in shares:
        hi, lo = hi_lo(share / whole)
        coefs.append(jnp.where(part_of == 0, hi.astype(F32), lo.astype(F32)).astype(BF))
    scale = dot(jnp.concatenate(coefs, axis=0), expand)
    mix = jnp.zeros((TOKS, C_S), F32)
    for i, m in enumerate(msgs):
        mix = mix + scale[i * TOKS : (i + 1) * TOKS] * m[:, :C_S].astype(F32)
    folded = dot(mix.astype(BF), back_ref[...].reshape(C_S, 256))
    returned = dot(token_in_ref[...].astype(BF), wback_ref[...]) + folded[:, :C_A] + folded[:, C_A:]
    row, _, end_row, _ = spans(counts_ref)
    slots = iota((ATOMS, TOKS), 0).astype(F32)
    onehot = jnp.where((slots < end_row) & (slots >= end_row - row), 1.0, 0.0).astype(BF)
    r_hi, r_lo = hi_lo(returned)
    spread = dot(onehot, r_hi) + dot(onehot, r_lo)
    alive = iota((ATOMS, C_A), 0) < jnp.sum(counts_ref[...], axis=1, keepdims=True)
    out_ref[...] = jnp.where(alive, state_ref[...] + spread, 0.0).astype(BF)


def around(array, axis, size):
    return [lax.ppermute(array, axis, [(i, (i + s) % size) for i in range(size)]) for s in range(1, size)]


def local(
    atom_single, positions, noise_index, token_counts, token_single, pair_repr, w_pos, atom_wq, atom_wk, atom_wv,
    atom_wo, w_pool, trans_w1, trans_w2, w_bias, token_wq, token_wk, token_wv, token_wo, w_back,
):
    atoms = NY * NZ * NK
    counts = token_counts.reshape(1, TOKS)
    col = lax.axis_index("col")
    place = jnp.stack([col, lax.axis_index("atom") % NK]).astype(jnp.int32)

    initial, normed, first, last = call(
        atom_in_kernel,
        [((ATOMS, C_A), F32), ((ATOMS, C_A), BF), ((MARGIN, 2 * C_A), BF), ((MARGIN, 2 * C_A), BF)],
        noise_index, positions, w_pos, atom_single, counts, name="atom_in", smem=(0,), flops=10**8,
    )
    before = lax.ppermute(last, "atom", [(i, i + 1) for i in range(atoms - 1)])
    after = lax.ppermute(first, "atom", [(i + 1, i) for i in range(atoms - 1)])
    (packed,) = call(
        weights_kernel, [((C_S + GW, 256), BF)], token_wv, token_wo, w_back, name="weights", flops=10**8
    )
    weights = [packed] + around(packed, "col", NC)
    state, token_in, token_normed, t_own = call(
        atom_mid_kernel,
        [((ATOMS, C_A), F32), ((TOKS, C_S), F32), ((TOKS, C_S), BF), ((GROUP * TOKS, C_S), BF)],
        normed, initial, before, after, counts, atom_wq, atom_wk, atom_wv, atom_wo, w_pool, token_single,
        token_wq, token_wk, name="atom_mid", flops=10**9,
    )
    flip = [
        ((y * NZ * NK + i) * NC + x, (x * NZ * NK + i) * NC + y)
        for y in range(NY) for i in range(NZ * NK) for x in range(NC)
    ]
    turned = lax.ppermute(token_normed, ("atom", "col"), flip)
    lines = [[(y * NZ + z) * NK + k for z in range(NZ)] for y in range(NY) for k in range(NK)]
    own = lax.all_to_all(
        jnp.broadcast_to(turned[None], (NZ, TOKS, C_S)), "atom", 0, 0, axis_index_groups=lines, tiled=True
    )
    other = lax.ppermute(own, "atom", [(i, i ^ 1) for i in range(atoms)])
    queries = [t_own] + around(t_own, "col", NC)

    prior = None
    for start in range(TOKS // ROWS):
        prior = pair_call(pair_repr, trans_w1, trans_w2, w_bias, prior, start, 1)
    pair_out, bias = prior

    msg, back = pl.pallas_call(
        attention_kernel,
        in_specs=[pl.BlockSpec(memory_space=pltpu.SMEM)] + [pl.BlockSpec(memory_space=pltpu.VMEM)] * 11,
        out_specs=[pl.BlockSpec(memory_space=pltpu.VMEM)] * 2,
        out_shape=[
            jax.ShapeDtypeStruct((TOKS, C_S + 128), BF),
            jax.ShapeDtypeStruct((NC, GW, 256), BF),
        ],
        scratch_shapes=[pltpu.VMEM((NZ, NK, TOKS, C_S), BF), pltpu.VMEM((NC, TOKS, 256), F32)],
        compiler_params=VMEM,
        cost_estimate=pl.CostEstimate(flops=3 * 10**9, bytes_accessed=2**20, transcendentals=0),
        name="attention",
    )(place, *queries, own, other, bias.reshape(NC, GROUP * TOKS, COLS), *weights)
    msgs = [msg] + around(msg, "col", NC)
    (atom_out,) = call(
        final_kernel, [((ATOMS, C_A), BF)], *msgs, token_in, state, counts, w_back, back, name="final", flops=10**8
    )
    return (atom_out, pair_out)


def solution(mesh):
    placed = (
        P("atom", None), P(None, "atom"), P(), P("atom"), P("atom", None), P("atom", "col", None),
        P(), P(), P(), P(), P(), P(), P(), P(), P(),
        P(None, "col"), P(None, "col"), P(None, "col"), P("col", None), P(),
    )
    return jax.shard_map(
        local,
        mesh=mesh,
        in_specs=placed,
        out_specs=(P("atom", None), P("atom", "col", None)),
        check_vma=False,
    )
```

time: 151 us -> 90.7 us (0.60); the launches traced: 148 us -> 90.1 us
  Pallas kernels: 0 us -> 40.8 us
  other arithmetic: 40.2 us -> 0.55 us
  matrix products: 30.7 us -> 0 us
  starting transfers between devices: 16.6 us -> 34.1 us
  between operations: 15.2 us -> 1.49 us
  blocking collectives: 13.5 us -> 0 us
  waiting for transfers between devices: 17.3 us -> 4.46 us
  local copies, waits for them, and re-layouts: 14.4 us -> 8.69 us
    pallas_call x0 -> x9, Pallas kernels: none -> 40.8 us  [the longest x4 20.5 us: pair_call(): pl.pallas_call(lambda *refs: pair_kernel(*refs, fresh=fresh), grid=(count...]
    dot_general x27 -> x0, matrix products: 30.7 us -> none  [the longest x4 6.46 us: pair_block(): jnp.dot(hidden, trans_w2, preferred_element_type=jnp.float32)]
    reduce_sum x15 -> x0, other arithmetic: 21.3 us -> none  [the longest x10 14.8 us: normalize(): variance = jnp.mean(centred * centred, axis=-1, keepdims=True)]
    convert_element_type x11 -> x0, other arithmetic: 16.6 us -> none  [the longest x4 9.17 us: pair_block(): normed_in = normalize(flattened).astype(jnp.bfloat16)]
    ppermute x4 -> x13, starting transfers between devices: 12.4 us -> 26.4 us  [the longest x9 13.5 us: around(): lax.ppermute(array, axis, [(i, (i + s) % size) for i in range(size)])]
    psum x1 -> x0, blocking collectives: 13.5 us -> none  [local(): lax.psum(partial_out.astype(jnp.bfloat16), 'col').astype(jnp.float32)]
    all_gather x1 -> x0, waiting for transfers between devices: 9.51 us -> none  [local(): lax.all_gather(token_normed, 'atom', axis=0, tiled=True)]
    dynamic_update_slice x8 -> x0, local copies, waits for them, and re-layouts: 6.95 us -> none  [local(): lax.map(process, pair_repr.reshape(tok_rows // rows_per, rows_per, col_co...]
  transfers between devices with their start and end apart: 6 -> 14, of which waited for: 3 -> 3; matrix products, arithmetic and copies ran while one was open for 45% -> 7% of each run, Pallas kernels for 0% -> 25%
where the time goes in v1:
time: 90.7 us; the launch traced here: 90.1 us
  Pallas kernels  40.8 us (45%)
  starting transfers between devices  34.1 us (38%)
  local copies, waits for them, and re-layouts  8.69 us (10%)
  waiting for transfers between devices  4.46 us (5%)
  between operations  1.49 us (2%)
    pallas_call x4, Pallas kernels, pair_call(): pl.pallas_call(lambda *refs: pair_kernel(*refs, fresh=fresh), grid=(count...  20.5 us
    pallas_call x4, Pallas kernels, call(): pl.pallas_call(kernel, in_specs=[sm if i in smem else vm for i in range(l...  15.9 us
    ppermute x9, starting transfers between devices, around(): lax.ppermute(array, axis, [(i, (i + s) % size) for i in range(size)])  13.5 us
    unnamed x36, local copies, waits for them, and re-layouts  7.91 us
    all_to_all x1, starting transfers between devices, local(): lax.all_to_all(jnp.broadcast_to(turned[None], (NZ, TOKS, C_S)), 'atom', 0...  7.68 us
    ppermute x1, starting transfers between devices, local(): before = lax.ppermute(last, 'atom', [(i, i + 1) for i in range(atoms - 1)])  4.92 us
    ppermute x1, starting transfers between devices, local(): other = lax.ppermute(own, 'atom', [(i, i ^ 1) for i in range(atoms)])  4.56 us
    ppermute x9, waiting for transfers between devices, around(): lax.ppermute(array, axis, [(i, (i + s) % size) for i in range(size)])  4.45 us
  transfers between devices with their start and end apart: 14, of which 3 were waited for; matrix products, arithmetic and copies ran while one was open for 7% of the time, Pallas kernels for 25%

profile of v1, /device:TPU:1, one launch (start us, length us, event | category | flops | bytes accessed | tf_op | source)
XLA Modules:
  0.0 90.1 jit_solution(1038875194906753000)
XLA Ops:
  1.3 2.2 %atom_in.1 = (f32[512,128]{1,0:T(8,128)}, bf16[512,128]{1,0:T(8,128)(2,1)}, bf16[48,256]{1,0:T(8,128)(2,1)}, bf16[48,256]{1,0:T(8,128)(2,1)}) custom-call(s32[1]{0:T(128)S(6)} %copy.41.noise_ref, f32[3,512]{1,0:T(4,128)} %pos_ref.1, f32[3,128]{1,0:T(4,128)} %wpos_ref.1, bf16[512,128]{1,0:T(8,128)(2,1)} %single_ref.2, s32[1,32]{1,0:T(1,128)} %bitcast.4), custom_call_target="tpu_custom_call" | custom-call | flops 100000000 | bytes 1048576 | tf_op jit(solution)/shard_map/atom_in/pallas_call | solution.py:77
  3.5 4.9 %collective-permute-start = (bf16[48,256]{1,0:T(8,128)(2,1)}, bf16[48,256]{1,0:T(8,128)(2,1)S(1)}, u32[]{:S(2)}, u32[]{:S(2)}) collective-permute-start(bf16[48,256]{1,0:T(8,128)(2,1)} %get-tuple-element.22), channel_id=1, source_target_pairs={{0,4},{4,8},{8,12},{12,16},{16,20},{20,24},{24,28},{28,32},{32,36}... | collective-permute-start | bytes 73736 | tf_op jit(solution)/shard_map/ppermute | solution.py:376
  8.5 1.9 %collective-permute-start.1 = (bf16[48,256]{1,0:T(8,128)(2,1)}, bf16[48,256]{1,0:T(8,128)(2,1)S(1)}, u32[]{:S(2)}, u32[]{:S(2)}) collective-permute-start(bf16[48,256]{1,0:T(8,128)(2,1)} %get-tuple-element.23), channel_id=1, source_target_pairs={{4,0},{8,4},{12,8},{16,12},{20,16},{24,20},{28,24},{32,28},{36,32}... | collective-permute-start | bytes 73736 | tf_op jit(solution)/shard_map/ppermute | solution.py:377
  10.4 1.9 %copy.28.twq_ref = bf16[768,192]{1,0:T(8,128)(2,1)} copy(bf16[768,192]{0,1:T(8,128)(2,1)} %param.35) | data formatting | bytes 589824 | tf_op args[15]
  12.3 1.9 %copy.29.twk_ref = bf16[768,192]{1,0:T(8,128)(2,1)} copy(bf16[768,192]{0,1:T(8,128)(2,1)} %param.36) | data formatting | bytes 589824 | tf_op args[16]
  14.8 8.7 %atom_mid.1 = (f32[512,128]{1,0:T(8,128)}, f32[32,768]{1,0:T(8,128)}, bf16[32,768]{1,0:T(8,128)(2,1)}, bf16[128,768]{1,0:T(8,128)(2,1)}) custom-call(bf16[512,128]{1,0:T(8,128)(2,1)} %get-tuple-element.20.normed_ref, f32[512,128]{1,0:T(8,128)} %get-tuple-element.21.initial_ref, bf16[48,256]{1,0:T(8,128)(2,1)} %copy-done.14, bf16[48,256]{1,0:T(8,128)(2,1)} %copy-done.15, ...), custom_call_target="tpu_custom_call" | custom-call | flops 1000000000 | bytes 1048576 | tf_op jit(solution)/shard_map/atom_mid/pallas_call | solution.py:77
  23.5 1.4 %collective-permute-start.5 = (bf16[32,768]{1,0:T(8,128)(2,1)}, bf16[32,768]{1,0:T(8,128)(2,1)S(1)}, u32[]{:S(2)}, u32[]{:S(2)}) collective-permute-start(bf16[32,768]{1,0:T(8,128)(2,1)} %get-tuple-element.25), channel_id=1, source_target_pairs={{0,0},{1,64},{2,128},{3,192},{4,4},{5,68},{6,132},{7,196},{8,8},{9... | collective-permute-start | bytes 147464 | tf_op jit(solution)/shard_map/ppermute | solution.py:392
  25.9 2.2 %weights.1.w0 = bf16[960,256]{1,0:T(8,128)(2,1)} custom-call(bf16[768,192]{1,0:T(8,128)(2,1)} %copy.34.wv_ref, bf16[192,768]{1,0:T(8,128)(2,1)} %wo_ref.3, bf16[768,128]{1,0:T(8,128)(2,1)} %wback_ref.1), custom_call_target="tpu_custom_call" | custom-call | flops 100000000 | bytes 1048576 | tf_op jit(solution)/shard_map/weights/pallas_call | solution.py:77
  28.1 2.9 %collective-permute-start.7 = (bf16[960,256]{1,0:T(8,128)(2,1)}, bf16[960,256]{1,0:T(8,128)(2,1)S(1)}, u32[]{:S(2)}, u32[]{:S(2)}) collective-permute-start(bf16[960,256]{1,0:T(8,128)(2,1)} %weights.1.w0), channel_id=1, source_target_pairs={{0,1},{1,2},{2,3},{3,0},{4,5},{5,6},{6,7},{7,4},{8,9},{9,10},{10,1... | collective-permute-start | bytes 1474568 | tf_op jit(solution)/shard_map/ppermute | solution.py:359
  31.0 3.8 %collective-permute-start.8 = (bf16[960,256]{1,0:T(8,128)(2,1)}, bf16[960,256]{1,0:T(8,128)(2,1)S(1)}, u32[]{:S(2)}, u32[]{:S(2)}) collective-permute-start(bf16[960,256]{1,0:T(8,128)(2,1)} %weights.1.w0), channel_id=1, source_target_pairs={{0,2},{1,3},{2,0},{3,1},{4,6},{5,7},{6,4},{7,5},{8,10},{9,11},{10,... | collective-permute-start | bytes 1474568 | tf_op jit(solution)/shard_map/ppermute | solution.py:359
  34.9 1.4 %collective-permute-start.9 = (bf16[960,256]{1,0:T(8,128)(2,1)}, bf16[960,256]{1,0:T(8,128)(2,1)S(1)}, u32[]{:S(2)}, u32[]{:S(2)}) collective-permute-start(bf16[960,256]{1,0:T(8,128)(2,1)} %weights.1.w0), channel_id=1, source_target_pairs={{0,3},{1,0},{2,1},{3,2},{4,7},{5,4},{6,5},{7,6},{8,11},{9,8},{10,9... | collective-permute-start | bytes 1474568 | tf_op jit(solution)/shard_map/ppermute | solution.py:359
  37.7 7.7 %all-to-all-start = ((bf16[8,32,768]{2,1,0:T(8,128)(2,1)}), bf16[8,32,768]{2,1,0:T(8,128)(2,1)S(1)}, u32[]{:S(2)}, u32[]{:S(2)}) async-start(bf16[8,32,768]{2,1,0:T(8,128)(2,1)} %broadcast_in_dim.2), calls=%async_computation | async-start | bytes 786432 | tf_op jit(solution)/shard_map/all_to_all | solution.py:394
  45.4 5.1 %pair.4 = (bf16[32,512,128]{2,1,0:T(8,128)(2,1)}, bf16[4,4,32,512]{3,2,1,0:T(8,128)(2,1)}) custom-call(bf16[32,512,128]{2,1,0:T(8,128)(2,1)} %refs_0_.7, bf16[128,512]{1,0:T(8,128)(2,1)} %refs_1_.7, bf16[256,128]{1,0:T(8,128)(2,1)} %refs_2_.7, bf16[128,16]{1,0:T(8,128)(2,1)} %copy.33.refs_3_), custom_call_target="tpu_custom_call" | custom-call | flops 3000000000 | bytes 2097152 | tf_op jit(solution)/shard_map/pair/pallas_call | solution.py:240
  50.5 5.2 %pair.5 = (bf16[32,512,128]{2,1,0:T(8,128)(2,1)}, bf16[4,4,32,512]{3,2,1,0:T(8,128)(2,1)}) custom-call(bf16[32,512,128]{2,1,0:T(8,128)(2,1)} %refs_0_.7, bf16[128,512]{1,0:T(8,128)(2,1)} %refs_1_.7, bf16[256,128]{1,0:T(8,128)(2,1)} %refs_2_.7, bf16[128,16]{1,0:T(8,128)(2,1)} %copy.33.refs_3_, ...), custom_call_target="tpu_custom_call", output_to_operand_aliasing={{0}: (4, {}), {1}: (5, {})} | custom-call | flops 3000000000 | bytes 2097152 | tf_op jit(solution)/shard_map/pair/pallas_call | solution.py:240
  55.8 1.1 %collective-permute-start.3 = (bf16[128,768]{1,0:T(8,128)(2,1)S(1)}, bf16[128,768]{1,0:T(8,128)(2,1)S(1)}, u32[]{:S(2)}, u32[]{:S(2)}) collective-permute-start(bf16[128,768]{1,0:T(8,128)(2,1)S(1)} %copy-done.10), channel_id=1, source_target_pairs={{0,2},{1,3},{2,0},{3,1},{4,6},{5,7},{6,4},{7,5},{8,10},{9,11},{10,... | collective-permute-start | bytes 589832 | tf_op jit(solution)/shard_map/ppermute | solution.py:359
  56.9 5.1 %pair.6 = (bf16[32,512,128]{2,1,0:T(8,128)(2,1)}, bf16[4,4,32,512]{3,2,1,0:T(8,128)(2,1)}) custom-call(bf16[32,512,128]{2,1,0:T(8,128)(2,1)} %refs_0_.7, bf16[128,512]{1,0:T(8,128)(2,1)} %refs_1_.7, bf16[256,128]{1,0:T(8,128)(2,1)} %refs_2_.7, bf16[128,16]{1,0:T(8,128)(2,1)} %copy.33.refs_3_, ...), custom_call_target="tpu_custom_call", output_to_operand_aliasing={{0}: (4, {}), {1}: (5, {})} | custom-call | flops 3000000000 | bytes 2097152 | tf_op jit(solution)/shard_map/pair/pallas_call | solution.py:240
  62.0 2.2 %collective-permute-done.2.t1 = bf16[128,768]{1,0:T(8,128)(2,1)S(1)} collective-permute-done((bf16[128,768]{1,0:T(8,128)(2,1)S(1)}, bf16[128,768]{1,0:T(8,128)(2,1)S(1)}, u32[]{:S(2)}, u32[]{:S(2)}) %collective-permute-start.2) | collective-permute-done | bytes 196640 | tf_op jit(solution)/shard_map/ppermute | solution.py:359
  64.2 4.6 %collective-permute-start.6 = (bf16[8,32,768]{2,1,0:T(8,128)(2,1)S(1)}, bf16[8,32,768]{2,1,0:T(8,128)(2,1)S(1)}, u32[]{:S(2)}, u32[]{:S(2)}) collective-permute-start(bf16[8,32,768]{2,1,0:T(8,128)(2,1)S(1)} %all-to-all-done.own_ref), channel_id=1, source_target_pairs={{0,4},{4,0},{8,12},{12,8},{16,20},{20,16},{24,28},{28,24},{32,36},... | collective-permute-start | bytes 1179656 | tf_op jit(solution)/shard_map/ppermute | solution.py:397
  68.8 5.1 %pair.7 = (bf16[32,512,128]{2,1,0:T(8,128)(2,1)}, bf16[4,4,32,512]{3,2,1,0:T(8,128)(2,1)}) custom-call(bf16[32,512,128]{2,1,0:T(8,128)(2,1)} %refs_0_.7, bf16[128,512]{1,0:T(8,128)(2,1)} %refs_1_.7, bf16[256,128]{1,0:T(8,128)(2,1)} %refs_2_.7, bf16[128,16]{1,0:T(8,128)(2,1)} %copy.33.refs_3_, ...), custom_call_target="tpu_custom_call", output_to_operand_aliasing={{0}: (4, {}), {1}: (5, {})} | custom-call | flops 3000000000 | bytes 2097152 | tf_op jit(solution)/shard_map/pair/pallas_call | solution.py:240
  75.8 4.4 %attention.1 = (bf16[32,896]{1,0:T(8,128)(2,1)}, bf16[4,192,256]{2,1,0:T(8,128)(2,1)}) custom-call(s32[2]{0:T(128)} %pad_add_fusion.place_ref, bf16[128,768]{1,0:T(8,128)(2,1)} %get-tuple-element.24.t0, bf16[128,768]{1,0:T(8,128)(2,1)} %copy-done.11, bf16[128,768]{1,0:T(8,128)(2,1)} %copy-done.12, bf16[128,768]{1,0:T(8,128)(2,1)} %copy-done.13, ...), custom_call_target="tpu_custom_call" | custom-call | flops 3000000000 | bytes 1048576 | tf_op jit(solution)/shard_map/attention/pallas_call | solution.py:405
  80.3 1.7 %collective-permute-start.10 = (bf16[32,896]{1,0:T(8,128)(2,1)}, bf16[32,896]{1,0:T(8,128)(2,1)S(1)}, u32[]{:S(2)}, u32[]{:S(2)}) collective-permute-start(bf16[32,896]{1,0:T(8,128)(2,1)} %get-tuple-element.33.m0), channel_id=1, source_target_pairs={{0,1},{1,2},{2,3},{3,0},{4,5},{5,6},{6,7},{7,4},{8,9},{9,10},{10,1... | collective-permute-start | bytes 172040 | tf_op jit(solution)/shard_map/ppermute | solution.py:359
  82.2 2.3 %collective-permute-start.12 = (bf16[32,896]{1,0:T(8,128)(2,1)}, bf16[32,896]{1,0:T(8,128)(2,1)S(1)}, u32[]{:S(2)}, u32[]{:S(2)}) collective-permute-start(bf16[32,896]{1,0:T(8,128)(2,1)} %get-tuple-element.33.m0), channel_id=1, source_target_pairs={{0,3},{1,0},{2,1},{3,2},{4,7},{5,4},{6,5},{7,6},{8,11},{9,8},{10,9... | collective-permute-start | bytes 172040 | tf_op jit(solution)/shard_map/ppermute | solution.py:359
  85.2 1.5 %collective-permute-done.11.m2 = bf16[32,896]{1,0:T(8,128)(2,1)S(1)} collective-permute-done((bf16[32,896]{1,0:T(8,128)(2,1)}, bf16[32,896]{1,0:T(8,128)(2,1)S(1)}, u32[]{:S(2)}, u32[]{:S(2)}) %collective-permute-start.11) | collective-permute-done | bytes 57376 | tf_op jit(solution)/shard_map/ppermute | solution.py:359
  87.4 2.7 %final.1 = bf16[512,128]{1,0:T(8,128)(2,1)} custom-call(bf16[32,896]{1,0:T(8,128)(2,1)} %get-tuple-element.33.m0, bf16[32,896]{1,0:T(8,128)(2,1)} %copy-done.2, bf16[32,896]{1,0:T(8,128)(2,1)} %copy-done.3, bf16[32,896]{1,0:T(8,128)(2,1)} %copy-done.4, f32[32,768]{1,0:T(8,128)} %get-tuple-element.34.token_in_ref, f32[512,128]{1,0:T(8,128)} %get-tuple-element.35.state_ref, ...), custom_call_target="tpu_custom_call" | custom-call | flops 100000000 | bytes 1048576 | tf_op jit(solution)/shard_map/final/pallas_call | solution.py:77
  (51 shorter events, 6.6 us)
Async XLA Ops:
  0.6 24.4 %copy-start.1 = (bf16[768,192]{0,1:T(8,128)(2,1)S(1)}, bf16[768,192]{0,1:T(8,128)(2,1)}, u32[]{:S(2)}) copy-start(bf16[768,192]{0,1:T(8,128)(2,1)} %param.37) | copy-start | bytes 884740
  0.6 35.6 %copy-start.5 = (bf16[128,16]{0,1:T(8,128)(2,1)S(1)}, bf16[128,16]{0,1:T(8,128)(2,1)}, u32[]{:S(2)}) copy-start(bf16[128,16]{0,1:T(8,128)(2,1)} %param.34) | copy-start | bytes 12292
  3.5 10.6 %collective-permute-start = (bf16[48,256]{1,0:T(8,128)(2,1)}, bf16[48,256]{1,0:T(8,128)(2,1)S(1)}, u32[]{:S(2)}, u32[]{:S(2)}) collective-permute-start(bf16[48,256]{1,0:T(8,128)(2,1)} %get-tuple-element.22), channel_id=1, source_target_pairs={{0,4},{4,8},{8,12},{12,16},{16,20},{20,24},{24,28},{28,32},{32,36}... | collective-permute-start | bytes 73736 | tf_op jit(solution)/shard_map/ppermute | solution.py:376
  8.5 5.7 %collective-permute-start.1 = (bf16[48,256]{1,0:T(8,128)(2,1)}, bf16[48,256]{1,0:T(8,128)(2,1)S(1)}, u32[]{:S(2)}, u32[]{:S(2)}) collective-permute-start(bf16[48,256]{1,0:T(8,128)(2,1)} %get-tuple-element.23), channel_id=1, source_target_pairs={{4,0},{8,4},{12,8},{16,12},{20,16},{24,20},{28,24},{32,28},{36,32}... | collective-permute-start | bytes 73736 | tf_op jit(solution)/shard_map/ppermute | solution.py:377
  23.5 13.4 %collective-permute-start.5 = (bf16[32,768]{1,0:T(8,128)(2,1)}, bf16[32,768]{1,0:T(8,128)(2,1)S(1)}, u32[]{:S(2)}, u32[]{:S(2)}) collective-permute-start(bf16[32,768]{1,0:T(8,128)(2,1)} %get-tuple-element.25), channel_id=1, source_target_pairs={{0,0},{1,64},{2,128},{3,192},{4,4},{5,68},{6,132},{7,196},{8,8},{9... | collective-permute-start | bytes 147464 | tf_op jit(solution)/shard_map/ppermute | solution.py:392
  28.1 46.4 %collective-permute-start.7 = (bf16[960,256]{1,0:T(8,128)(2,1)}, bf16[960,256]{1,0:T(8,128)(2,1)S(1)}, u32[]{:S(2)}, u32[]{:S(2)}) collective-permute-start(bf16[960,256]{1,0:T(8,128)(2,1)} %weights.1.w0), channel_id=1, source_target_pairs={{0,1},{1,2},{2,3},{3,0},{4,5},{5,6},{6,7},{7,4},{8,9},{9,10},{10,1... | collective-permute-start | bytes 1474568 | tf_op jit(solution)/shard_map/ppermute | solution.py:359
  31.0 43.5 %collective-permute-start.8 = (bf16[960,256]{1,0:T(8,128)(2,1)}, bf16[960,256]{1,0:T(8,128)(2,1)S(1)}, u32[]{:S(2)}, u32[]{:S(2)}) collective-permute-start(bf16[960,256]{1,0:T(8,128)(2,1)} %weights.1.w0), channel_id=1, source_target_pairs={{0,2},{1,3},{2,0},{3,1},{4,6},{5,7},{6,4},{7,5},{8,10},{9,11},{10,... | collective-permute-start | bytes 1474568 | tf_op jit(solution)/shard_map/ppermute | solution.py:359
  34.9 39.7 %collective-permute-start.9 = (bf16[960,256]{1,0:T(8,128)(2,1)}, bf16[960,256]{1,0:T(8,128)(2,1)S(1)}, u32[]{:S(2)}, u32[]{:S(2)}) collective-permute-start(bf16[960,256]{1,0:T(8,128)(2,1)} %weights.1.w0), channel_id=1, source_target_pairs={{0,3},{1,0},{2,1},{3,2},{4,7},{5,4},{6,5},{7,6},{8,11},{9,8},{10,9... | collective-permute-start | bytes 1474568 | tf_op jit(solution)/shard_map/ppermute | solution.py:359
  37.7 26.5 %all-to-all-start = ((bf16[8,32,768]{2,1,0:T(8,128)(2,1)}), bf16[8,32,768]{2,1,0:T(8,128)(2,1)S(1)}, u32[]{:S(2)}, u32[]{:S(2)}) async-start(bf16[8,32,768]{2,1,0:T(8,128)(2,1)} %broadcast_in_dim.2), calls=%async_computation | async-start | bytes 786432 | tf_op jit(solution)/shard_map/all_to_all | solution.py:394
  50.5 5.2 %copy-start.10 = (bf16[128,768]{1,0:T(8,128)(2,1)S(1)}, bf16[128,768]{1,0:T(8,128)(2,1)}, u32[]{:S(2)}) copy-start(bf16[128,768]{1,0:T(8,128)(2,1)} %get-tuple-element.24.t0) | copy-start | bytes 589828
  55.7 8.5 %collective-permute-start.2 = (bf16[128,768]{1,0:T(8,128)(2,1)S(1)}, bf16[128,768]{1,0:T(8,128)(2,1)S(1)}, u32[]{:S(2)}, u32[]{:S(2)}) collective-permute-start(bf16[128,768]{1,0:T(8,128)(2,1)S(1)} %copy-done.10), channel_id=1, source_target_pairs={{0,1},{1,2},{2,3},{3,0},{4,5},{5,6},{6,7},{7,4},{8,9},{9,10},{10,1... | collective-permute-start | bytes 589832 | tf_op jit(solution)/shard_map/ppermute | solution.py:359
  55.8 8.4 %collective-permute-start.3 = (bf16[128,768]{1,0:T(8,128)(2,1)S(1)}, bf16[128,768]{1,0:T(8,128)(2,1)S(1)}, u32[]{:S(2)}, u32[]{:S(2)}) collective-permute-start(bf16[128,768]{1,0:T(8,128)(2,1)S(1)} %copy-done.10), channel_id=1, source_target_pairs={{0,2},{1,3},{2,0},{3,1},{4,6},{5,7},{6,4},{7,5},{8,10},{9,11},{10,... | collective-permute-start | bytes 589832 | tf_op jit(solution)/shard_map/ppermute | solution.py:359
  64.2 9.7 %copy-start.11 = (bf16[128,768]{1,0:T(8,128)(2,1)}, bf16[128,768]{1,0:T(8,128)(2,1)S(1)}, u32[]{:S(2)}) copy-start(bf16[128,768]{1,0:T(8,128)(2,1)S(1)} %collective-permute-done.2.t1) | copy-start | bytes 589828
  64.2 10.3 %collective-permute-start.4 = (bf16[128,768]{1,0:T(8,128)(2,1)S(1)}, bf16[128,768]{1,0:T(8,128)(2,1)S(1)}, u32[]{:S(2)}, u32[]{:S(2)}) collective-permute-start(bf16[128,768]{1,0:T(8,128)(2,1)S(1)} %copy-done.10), channel_id=1, source_target_pairs={{0,3},{1,0},{2,1},{3,2},{4,7},{5,4},{6,5},{7,6},{8,11},{9,8},{10,9... | collective-permute-start | bytes 589832 | tf_op jit(solution)/shard_map/ppermute | solution.py:359
  64.2 9.7 %copy-start.12 = (bf16[128,768]{1,0:T(8,128)(2,1)}, bf16[128,768]{1,0:T(8,128)(2,1)S(1)}, u32[]{:S(2)}) copy-start(bf16[128,768]{1,0:T(8,128)(2,1)S(1)} %collective-permute-done.3.t2) | copy-start | bytes 589828
  64.2 9.7 %copy-start = (bf16[8,32,768]{2,1,0:T(8,128)(2,1)}, bf16[8,32,768]{2,1,0:T(8,128)(2,1)S(1)}, u32[]{:S(2)}) copy-start(bf16[8,32,768]{2,1,0:T(8,128)(2,1)S(1)} %all-to-all-done.own_ref) | copy-start | bytes 1179652
  64.2 10.3 %collective-permute-start.6 = (bf16[8,32,768]{2,1,0:T(8,128)(2,1)S(1)}, bf16[8,32,768]{2,1,0:T(8,128)(2,1)S(1)}, u32[]{:S(2)}, u32[]{:S(2)}) collective-permute-start(bf16[8,32,768]{2,1,0:T(8,128)(2,1)S(1)} %all-to-all-done.own_ref), channel_id=1, source_target_pairs={{0,4},{4,0},{8,12},{12,8},{16,20},{20,16},{24,28},{28,24},{32,36},... | collective-permute-start | bytes 1179656 | tf_op jit(solution)/shard_map/ppermute | solution.py:397
  74.5 1.0 %copy-start.7 = (bf16[960,256]{1,0:T(8,128)(2,1)}, bf16[960,256]{1,0:T(8,128)(2,1)S(1)}, u32[]{:S(2)}) copy-start(bf16[960,256]{1,0:T(8,128)(2,1)S(1)} %collective-permute-done.8.w2) | copy-start | bytes 1474564
  74.6 1.2 %copy-start.8 = (bf16[960,256]{1,0:T(8,128)(2,1)}, bf16[960,256]{1,0:T(8,128)(2,1)S(1)}, u32[]{:S(2)}) copy-start(bf16[960,256]{1,0:T(8,128)(2,1)S(1)} %collective-permute-done.9.w3) | copy-start | bytes 1474564
  74.6 1.2 %copy-start.9 = (bf16[8,32,768]{2,1,0:T(8,128)(2,1)}, bf16[8,32,768]{2,1,0:T(8,128)(2,1)S(1)}, u32[]{:S(2)}) copy-start(bf16[8,32,768]{2,1,0:T(8,128)(2,1)S(1)} %collective-permute-done.6.other_ref) | copy-start | bytes 1179652
  80.3 5.0 %collective-permute-start.10 = (bf16[32,896]{1,0:T(8,128)(2,1)}, bf16[32,896]{1,0:T(8,128)(2,1)S(1)}, u32[]{:S(2)}, u32[]{:S(2)}) collective-permute-start(bf16[32,896]{1,0:T(8,128)(2,1)} %get-tuple-element.33.m0), channel_id=1, source_target_pairs={{0,1},{1,2},{2,3},{3,0},{4,5},{5,6},{6,7},{7,4},{8,9},{9,10},{10,1... | collective-permute-start | bytes 172040 | tf_op jit(solution)/shard_map/ppermute | solution.py:359
  82.0 4.7 %collective-permute-start.11 = (bf16[32,896]{1,0:T(8,128)(2,1)}, bf16[32,896]{1,0:T(8,128)(2,1)S(1)}, u32[]{:S(2)}, u32[]{:S(2)}) collective-permute-start(bf16[32,896]{1,0:T(8,128)(2,1)} %get-tuple-element.33.m0), channel_id=1, source_target_pairs={{0,2},{1,3},{2,0},{3,1},{4,6},{5,7},{6,4},{7,5},{8,10},{9,11},{10,... | collective-permute-start | bytes 172040 | tf_op jit(solution)/shard_map/ppermute | solution.py:359
  82.2 4.6 %collective-permute-start.12 = (bf16[32,896]{1,0:T(8,128)(2,1)}, bf16[32,896]{1,0:T(8,128)(2,1)S(1)}, u32[]{:S(2)}, u32[]{:S(2)}) collective-permute-start(bf16[32,896]{1,0:T(8,128)(2,1)} %get-tuple-element.33.m0), channel_id=1, source_target_pairs={{0,3},{1,0},{2,1},{3,2},{4,7},{5,4},{6,5},{7,6},{8,11},{9,8},{10,9... | collective-permute-start | bytes 172040 | tf_op jit(solution)/shard_map/ppermute | solution.py:359
  85.2 1.5 %copy-start.2 = (bf16[32,896]{1,0:T(8,128)(2,1)}, bf16[32,896]{1,0:T(8,128)(2,1)S(1)}, u32[]{:S(2)}) copy-start(bf16[32,896]{1,0:T(8,128)(2,1)S(1)} %collective-permute-done.10.m1) | copy-start | bytes 172036
  (6 other events, 4.0 us)

commit v2 on v1

v2 whole, which is shorter than its diff:
```python
import math

import jax
import jax.numpy as jnp
from jax import lax
from jax.experimental import pallas as pl
from jax.experimental.pallas import tpu as pltpu
from jax.sharding import PartitionSpec as P

H_A = 4
H_T = 16
WIN_Q = 32
WIN_K = 128
MARGIN = (WIN_K - WIN_Q) // 2
STEPS = 200
EPS = 1e-05
SIGMA_DATA = 16.0
SIGMA_MAX = 160.0
SIGMA_MIN = 0.0004
RHO = 7
MASKED = -1000000000.0

NY = 4
NZ = 8
NK = 2
NC = 4

ATOMS = 512
TOKS = 32
C_A = 128
C_S = 768
GROUP = 4
HEAD = 48
GW = GROUP * HEAD
FOLD = GW * C_A // C_S
ROWS = 8
COLS = 512
CHUNKS = ((0, 1), (1, 2), (3, 1))

F32 = jnp.float32
BF = jnp.bfloat16


def dot(a, b):
    return jnp.dot(a, b, preferred_element_type=F32)


def dot_nt(a, b):
    return lax.dot_general(a, b, (((1,), (1,)), ((), ())), preferred_element_type=F32)


def iota(shape, dim):
    return lax.broadcasted_iota(jnp.int32, shape, dim)


def hi_lo(v):
    hi = v.astype(BF)
    return hi, (v - hi.astype(F32)).astype(BF)


def three(v):
    hi = v.astype(BF)
    rest = v - hi.astype(F32)
    mid = rest.astype(BF)
    return hi, mid, (rest - mid.astype(F32)).astype(BF)


def normalize(values):
    average = jnp.mean(values, axis=-1, keepdims=True)
    centred = values - average
    variance = jnp.mean(centred * centred, axis=-1, keepdims=True)
    return centred * lax.rsqrt(variance + EPS)


class Fetched:
    def __init__(self, copy, buffer):
        self.copy, self.buffer, self.here, self.shape = copy, buffer, False, buffer.shape

    def arrive(self):
        if not self.here:
            self.copy.wait()
            self.here = True

    def __getitem__(self, index):
        self.arrive()
        return self.buffer[index]


class Sent:
    def __init__(self, copy, buffer):
        self.copy, self.buffer, self.gone = copy, buffer, False

    def __setitem__(self, index, value):
        self.buffer[index] = value

    def send(self):
        if not self.gone:
            self.copy.start()
            self.gone = True


def call(kernel, outs, args, *, name, smem=(), scratch=(), far=(), aliases=None, flops=0):
    n, m, k = len(args), len(outs), len(scratch)
    fetch = [i for i in range(n) if i not in smem and i not in far]
    send = [i for i in range(m) if n + i not in far]

    def body(*refs):
        ins, given, rest = list(refs[:n]), list(refs[n : n + m]), refs[n + m : n + m + k]
        buffers, sems = refs[n + m + k : -1], refs[-1]
        for slot, i in enumerate(fetch):
            copy = pltpu.make_async_copy(ins[i], buffers[slot], sems.at[slot])
            copy.start()
            ins[i] = Fetched(copy, buffers[slot])
        for slot, i in enumerate(send, len(fetch)):
            given[i] = Sent(pltpu.make_async_copy(buffers[slot], given[i], sems.at[slot]), buffers[slot])
        kernel(*ins, *given, *rest)
        for i in fetch:
            ins[i].arrive()
        for i in send:
            given[i].send()
        for i in send:
            given[i].copy.wait()

    return pl.pallas_call(
        body,
        in_specs=[pl.BlockSpec(memory_space=pltpu.SMEM if i in smem else pltpu.HBM) for i in range(n)],
        out_specs=[pl.BlockSpec(memory_space=pltpu.HBM)] * m,
        out_shape=[jax.ShapeDtypeStruct(s, d) for s, d in outs],
        scratch_shapes=[
            *scratch,
            *(pltpu.VMEM(args[i].shape, args[i].dtype) for i in fetch),
            *(pltpu.VMEM(*outs[i]) for i in send),
            pltpu.SemaphoreType.DMA((max(len(fetch) + len(send), 1),)),
        ],
        input_output_aliases=aliases or {},
        compiler_params=pltpu.CompilerParams(vmem_limit_bytes=56 * 2**20),
        cost_estimate=pl.CostEstimate(flops=flops, bytes_accessed=1024, transcendentals=0),
        name=name,
    )(*args)


def atom_in_kernel(
    noise_ref, pos_ref, wpos_ref, single_ref, counts_ref, initial_ref, normed_ref, inner_ref, outer_ref
):
    level = jnp.full((1, C_A), noise_ref[0], jnp.int32).astype(F32)
    upper = SIGMA_MAX ** (1.0 / RHO)
    lower = SIGMA_MIN ** (1.0 / RHO)
    root = upper + level / (STEPS - 1) * (lower - upper)
    square = root * root
    sigma = square * square * square * root
    gain = 1.0 / jnp.sqrt(sigma * sigma + SIGMA_DATA * SIGMA_DATA)
    lifted = lax.dot_general(
        pos_ref[...], wpos_ref[...] * gain, (((0,), (0,)), ((), ())),
        precision=lax.Precision.HIGHEST, preferred_element_type=F32,
    )
    initial = single_ref[...].astype(F32) + lifted
    normed = normalize(initial).astype(BF)
    total = jnp.sum(counts_ref[...], axis=1, keepdims=True)
    slots = iota((ATOMS, C_A), 0)
    live = jnp.where(slots < total, 1.0, 0.0).astype(BF)
    both = jnp.concatenate([normed, live], axis=1)
    first, last = both[:MARGIN].astype(F32), both[ATOMS - MARGIN :].astype(F32)
    lower = lax.axis_index("atom") % NK == 0
    inner_ref[...] = jnp.where(lower, last, first).astype(BF)
    inner_ref.send()
    outer_ref[...] = jnp.where(lower, first, last).astype(BF)
    outer_ref.send()
    normed_ref[...] = normed
    normed_ref.send()
    initial_ref[...] = initial
    initial_ref.send()


def pack_kernel(twv_ref, two_ref, back_ref, _, packed_ref):
    folded = dot(two_ref[...], back_ref[...]).astype(BF)
    packed_ref[GW:, :] = jnp.concatenate(
        [folded[i * FOLD : (i + 1) * FOLD] for i in range(GW // FOLD)], axis=1
    )
    packed_ref[:GW, :] = twv_ref[...]


def spans(counts_ref):
    row = counts_ref[...].astype(F32)
    grid = jnp.broadcast_to(row, (TOKS, TOKS))
    r, c = iota((TOKS, TOKS), 0), iota((TOKS, TOKS), 1)
    count_col = jnp.sum(jnp.where(r == c, grid, 0.0), axis=1, keepdims=True)
    end_col = jnp.sum(jnp.where(c <= r, grid, 0.0), axis=1, keepdims=True)
    end_row = jnp.sum(jnp.where(r <= c, jnp.broadcast_to(count_col, (TOKS, TOKS)), 0.0), axis=0, keepdims=True)
    return row, count_col, end_row, end_col


def atom_mid_kernel(
    normed_ref, inner_ref, outer_ref, counts_ref, wq_ref, wk_ref, wv_ref, initial_ref, wo_ref, pool_ref,
    single_ref, twq_ref, twk_ref, state_ref, token_in_ref, token_normed_ref, t_ref,
):
    lower = lax.axis_index("atom") % NK == 0
    inner, outer = inner_ref[...].astype(F32), outer_ref[...].astype(F32)
    before = jnp.where(lower, outer, inner).astype(BF)
    after = jnp.where(lower, inner, outer).astype(BF)
    normed = normed_ref[...]
    _, count_col, _, end_col = spans(counts_ref)
    slots = iota((TOKS, ATOMS), 1).astype(F32)
    onehot = jnp.where((slots < end_col) & (slots >= end_col - count_col), 1.0, 0.0).astype(BF)
    wide = jnp.concatenate([before[:, :C_A], normed, after[:, :C_A]], axis=0)
    n_before = jnp.sum(before[:, C_A:].astype(F32), axis=0, keepdims=True)
    n_after = jnp.sum(after[:, C_A:].astype(F32), axis=0, keepdims=True)
    n_own = jnp.sum(counts_ref[...].astype(F32), axis=1, keepdims=True)
    queries = dot(normed, wq_ref[...]).astype(BF)
    keys = dot(wide, wk_ref[...]).astype(BF)
    values = dot(wide, wv_ref[...]).astype(BF)
    stacked = H_A * WIN_Q
    mine = iota((stacked, C_A), 1) // (C_A // H_A) == iota((stacked, C_A), 0) // WIN_Q
    pick = jnp.where(mine, 1.0, 0.0).astype(BF)
    scale = 1.0 / math.sqrt(C_A // H_A)
    windows = ATOMS // WIN_Q
    scores = []
    for w in range(windows):
        q = queries[w * WIN_Q : (w + 1) * WIN_Q]
        q4 = jnp.concatenate([q] * H_A, axis=0) * pick
        slot = (iota((1, WIN_K), 1) + (w * WIN_Q - MARGIN)).astype(F32)
        bound = jnp.broadcast_to(n_own, (1, WIN_K))
        if w * WIN_Q < MARGIN:
            bound = jnp.where(slot < 0, n_before - MARGIN, bound)
        if w * WIN_Q - MARGIN + WIN_K > ATOMS:
            bound = jnp.where(slot >= ATOMS, n_after + ATOMS, bound)
        penalty = jnp.where(slot < bound, 0.0, MASKED)
        scores.append(dot_nt(q4, keys[w * WIN_Q : w * WIN_Q + WIN_K]) * scale + penalty)
    scores = jnp.concatenate(scores, axis=0)
    p = jnp.exp(scores - jnp.max(scores, axis=1, keepdims=True))
    weight = (p / jnp.sum(p, axis=1, keepdims=True)).astype(BF)
    mixes = []
    for w in range(windows):
        o = dot(weight[w * stacked : (w + 1) * stacked], values[w * WIN_Q : w * WIN_Q + WIN_K])
        o = jnp.where(mine, o, 0.0)
        mixes.append(o[:32] + o[32:64] + o[64:96] + o[96:])
    mix = jnp.concatenate(mixes, axis=0).astype(BF)
    state = initial_ref[...] + dot(mix, wo_ref[...])
    state_ref[...] = state
    state_ref.send()
    features = jnp.maximum(dot(state.astype(BF), pool_ref[...]), 0.0)
    f_hi, f_lo = hi_lo(features)
    sums = dot(onehot, f_hi) + dot(onehot, f_lo)
    token_in = single_ref[...].astype(F32) + sums / count_col
    token_normed = normalize(token_in).astype(BF)
    token_normed_ref[...] = token_normed
    token_normed_ref.send()
    token_in_ref[...] = token_in
    token_in_ref.send()
    tq = dot_nt(token_normed, twq_ref[...]).astype(BF).astype(F32)
    lanes = iota((ROWS, GW), 1) // HEAD
    pieces = [
        jnp.where(lanes == h, tq[ib * ROWS : (ib + 1) * ROWS], 0.0)
        for ib in range(TOKS // ROWS)
        for h in range(GROUP)
    ]
    spread = jnp.concatenate(pieces, axis=0).astype(BF)
    t_ref[...] = (dot(spread, twk_ref[...]) * (1.0 / math.sqrt(HEAD))).astype(BF)


def pair_kernel(x_ref, w1_ref, w2_ref, wb_ref, *refs, start, count):
    out_ref, bias_ref, x_s, y_s, b_s, w1_s, w2_s, in_sem, out_sem, bias_sem = refs[-10:]
    pairs = ROWS // 2
    arrivals = [
        pltpu.make_async_copy(x_ref.at[pl.ds((start + i) * ROWS, ROWS)], x_s.at[i], in_sem.at[i])
        for i in range(count)
    ]
    leaving = [
        pltpu.make_async_copy(
            y_s.at[i, pl.ds(k * pairs, pairs)],
            out_ref.at[pl.ds((start + i) * ROWS + k * pairs, pairs)],
            out_sem.at[2 * i + k],
        )
        for i in range(count)
        for k in range(2)
    ]
    biases = [
        pltpu.make_async_copy(b_s.at[:, i], bias_ref.at[:, i], bias_sem.at[i]) for i in range(count)
    ]
    for copy in arrivals:
        copy.start()
    r, c = iota((256, 256), 0), iota((256, 256), 1)
    same = (r // 128) == (c // 128)
    centre = (jnp.where(r == c, 1.0, 0.0) - jnp.where(same, 1.0 / 128, 0.0)).astype(BF)
    w1_s[:, :256] = w1_ref[:, :256] * jnp.asarray(0.5, BF)
    w1_s[:, 256:] = w1_ref[:, 256:]
    w2 = w2_ref[...]
    w2_s[:, :128] = w2
    wide = w2.astype(F32)
    w2_s[:, 128:] = (wide - jnp.mean(wide, axis=1, keepdims=True)).astype(BF)
    head, lane = iota((H_T, 128), 0), iota((H_T, 128), 1)
    wb = wb_ref[...]
    heads = [
        lax.dot_general(
            wb, jnp.where(lane == head * ROWS + g, 1.0, 0.0).astype(BF), (((0,), (0,)), ((), ())),
            preferred_element_type=F32,
        ).astype(BF)
        for g in range(ROWS)
    ]
    heads = [jnp.concatenate([heads[p], heads[pairs + p]], axis=0) for p in range(pairs)]
    m = pairs * COLS
    for step in range(count):
        arrivals[step].wait()
        xs = [x_s[step, :pairs].reshape(m, 128), x_s[step, pairs:].reshape(m, 128)]
        c = dot(jnp.concatenate(xs, axis=1), centre)
        kept = []
        for k in range(2):
            ck = c[:, 128 * k : 128 * k + 128]
            n = (ck * lax.rsqrt(jnp.mean(ck * ck, axis=1, keepdims=True) + EPS)).astype(BF)
            g = dot(n, w1_s[...])
            gate, up = g[:, :256], g[:, 256:]
            h = ((gate + gate * jnp.tanh(gate)) * up).astype(BF)
            u = dot(h, w2_s[...])
            y_s[step, k * pairs : (k + 1) * pairs] = (
                (xs[k].astype(F32) + u[:, :128]).astype(BF).reshape(pairs, COLS, 128)
            )
            c2 = ck + u[:, 128:]
            kept.append((c2 * lax.rsqrt(jnp.mean(c2 * c2, axis=1, keepdims=True) + EPS)).astype(BF))
            leaving[2 * step + k].start()
        cc = jnp.concatenate(kept, axis=1)
        acc = jnp.zeros((COLS, 128), F32)
        for p in range(pairs):
            acc = acc + dot(cc[p * COLS : (p + 1) * COLS], heads[p])
        b_s[:, step] = acc.T.astype(BF).reshape(NC, GROUP * ROWS, COLS)
        biases[step].start()
    for copy in (*leaving, *biases):
        copy.wait()


def pair_call(x, w1, w2, wb, prior, after, start, count):
    block = (count, ROWS, COLS, 128)
    more = [a for a in (prior, after) if a is not None]
    n = 4 + len(more)
    return call(
        lambda *refs: pair_kernel(*refs, start=start, count=count),
        [(x.shape, BF), ((NC, count, GROUP * ROWS, COLS), BF)],
        (x, w1, w2, wb, *more),
        name="pair", far=(0, *range(4, n + 2)), aliases={} if prior is None else {4: 0},
        scratch=[
            pltpu.VMEM(block, BF), pltpu.VMEM(block, BF), pltpu.VMEM((NC, count, GROUP * ROWS, COLS), BF),
            pltpu.VMEM((128, 512), BF), pltpu.VMEM((256, 256), BF),
            *(pltpu.SemaphoreType.DMA((i * count,)) for i in (1, 2, 1)),
        ],
        flops=1000,
    )


def attention_kernel(
    t0, t1, t2, t3, own_ref, other_ref, w0, w1, w2, w3, *refs
):
    *biases, msg_ref, back_ref, xk_s, o_s = refs
    col, core = lax.axis_index("col"), lax.axis_index("atom") % NK
    wide = GROUP * TOKS
    packed = (w0, w1, w2, w3)
    t = jnp.concatenate([t0[...], t1[...], t2[...], t3[...]], axis=0)
    xk_s[:, pl.ds(core, 1)] = own_ref[...].reshape(NZ, 1, TOKS, C_S)
    xk_s[:, pl.ds(1 - core, 1)] = other_ref[...].reshape(NZ, 1, TOKS, C_S)
    xk = xk_s[...].reshape(COLS, C_S)
    scores = dot_nt(t, xk)
    groups = [(col + NC - s) % NC for s in range(NC)]
    scores = jnp.concatenate(
        [
            scores[s * wide : (s + 1) * wide]
            + jnp.concatenate(
                [b[pl.ds(groups[s], 1)].reshape(b.shape[1] * GROUP * ROWS, COLS) for b in biases], axis=0
            ).astype(F32)
            for s in range(NC)
        ],
        axis=0,
    )
    top = jnp.max(scores, axis=1, keepdims=True)
    p = jnp.exp(scores - top)
    total = jnp.sum(p, axis=1, keepdims=True)
    mixed = (dot(p.astype(BF), xk) / total).astype(BF)
    blocks = TOKS // ROWS
    lane_head = iota((1, GROUP, 1, GW), 3) // HEAD
    row_head = iota((1, GROUP, 1, GW), 1)
    lane16 = iota((1, GROUP, 1, 128), 3) % H_T
    row16 = iota((1, GROUP, 1, 128), 1)
    tops = jnp.zeros((TOKS, 128), F32)
    totals = jnp.zeros((TOKS, 128), F32)
    for s, w in enumerate(packed):
        lo = s * wide
        o = dot_nt(mixed[lo : lo + wide], w[:GW, :]).reshape(blocks, GROUP, ROWS, GW)
        o = jnp.sum(jnp.where(lane_head == row_head, o, 0.0), axis=1).reshape(TOKS, GW)
        o_s[pl.ds(groups[s], 1)] = o.reshape(1, TOKS, GW)
        folded = jnp.concatenate([w[GW:, i * C_A : (i + 1) * C_A] for i in range(GW // FOLD)], axis=0)
        back_ref.buffer[pl.ds(groups[s], 1)] = folded.reshape(1, GW, C_A)
        here = lane16 == row16 + groups[s] * GROUP
        for value, which in ((top, 0), (total, 1)):
            part = jnp.broadcast_to(value[lo : lo + wide], (wide, 128)).reshape(blocks, GROUP, ROWS, 128)
            part = jnp.sum(jnp.where(here, part, 0.0), axis=1).reshape(TOKS, 128)
            if which == 0:
                tops = tops + part
            else:
                totals = totals + part
    part_of = iota((TOKS, 128), 1) // H_T
    stats = jnp.zeros((TOKS, 128), F32)
    for i, piece in enumerate((*three(tops), *three(totals))):
        stats = jnp.where(part_of == i, piece.astype(F32), stats)
    msg_ref[...] = jnp.concatenate([o_s[g] for g in range(NC)] + [stats], axis=1).astype(BF)


def final_kernel(m0, m1, m2, m3, token_in_ref, state_ref, counts_ref, wback_ref, back_ref, out_ref):
    msgs = [m0[...], m1[...], m2[...], m3[...]]
    r, c = iota((128, 256), 0), iota((128, 256), 1)
    pick = ((r // H_T) // 3 == c // 128) & (r % H_T == c % H_T) & (r < 6 * H_T)
    stats = dot(jnp.concatenate([m[:, C_S:] for m in msgs], axis=0), jnp.where(pick, 1.0, 0.0).astype(BF))
    tops = [stats[i * TOKS : (i + 1) * TOKS, :128] for i in range(NC)]
    totals = [stats[i * TOKS : (i + 1) * TOKS, 128:] for i in range(NC)]
    top = jnp.maximum(jnp.maximum(tops[0], tops[1]), jnp.maximum(tops[2], tops[3]))
    shares = [l * jnp.exp(t - top) for l, t in zip(totals, tops)]
    whole = shares[0] + shares[1] + shares[2] + shares[3]
    r, c = iota((128, C_S), 0), iota((128, C_S), 1)
    expand = jnp.where((r % H_T == c // HEAD) & (r < 2 * H_T), 1.0, 0.0).astype(BF)
    part_of = iota((TOKS, 128), 1) // H_T
    coefs = []
    for share in shares:
        hi, lo = hi_lo(share / whole)
        coefs.append(jnp.where(part_of == 0, hi.astype(F32), lo.astype(F32)).astype(BF))
    scale = dot(jnp.concatenate(coefs, axis=0), expand)
    mix = jnp.zeros((TOKS, C_S), F32)
    for i, m in enumerate(msgs):
        mix = mix + scale[i * TOKS : (i + 1) * TOKS] * m[:, :C_S].astype(F32)
    folded = dot(mix.astype(BF), back_ref[...].reshape(C_S, C_A))
    returned = dot(token_in_ref[...].astype(BF), wback_ref[...]) + folded
    row, _, end_row, _ = spans(counts_ref)
    slots = iota((ATOMS, TOKS), 0).astype(F32)
    onehot = jnp.where((slots < end_row) & (slots >= end_row - row), 1.0, 0.0).astype(BF)
    r_hi, r_lo = hi_lo(returned)
    spread = dot(onehot, r_hi) + dot(onehot, r_lo)
    alive = iota((ATOMS, C_A), 0) < jnp.sum(counts_ref[...], axis=1, keepdims=True)
    out_ref[...] = jnp.where(alive, state_ref[...] + spread, 0.0).astype(BF)


def around(array, axis, size):
    return [lax.ppermute(array, axis, [(i, (i + s) % size) for i in range(size)]) for s in range(1, size)]


def local(
    atom_single, positions, noise_index, token_counts, token_single, pair_repr, w_pos, atom_wq, atom_wk, atom_wv,
    atom_wo, w_pool, trans_w1, trans_w2, w_bias, token_wq, token_wk, token_wv, token_wo, w_back,
):
    atoms = NY * NZ * NK
    counts = token_counts.reshape(1, TOKS)
    initial, normed, inner, outer = call(
        atom_in_kernel,
        [((ATOMS, C_A), F32), ((ATOMS, C_A), BF)] + [((MARGIN, 2 * C_A), BF)] * 2,
        (noise_index, positions, w_pos, atom_single, counts),
        name="atom_in", smem=(0,), flops=1000,
    )
    outer = lax.ppermute(outer, "atom", [(i, i + (1 if i % 2 else -1)) for i in range(1, atoms - 1)])
    inner = lax.ppermute(inner, "atom", [(i, i ^ 1) for i in range(atoms)])
    (packed,) = call(
        pack_kernel, [((GW + FOLD, C_S), BF)], (token_wv.T, token_wo, w_back, normed), name="pack", far=(3,), flops=1000
    )
    weights = [packed] + around(packed, "col", NC)
    pair_out, biases = None, []

    def pair(i, after=None):
        nonlocal pair_out
        pair_out, bias = pair_call(pair_repr, trans_w1, trans_w2, w_bias.T, pair_out, after, *CHUNKS[i])
        biases.append(bias)

    pair(0)
    state, token_in, token_normed, t_own = call(
        atom_mid_kernel,
        [((ATOMS, C_A), F32), ((TOKS, C_S), F32), ((TOKS, C_S), BF), ((GROUP * TOKS, C_S), BF)],
        (
            normed, inner, outer, counts, atom_wq, atom_wk, atom_wv, initial, atom_wo, w_pool, token_single,
            token_wq.T, token_wk.T,
        ),
        name="atom_mid", flops=1000,
    )
    flip = [
        ((y * NZ * NK + i) * NC + x, (x * NZ * NK + i) * NC + y)
        for y in range(NY) for i in range(NZ * NK) for x in range(NC)
    ]
    turned = lax.ppermute(token_normed, ("atom", "col"), flip)
    lines = [[(y * NZ + z) * NK + k for z in range(NZ)] for y in range(NY) for k in range(NK)]
    turned, biases[0], weights = lax.optimization_barrier((turned, biases[0], weights))
    queries = around(t_own, "col", NC)
    own = lax.all_to_all(
        jnp.broadcast_to(turned[None], (NZ, TOKS, C_S)), "atom", 0, 0, axis_index_groups=lines, tiled=True
    )
    pair(1)
    own, biases[1], queries = lax.optimization_barrier((own, biases[1], queries))
    other = lax.ppermute(own, "atom", [(i, i ^ 1) for i in range(atoms)])
    for i in range(2, len(CHUNKS)):
        pair(i)

    msg, back = call(
        attention_kernel,
        [((TOKS, C_S + 128), BF), ((NC, GW, C_A), BF)],
        (t_own, *queries, own, other, *weights, *biases),
        name="attention", flops=1000,
        scratch=[pltpu.VMEM((NZ, NK, TOKS, C_S), BF), pltpu.VMEM((NC, TOKS, GW), F32)],
    )
    msgs = [msg] + around(msg, "col", NC)
    (atom_out,) = call(
        final_kernel, [((ATOMS, C_A), BF)], (*msgs, token_in, state, counts, w_back, back),
        name="final", flops=1000,
    )
    return (atom_out, pair_out)


def solution(mesh):
    placed = (
        P("atom", None), P(None, "atom"), P(), P("atom"), P("atom", None), P("atom", "col", None),
        P(), P(), P(), P(), P(), P(), P(), P(), P(),
        P(None, "col"), P(None, "col"), P(None, "col"), P("col", None), P(),
    )
    return jax.shard_map(
        local,
        mesh=mesh,
        in_specs=placed,
        out_specs=(P("atom", None), P("atom", "col", None)),
        check_vma=False,
    )
```

time: 90.7 us -> 81.6 us (0.90)
  local copies, waits for them, and re-layouts: 8.69 us -> 2.86 us
  Pallas kernels: 40.8 us -> 35.1 us
  waiting for transfers between devices: 4.46 us -> 9.17 us
  starting transfers between devices: 34.1 us -> 32.4 us
    unnamed x36 -> x28, local copies, waits for them, and re-layouts: 7.91 us -> 2 us
    pallas_call x9 -> x8, Pallas kernels: 40.8 us -> 35.1 us  [call(): pl.pallas_call(body, in_specs=[pl.BlockSpec(memory_space=pltpu.SMEM if i...]
    ppermute x1, starting transfers between devices: 4.56 us -> 0.76 us  [local(): other = lax.ppermute(own, 'atom', [(i, i ^ 1) for i in range(atoms)])]
    ppermute x9, starting transfers between devices: 13.5 us -> 16.1 us  [around(): lax.ppermute(array, axis, [(i, (i + s) % size) for i in range(size)])]
    ppermute x9, waiting for transfers between devices: 4.45 us -> 6.98 us  [around(): lax.ppermute(array, axis, [(i, (i + s) % size) for i in range(size)])]
    ppermute x2, waiting for transfers between devices: 0.01 us -> 2.18 us  [the longest x1 2.18 us: local(): lax.ppermute(outer, 'atom', [(i, i + (1 if i % 2 else -1)) for i in range...]
    ppermute x2, starting transfers between devices: 6.84 us -> 4.94 us  [the longest x1 3.43 us: local(): lax.ppermute(outer, 'atom', [(i, i + (1 if i % 2 else -1)) for i in range...]
    all_to_all x1, starting transfers between devices: 7.68 us -> 8.97 us  [local(): lax.all_to_all(jnp.broadcast_to(turned[None], (NZ, TOKS, C_S)), 'atom', 0...]
  transfers between devices with their start and end apart: 14 -> 14, of which waited for: 3 -> 4; matrix products, arithmetic and copies ran while one was open for 7% -> 0% of each run, Pallas kernels for 25% -> 28%
where the time goes in v2:
time: 81.6 us; the launch traced here: 81.2 us
  Pallas kernels  35.1 us (43%)
  starting transfers between devices  32.4 us (40%)
  waiting for transfers between devices  9.17 us (11%)
  local copies, waits for them, and re-layouts  2.86 us (4%)
  between operations  1.7 us (2%)
    pallas_call x8, Pallas kernels, call(): pl.pallas_call(body, in_specs=[pl.BlockSpec(memory_space=pltpu.SMEM if i...  35.1 us
    ppermute x9, starting transfers between devices, around(): lax.ppermute(array, axis, [(i, (i + s) % size) for i in range(size)])  16.1 us
    all_to_all x1, starting transfers between devices, local(): lax.all_to_all(jnp.broadcast_to(turned[None], (NZ, TOKS, C_S)), 'atom', 0...  8.97 us
    ppermute x9, waiting for transfers between devices, around(): lax.ppermute(array, axis, [(i, (i + s) % size) for i in range(size)])  6.98 us
    ppermute x1, starting transfers between devices, local(): lax.ppermute(outer, 'atom', [(i, i + (1 if i % 2 else -1)) for i in range...  3.43 us
    ppermute x1, waiting for transfers between devices, local(): lax.ppermute(outer, 'atom', [(i, i + (1 if i % 2 else -1)) for i in range...  2.18 us
    unnamed x28, local copies, waits for them, and re-layouts  2 us
  transfers between devices with their start and end apart: 14, of which 4 were waited for; matrix products, arithmetic and copies ran while one was open for 0% of the time, Pallas kernels for 28%

profile of v2, /device:TPU:1, one launch (start us, length us, event | category | flops | bytes accessed | tf_op | source)
XLA Modules:
  0.0 81.2 jit_solution(16683859553594584602)
XLA Ops:
  1.3 2.3 %atom_in.1 = (f32[512,128]{1,0:T(8,128)}, bf16[512,128]{1,0:T(8,128)(2,1)}, bf16[48,256]{1,0:T(8,128)(2,1)}, bf16[48,256]{1,0:T(8,128)(2,1)}) custom-call(s32[1]{0:T(128)S(6)} %copy.26.refs_0_, f32[3,512]{1,0:T(4,128)} %refs_1_.5, f32[3,128]{1,0:T(4,128)} %refs_2_.5, bf16[512,128]{1,0:T(8,128)(2,1)} %refs_3_.1, s32[1,32]{1,0:T(1,128)} %bitcast.11), custom_call_target="tpu_custom_call" | custom-call | flops 1000 | bytes 1024 | tf_op jit(solution)/shard_map/atom_in/pallas_call | solution.py:124
  3.6 2.1 %pack.1.refs_6_ = bf16[224,768]{1,0:T(8,128)(2,1)} custom-call(bf16[192,768]{1,0:T(8,128)(2,1)} %bitcast.5, bf16[192,768]{1,0:T(8,128)(2,1)} %refs_1_.7, bf16[768,128]{1,0:T(8,128)(2,1)} %refs_7_.1, bf16[512,128]{1,0:T(8,128)(2,1)} %get-tuple-element.29.refs_0_.refs_3_), custom_call_target="tpu_custom_call" | custom-call | flops 1000 | bytes 1024 | tf_op jit(solution)/shard_map/pack/pallas_call | solution.py:124
  5.7 3.4 %collective-permute-start.5 = (bf16[224,768]{1,0:T(8,128)(2,1)}, bf16[224,768]{1,0:T(8,128)(2,1)S(1)}, u32[]{:S(2)}, u32[]{:S(2)}) collective-permute-start(bf16[224,768]{1,0:T(8,128)(2,1)} %pack.1.refs_6_), channel_id=1, source_target_pairs={{0,3},{1,0},{2,1},{3,2},{4,7},{5,4},{6,5},{7,6},{8,11},{9,8},{10,9... | collective-permute-start | bytes 1032200 | tf_op jit(solution)/shard_map/ppermute | solution.py:436
  10.2 1.5 %collective-permute-start = (bf16[48,256]{1,0:T(8,128)(2,1)}, bf16[48,256]{1,0:T(8,128)(2,1)S(1)}, u32[]{:S(2)}, u32[]{:S(2)}) collective-permute-start(bf16[48,256]{1,0:T(8,128)(2,1)} %get-tuple-element.30), channel_id=1, source_target_pairs={{0,4},{4,0},{8,12},{12,8},{16,20},{20,16},{24,28},{28,24},{32,36},... | collective-permute-start | bytes 73736 | tf_op jit(solution)/shard_map/ppermute | solution.py:452
  11.7 3.4 %collective-permute-start.1 = (bf16[48,256]{1,0:T(8,128)(2,1)}, bf16[48,256]{1,0:T(8,128)(2,1)S(1)}, u32[]{:S(2)}, u32[]{:S(2)}) collective-permute-start(bf16[48,256]{1,0:T(8,128)(2,1)} %get-tuple-element.31), channel_id=1, source_target_pairs={{4,8},{8,4},{12,16},{16,12},{20,24},{24,20},{28,32},{32,28},{36,40... | collective-permute-start | bytes 73736 | tf_op jit(solution)/shard_map/ppermute | solution.py:451
  15.2 2.2 %collective-permute-done.1.refs_2_ = bf16[48,256]{1,0:T(8,128)(2,1)S(1)} collective-permute-done((bf16[48,256]{1,0:T(8,128)(2,1)}, bf16[48,256]{1,0:T(8,128)(2,1)S(1)}, u32[]{:S(2)}, u32[]{:S(2)}) %collective-permute-start.1) | collective-permute-done | bytes 24608 | tf_op jit(solution)/shard_map/ppermute | solution.py:451
  18.0 4.8 %atom_mid.1 = (f32[512,128]{1,0:T(8,128)}, f32[32,768]{1,0:T(8,128)}, bf16[32,768]{1,0:T(8,128)(2,1)}, bf16[128,768]{1,0:T(8,128)(2,1)}) custom-call(bf16[512,128]{1,0:T(8,128)(2,1)} %get-tuple-element.29.refs_0_.refs_3_, bf16[48,256]{1,0:T(8,128)(2,1)} %copy-done.12, bf16[48,256]{1,0:T(8,128)(2,1)} %copy-done.13, s32[1,32]{1,0:T(1,128)} %bitcast.12, ...), custom_call_target="tpu_custom_call" | custom-call | flops 1000 | bytes 1024 | tf_op jit(solution)/shard_map/atom_mid/pallas_call | solution.py:124
  22.8 1.6 %collective-permute-start.2 = (bf16[32,768]{1,0:T(8,128)(2,1)}, bf16[32,768]{1,0:T(8,128)(2,1)S(1)}, u32[]{:S(2)}, u32[]{:S(2)}) collective-permute-start(bf16[32,768]{1,0:T(8,128)(2,1)} %get-tuple-element.34), channel_id=1, source_target_pairs={{0,0},{1,64},{2,128},{3,192},{4,4},{5,68},{6,132},{7,196},{8,8},{9... | collective-permute-start | bytes 147464 | tf_op jit(solution)/shard_map/ppermute | solution.py:478
  24.4 5.0 %pair.3 = (bf16[32,512,128]{2,1,0:T(8,128)(2,1)}, bf16[4,1,32,512]{3,2,1,0:T(8,128)(2,1)}) custom-call(bf16[32,512,128]{2,1,0:T(8,128)(2,1)} %refs_0_.6, bf16[128,512]{1,0:T(8,128)(2,1)} %refs_1_.9, bf16[256,128]{1,0:T(8,128)(2,1)} %refs_2_.9, bf16[16,128]{1,0:T(8,128)(2,1)} %bitcast.8), custom_call_target="tpu_custom_call" | custom-call | flops 1000 | bytes 1024 | tf_op jit(solution)/shard_map/pair/pallas_call | solution.py:124
  29.5 0.9 %broadcast_in_dim.2 = bf16[8,32,768]{2,1,0:T(8,128)(2,1)} broadcast(bf16[32,768]{1,0:T(8,128)(2,1)S(1)} %collective-permute-done.2), dimensions={1,2} | broadcast | bytes 442368 | tf_op jit(solution)/shard_map/broadcast_in_dim | solution.py:483
  30.4 9.0 %all-to-all-start = ((bf16[8,32,768]{2,1,0:T(8,128)(2,1)}), bf16[8,32,768]{2,1,0:T(8,128)(2,1)S(1)}, u32[]{:S(2)}, u32[]{:S(2)}) async-start(bf16[8,32,768]{2,1,0:T(8,128)(2,1)} %broadcast_in_dim.2), calls=%async_computation | async-start | bytes 786432 | tf_op jit(solution)/shard_map/all_to_all | solution.py:482
  39.4 4.9 %collective-permute-start.8 = (bf16[128,768]{1,0:T(8,128)(2,1)S(1)}, bf16[128,768]{1,0:T(8,128)(2,1)S(1)}, u32[]{:S(2)}, u32[]{:S(2)}) collective-permute-start(bf16[128,768]{1,0:T(8,128)(2,1)S(1)} %copy-done.5), channel_id=1, source_target_pairs={{0,3},{1,0},{2,1},{3,2},{4,7},{5,4},{6,5},{7,6},{8,11},{9,8},{10,9... | collective-permute-start | bytes 589832 | tf_op jit(solution)/shard_map/ppermute | solution.py:436
  44.3 1.4 %collective-permute-start.7 = (bf16[128,768]{1,0:T(8,128)(2,1)S(1)}, bf16[128,768]{1,0:T(8,128)(2,1)S(1)}, u32[]{:S(2)}, u32[]{:S(2)}) collective-permute-start(bf16[128,768]{1,0:T(8,128)(2,1)S(1)} %copy-done.5), channel_id=1, source_target_pairs={{0,2},{1,3},{2,0},{3,1},{4,6},{5,7},{6,4},{7,5},{8,10},{9,11},{10,... | collective-permute-start | bytes 589832 | tf_op jit(solution)/shard_map/ppermute | solution.py:436
  45.6 0.8 collective-permute-start.6
  46.4 7.9 %pair.4 = (bf16[32,512,128]{2,1,0:T(8,128)(2,1)}, bf16[4,2,32,512]{3,2,1,0:T(8,128)(2,1)}) custom-call(bf16[32,512,128]{2,1,0:T(8,128)(2,1)} %refs_0_.6, bf16[128,512]{1,0:T(8,128)(2,1)} %refs_1_.9, bf16[256,128]{1,0:T(8,128)(2,1)} %refs_2_.9, bf16[16,128]{1,0:T(8,128)(2,1)} %bitcast.9, ...), custom_call_target="tpu_custom_call", output_to_operand_aliasing={{0}: (4, {})} | custom-call | flops 1000 | bytes 1024 | tf_op jit(solution)/shard_map/pair/pallas_call | solution.py:124
  54.4 2.2 %collective-permute-done.6.refs_1_ = bf16[128,768]{1,0:T(8,128)(2,1)S(1)} collective-permute-done((bf16[128,768]{1,0:T(8,128)(2,1)S(1)}, bf16[128,768]{1,0:T(8,128)(2,1)S(1)}, u32[]{:S(2)}, u32[]{:S(2)}) %collective-permute-start.6) | collective-permute-done | bytes 196640 | tf_op jit(solution)/shard_map/ppermute | solution.py:436
  56.6 0.8 collective-permute-start.9
  57.4 5.0 %pair.5 = (bf16[32,512,128]{2,1,0:T(8,128)(2,1)}, bf16[4,1,32,512]{3,2,1,0:T(8,128)(2,1)}) custom-call(bf16[32,512,128]{2,1,0:T(8,128)(2,1)} %refs_0_.6, bf16[128,512]{1,0:T(8,128)(2,1)} %refs_1_.9, bf16[256,128]{1,0:T(8,128)(2,1)} %refs_2_.9, bf16[16,128]{1,0:T(8,128)(2,1)} %bitcast.10, ...), custom_call_target="tpu_custom_call", output_to_operand_aliasing={{0}: (4, {})} | custom-call | flops 1000 | bytes 1024 | tf_op jit(solution)/shard_map/pair/pallas_call | solution.py:124
  63.2 5.1 %attention.1 = (bf16[32,896]{1,0:T(8,128)(2,1)}, bf16[4,192,128]{2,1,0:T(8,128)(2,1)}) custom-call(bf16[128,768]{1,0:T(8,128)(2,1)} %get-tuple-element.33.refs_0_, bf16[128,768]{1,0:T(8,128)(2,1)} %copy-done.8, bf16[128,768]{1,0:T(8,128)(2,1)} %copy-done.7, bf16[128,768]{1,0:T(8,128)(2,1)} %copy-done.6, bf16[8,32,768]{2,1,0:T(8,128)(2,1)} %copy-done, ...), custom_call_target="tpu_custom_call" | custom-call | flops 1000 | bytes 1024 | tf_op jit(solution)/shard_map/attention/pallas_call | solution.py:124
  68.3 2.5 %collective-permute-start.12 = (bf16[32,896]{1,0:T(8,128)(2,1)}, bf16[32,896]{1,0:T(8,128)(2,1)S(1)}, u32[]{:S(2)}, u32[]{:S(2)}) collective-permute-start(bf16[32,896]{1,0:T(8,128)(2,1)} %get-tuple-element.51.refs_0_), channel_id=1, source_target_pairs={{0,3},{1,0},{2,1},{3,2},{4,7},{5,4},{6,5},{7,6},{8,11},{9,8},{10,9... | collective-permute-start | bytes 172040 | tf_op jit(solution)/shard_map/ppermute | solution.py:436
  70.8 1.4 %collective-permute-start.11 = (bf16[32,896]{1,0:T(8,128)(2,1)}, bf16[32,896]{1,0:T(8,128)(2,1)S(1)}, u32[]{:S(2)}, u32[]{:S(2)}) collective-permute-start(bf16[32,896]{1,0:T(8,128)(2,1)} %get-tuple-element.51.refs_0_), channel_id=1, source_target_pairs={{0,2},{1,3},{2,0},{3,1},{4,6},{5,7},{6,4},{7,5},{8,10},{9,11},{10,... | collective-permute-start | bytes 172040 | tf_op jit(solution)/shard_map/ppermute | solution.py:436
  73.0 2.6 %collective-permute-done.11.refs_2_ = bf16[32,896]{1,0:T(8,128)(2,1)S(1)} collective-permute-done((bf16[32,896]{1,0:T(8,128)(2,1)}, bf16[32,896]{1,0:T(8,128)(2,1)S(1)}, u32[]{:S(2)}, u32[]{:S(2)}) %collective-permute-start.11) | collective-permute-done | bytes 57376 | tf_op jit(solution)/shard_map/ppermute | solution.py:436
  75.6 2.1 %collective-permute-done.10.refs_1_ = bf16[32,896]{1,0:T(8,128)(2,1)S(1)} collective-permute-done((bf16[32,896]{1,0:T(8,128)(2,1)}, bf16[32,896]{1,0:T(8,128)(2,1)S(1)}, u32[]{:S(2)}, u32[]{:S(2)}) %collective-permute-start.10) | collective-permute-done | bytes 57376 | tf_op jit(solution)/shard_map/ppermute | solution.py:436
  78.3 2.7 %final.1 = bf16[512,128]{1,0:T(8,128)(2,1)} custom-call(bf16[32,896]{1,0:T(8,128)(2,1)} %get-tuple-element.51.refs_0_, bf16[32,896]{1,0:T(8,128)(2,1)} %copy-done.11, bf16[32,896]{1,0:T(8,128)(2,1)} %copy-done.10, bf16[32,896]{1,0:T(8,128)(2,1)} %copy-done.9, f32[32,768]{1,0:T(8,128)} %get-tuple-element.52.refs_4_, f32[512,128]{1,0:T(8,128)} %get-tuple-element.53.refs_5_, ...), custom_call_target="tpu_custom_call" | custom-call | flops 1000 | bytes 1024 | tf_op jit(solution)/shard_map/final/pallas_call | solution.py:124
  (41 shorter events, 3.9 us)
Async XLA Ops:
  5.7 23.8 %collective-permute-start.5 = (bf16[224,768]{1,0:T(8,128)(2,1)}, bf16[224,768]{1,0:T(8,128)(2,1)S(1)}, u32[]{:S(2)}, u32[]{:S(2)}) collective-permute-start(bf16[224,768]{1,0:T(8,128)(2,1)} %pack.1.refs_6_), channel_id=1, source_target_pairs={{0,3},{1,0},{2,1},{3,2},{4,7},{5,4},{6,5},{7,6},{8,11},{9,8},{10,9... | collective-permute-start | bytes 1032200 | tf_op jit(solution)/shard_map/ppermute | solution.py:436
  9.1 20.4 %collective-permute-start.4 = (bf16[224,768]{1,0:T(8,128)(2,1)}, bf16[224,768]{1,0:T(8,128)(2,1)S(1)}, u32[]{:S(2)}, u32[]{:S(2)}) collective-permute-start(bf16[224,768]{1,0:T(8,128)(2,1)} %pack.1.refs_6_), channel_id=1, source_target_pairs={{0,2},{1,3},{2,0},{3,1},{4,6},{5,7},{6,4},{7,5},{8,10},{9,11},{10,... | collective-permute-start | bytes 1032200 | tf_op jit(solution)/shard_map/ppermute | solution.py:436
  9.6 19.9 %collective-permute-start.3 = (bf16[224,768]{1,0:T(8,128)(2,1)}, bf16[224,768]{1,0:T(8,128)(2,1)S(1)}, u32[]{:S(2)}, u32[]{:S(2)}) collective-permute-start(bf16[224,768]{1,0:T(8,128)(2,1)} %pack.1.refs_6_), channel_id=1, source_target_pairs={{0,1},{1,2},{2,3},{3,0},{4,5},{5,6},{6,7},{7,4},{8,9},{9,10},{10,1... | collective-permute-start | bytes 1032200 | tf_op jit(solution)/shard_map/ppermute | solution.py:436
  10.2 5.0 %collective-permute-start = (bf16[48,256]{1,0:T(8,128)(2,1)}, bf16[48,256]{1,0:T(8,128)(2,1)S(1)}, u32[]{:S(2)}, u32[]{:S(2)}) collective-permute-start(bf16[48,256]{1,0:T(8,128)(2,1)} %get-tuple-element.30), channel_id=1, source_target_pairs={{0,4},{4,0},{8,12},{12,8},{16,20},{20,16},{24,28},{28,24},{32,36},... | collective-permute-start | bytes 73736 | tf_op jit(solution)/shard_map/ppermute | solution.py:452
  11.7 5.6 %collective-permute-start.1 = (bf16[48,256]{1,0:T(8,128)(2,1)}, bf16[48,256]{1,0:T(8,128)(2,1)S(1)}, u32[]{:S(2)}, u32[]{:S(2)}) collective-permute-start(bf16[48,256]{1,0:T(8,128)(2,1)} %get-tuple-element.31), channel_id=1, source_target_pairs={{4,8},{8,4},{12,16},{16,12},{20,24},{24,20},{28,32},{32,28},{36,40... | collective-permute-start | bytes 73736 | tf_op jit(solution)/shard_map/ppermute | solution.py:451
  15.2 2.2 %copy-start.12 = (bf16[48,256]{1,0:T(8,128)(2,1)}, bf16[48,256]{1,0:T(8,128)(2,1)S(1)}, u32[]{:S(2)}) copy-start(bf16[48,256]{1,0:T(8,128)(2,1)S(1)} %collective-permute-done.refs_1_) | copy-start | bytes 73732
  22.8 16.5 %copy-start.5 = (bf16[128,768]{1,0:T(8,128)(2,1)S(1)}, bf16[128,768]{1,0:T(8,128)(2,1)}, u32[]{:S(2)}) copy-start(bf16[128,768]{1,0:T(8,128)(2,1)} %get-tuple-element.33.refs_0_) | copy-start | bytes 589828
  22.8 6.6 %collective-permute-start.2 = (bf16[32,768]{1,0:T(8,128)(2,1)}, bf16[32,768]{1,0:T(8,128)(2,1)S(1)}, u32[]{:S(2)}, u32[]{:S(2)}) collective-permute-start(bf16[32,768]{1,0:T(8,128)(2,1)} %get-tuple-element.34), channel_id=1, source_target_pairs={{0,0},{1,64},{2,128},{3,192},{4,4},{5,68},{6,132},{7,196},{8,8},{9... | collective-permute-start | bytes 147464 | tf_op jit(solution)/shard_map/ppermute | solution.py:478
  29.5 24.8 %copy-start.2 = (bf16[224,768]{1,0:T(8,128)(2,1)}, bf16[224,768]{1,0:T(8,128)(2,1)S(1)}, u32[]{:S(2)}) copy-start(bf16[224,768]{1,0:T(8,128)(2,1)S(1)} %collective-permute-done.5.refs_9_) | copy-start | bytes 1032196
  29.5 24.8 %copy-start.3 = (bf16[224,768]{1,0:T(8,128)(2,1)}, bf16[224,768]{1,0:T(8,128)(2,1)S(1)}, u32[]{:S(2)}) copy-start(bf16[224,768]{1,0:T(8,128)(2,1)S(1)} %collective-permute-done.4.refs_8_) | copy-start | bytes 1032196
  29.5 24.8 %copy-start.4 = (bf16[224,768]{1,0:T(8,128)(2,1)}, bf16[224,768]{1,0:T(8,128)(2,1)S(1)}, u32[]{:S(2)}) copy-start(bf16[224,768]{1,0:T(8,128)(2,1)S(1)} %collective-permute-done.3.refs_7_) | copy-start | bytes 1032196
  30.4 26.2 %all-to-all-start = ((bf16[8,32,768]{2,1,0:T(8,128)(2,1)}), bf16[8,32,768]{2,1,0:T(8,128)(2,1)S(1)}, u32[]{:S(2)}, u32[]{:S(2)}) async-start(bf16[8,32,768]{2,1,0:T(8,128)(2,1)} %broadcast_in_dim.2), calls=%async_computation | async-start | bytes 786432 | tf_op jit(solution)/shard_map/all_to_all | solution.py:482
  39.4 15.0 %collective-permute-start.8 = (bf16[128,768]{1,0:T(8,128)(2,1)S(1)}, bf16[128,768]{1,0:T(8,128)(2,1)S(1)}, u32[]{:S(2)}, u32[]{:S(2)}) collective-permute-start(bf16[128,768]{1,0:T(8,128)(2,1)S(1)} %copy-done.5), channel_id=1, source_target_pairs={{0,3},{1,0},{2,1},{3,2},{4,7},{5,4},{6,5},{7,6},{8,11},{9,8},{10,9... | collective-permute-start | bytes 589832 | tf_op jit(solution)/shard_map/ppermute | solution.py:436
  44.3 10.1 %collective-permute-start.7 = (bf16[128,768]{1,0:T(8,128)(2,1)S(1)}, bf16[128,768]{1,0:T(8,128)(2,1)S(1)}, u32[]{:S(2)}, u32[]{:S(2)}) collective-permute-start(bf16[128,768]{1,0:T(8,128)(2,1)S(1)} %copy-done.5), channel_id=1, source_target_pairs={{0,2},{1,3},{2,0},{3,1},{4,6},{5,7},{6,4},{7,5},{8,10},{9,11},{10,... | collective-permute-start | bytes 589832 | tf_op jit(solution)/shard_map/ppermute | solution.py:436
  45.6 11.0 %collective-permute-start.6 = (bf16[128,768]{1,0:T(8,128)(2,1)S(1)}, bf16[128,768]{1,0:T(8,128)(2,1)S(1)}, u32[]{:S(2)}, u32[]{:S(2)}) collective-permute-start(bf16[128,768]{1,0:T(8,128)(2,1)S(1)} %copy-done.5), channel_id=1, source_target_pairs={{0,1},{1,2},{2,3},{3,0},{4,5},{5,6},{6,7},{7,4},{8,9},{9,10},{10,1... | collective-permute-start | bytes 589832 | tf_op jit(solution)/shard_map/ppermute | solution.py:436
  54.4 8.1 %copy-start.6 = (bf16[128,768]{1,0:T(8,128)(2,1)}, bf16[128,768]{1,0:T(8,128)(2,1)S(1)}, u32[]{:S(2)}) copy-start(bf16[128,768]{1,0:T(8,128)(2,1)S(1)} %collective-permute-done.8.refs_3_) | copy-start | bytes 589828
  54.4 8.0 %copy-start.7 = (bf16[128,768]{1,0:T(8,128)(2,1)}, bf16[128,768]{1,0:T(8,128)(2,1)S(1)}, u32[]{:S(2)}) copy-start(bf16[128,768]{1,0:T(8,128)(2,1)S(1)} %collective-permute-done.7.refs_2_) | copy-start | bytes 589828
  56.6 5.8 %copy-start.8 = (bf16[128,768]{1,0:T(8,128)(2,1)}, bf16[128,768]{1,0:T(8,128)(2,1)S(1)}, u32[]{:S(2)}) copy-start(bf16[128,768]{1,0:T(8,128)(2,1)S(1)} %collective-permute-done.6.refs_1_) | copy-start | bytes 589828
  56.6 5.8 %copy-start = (bf16[8,32,768]{2,1,0:T(8,128)(2,1)}, bf16[8,32,768]{2,1,0:T(8,128)(2,1)S(1)}, u32[]{:S(2)}) copy-start(bf16[8,32,768]{2,1,0:T(8,128)(2,1)S(1)} %all-to-all-done.refs_4_) | copy-start | bytes 1179652
  56.6 5.8 %collective-permute-start.9 = (bf16[8,32,768]{2,1,0:T(8,128)(2,1)S(1)}, bf16[8,32,768]{2,1,0:T(8,128)(2,1)S(1)}, u32[]{:S(2)}, u32[]{:S(2)}) collective-permute-start(bf16[8,32,768]{2,1,0:T(8,128)(2,1)S(1)} %all-to-all-done.refs_4_), channel_id=1, source_target_pairs={{0,4},{4,0},{8,12},{12,8},{16,20},{20,16},{24,28},{28,24},{32,36},... | collective-permute-start | bytes 1179656 | tf_op jit(solution)/shard_map/ppermute | solution.py:487
  68.3 4.6 %collective-permute-start.12 = (bf16[32,896]{1,0:T(8,128)(2,1)}, bf16[32,896]{1,0:T(8,128)(2,1)S(1)}, u32[]{:S(2)}, u32[]{:S(2)}) collective-permute-start(bf16[32,896]{1,0:T(8,128)(2,1)} %get-tuple-element.51.refs_0_), channel_id=1, source_target_pairs={{0,3},{1,0},{2,1},{3,2},{4,7},{5,4},{6,5},{7,6},{8,11},{9,8},{10,9... | collective-permute-start | bytes 172040 | tf_op jit(solution)/shard_map/ppermute | solution.py:436
  70.8 4.7 %collective-permute-start.11 = (bf16[32,896]{1,0:T(8,128)(2,1)}, bf16[32,896]{1,0:T(8,128)(2,1)S(1)}, u32[]{:S(2)}, u32[]{:S(2)}) collective-permute-start(bf16[32,896]{1,0:T(8,128)(2,1)} %get-tuple-element.51.refs_0_), channel_id=1, source_target_pairs={{0,2},{1,3},{2,0},{3,1},{4,6},{5,7},{6,4},{7,5},{8,10},{9,11},{10,... | collective-permute-start | bytes 172040 | tf_op jit(solution)/shard_map/ppermute | solution.py:436
  72.2 5.5 %collective-permute-start.10 = (bf16[32,896]{1,0:T(8,128)(2,1)}, bf16[32,896]{1,0:T(8,128)(2,1)S(1)}, u32[]{:S(2)}, u32[]{:S(2)}) collective-permute-start(bf16[32,896]{1,0:T(8,128)(2,1)} %get-tuple-element.51.refs_0_), channel_id=1, source_target_pairs={{0,1},{1,2},{2,3},{3,0},{4,5},{5,6},{6,7},{7,4},{8,9},{9,10},{10,1... | collective-permute-start | bytes 172040 | tf_op jit(solution)/shard_map/ppermute | solution.py:436
  73.0 4.8 %copy-start.9 = (bf16[32,896]{1,0:T(8,128)(2,1)}, bf16[32,896]{1,0:T(8,128)(2,1)S(1)}, u32[]{:S(2)}) copy-start(bf16[32,896]{1,0:T(8,128)(2,1)S(1)} %collective-permute-done.12.refs_3_) | copy-start | bytes 172036
  (4 other events, 4.1 us)

commit v3 on v2

--- a/solution.py
+++ b/solution.py
@@ -35,7 +35,7 @@
 FOLD = GW * C_A // C_S
 ROWS = 8
 COLS = 512
-CHUNKS = ((0, 1), (1, 2), (3, 1))
+CHUNKS = ((0, 1), (1, 3))
 
 F32 = jnp.float32
 BF = jnp.bfloat16
@@ -168,15 +168,6 @@
     normed_ref[...] = normed
     normed_ref.send()
     initial_ref[...] = initial
-    initial_ref.send()
-
-
-def pack_kernel(twv_ref, two_ref, back_ref, _, packed_ref):
-    folded = dot(two_ref[...], back_ref[...]).astype(BF)
-    packed_ref[GW:, :] = jnp.concatenate(
-        [folded[i * FOLD : (i + 1) * FOLD] for i in range(GW // FOLD)], axis=1
-    )
-    packed_ref[:GW, :] = twv_ref[...]
 
 
 def spans(counts_ref):
@@ -191,7 +182,7 @@
 
 def atom_mid_kernel(
     normed_ref, inner_ref, outer_ref, counts_ref, wq_ref, wk_ref, wv_ref, initial_ref, wo_ref, pool_ref,
-    single_ref, twq_ref, twk_ref, state_ref, token_in_ref, token_normed_ref, t_ref,
+    single_ref, twq_ref, twk_ref, twv_ref, two_ref, back_ref, state_ref, token_in_ref, token_normed_ref, t_ref,
 ):
     lower = lax.axis_index("atom") % NK == 0
     inner, outer = inner_ref[...].astype(F32), outer_ref[...].astype(F32)
@@ -254,7 +245,12 @@
         for h in range(GROUP)
     ]
     spread = jnp.concatenate(pieces, axis=0).astype(BF)
-    t_ref[...] = (dot(spread, twk_ref[...]) * (1.0 / math.sqrt(HEAD))).astype(BF)
+    t_ref[: GROUP * TOKS, :] = (dot(spread, twk_ref[...]) * (1.0 / math.sqrt(HEAD))).astype(BF)
+    t_ref[GROUP * TOKS : GROUP * TOKS + GW, :] = twv_ref[...]
+    folded = dot(two_ref[...], back_ref[...]).astype(BF)
+    t_ref[GROUP * TOKS + GW :, :] = jnp.concatenate(
+        [folded[i * FOLD : (i + 1) * FOLD] for i in range(GW // FOLD)], axis=1
+    )
 
 
 def pair_kernel(x_ref, w1_ref, w2_ref, wb_ref, *refs, start, count):
@@ -340,21 +336,21 @@
             pltpu.VMEM((128, 512), BF), pltpu.VMEM((256, 256), BF),
             *(pltpu.SemaphoreType.DMA((i * count,)) for i in (1, 2, 1)),
         ],
-        flops=1000,
+        flops=count * 3 * 10**9,
     )
 
 
 def attention_kernel(
-    t0, t1, t2, t3, own_ref, other_ref, w0, w1, w2, w3, *refs
+    t0, t1, t2, t3, own_ref, other_ref, *refs
 ):
     *biases, msg_ref, back_ref, xk_s, o_s = refs
     col, core = lax.axis_index("col"), lax.axis_index("atom") % NK
-    wide = GROUP * TOKS
-    packed = (w0, w1, w2, w3)
-    t = jnp.concatenate([t0[...], t1[...], t2[...], t3[...]], axis=0)
     xk_s[:, pl.ds(core, 1)] = own_ref[...].reshape(NZ, 1, TOKS, C_S)
     xk_s[:, pl.ds(1 - core, 1)] = other_ref[...].reshape(NZ, 1, TOKS, C_S)
     xk = xk_s[...].reshape(COLS, C_S)
+    wide = GROUP * TOKS
+    packed = (t0, t1, t2, t3)
+    t = jnp.concatenate([p[:wide, :] for p in packed], axis=0)
     scores = dot_nt(t, xk)
     groups = [(col + NC - s) % NC for s in range(NC)]
     scores = jnp.concatenate(
@@ -380,10 +376,10 @@
     totals = jnp.zeros((TOKS, 128), F32)
     for s, w in enumerate(packed):
         lo = s * wide
-        o = dot_nt(mixed[lo : lo + wide], w[:GW, :]).reshape(blocks, GROUP, ROWS, GW)
+        o = dot_nt(mixed[lo : lo + wide], w[wide : wide + GW, :]).reshape(blocks, GROUP, ROWS, GW)
         o = jnp.sum(jnp.where(lane_head == row_head, o, 0.0), axis=1).reshape(TOKS, GW)
         o_s[pl.ds(groups[s], 1)] = o.reshape(1, TOKS, GW)
-        folded = jnp.concatenate([w[GW:, i * C_A : (i + 1) * C_A] for i in range(GW // FOLD)], axis=0)
+        folded = jnp.concatenate([w[wide + GW :, i * C_A : (i + 1) * C_A] for i in range(GW // FOLD)], axis=0)
         back_ref.buffer[pl.ds(groups[s], 1)] = folded.reshape(1, GW, C_A)
         here = lane16 == row16 + groups[s] * GROUP
         for value, which in ((top, 0), (total, 1)):
@@ -444,16 +440,12 @@
     counts = token_counts.reshape(1, TOKS)
     initial, normed, inner, outer = call(
         atom_in_kernel,
-        [((ATOMS, C_A), F32), ((ATOMS, C_A), BF)] + [((MARGIN, 2 * C_A), BF)] * 2,
+        [((ATOMS, C_A), F32), ((ATOMS, C_A), BF), ((MARGIN, 2 * C_A), BF), ((MARGIN, 2 * C_A), BF)],
         (noise_index, positions, w_pos, atom_single, counts),
-        name="atom_in", smem=(0,), flops=1000,
+        name="atom_in", smem=(0,), flops=10**8,
     )
     outer = lax.ppermute(outer, "atom", [(i, i + (1 if i % 2 else -1)) for i in range(1, atoms - 1)])
     inner = lax.ppermute(inner, "atom", [(i, i ^ 1) for i in range(atoms)])
-    (packed,) = call(
-        pack_kernel, [((GW + FOLD, C_S), BF)], (token_wv.T, token_wo, w_back, normed), name="pack", far=(3,), flops=1000
-    )
-    weights = [packed] + around(packed, "col", NC)
     pair_out, biases = None, []
 
     def pair(i, after=None):
@@ -464,12 +456,12 @@
     pair(0)
     state, token_in, token_normed, t_own = call(
         atom_mid_kernel,
-        [((ATOMS, C_A), F32), ((TOKS, C_S), F32), ((TOKS, C_S), BF), ((GROUP * TOKS, C_S), BF)],
+        [((ATOMS, C_A), F32), ((TOKS, C_S), F32), ((TOKS, C_S), BF), ((GROUP * TOKS + GW + FOLD, C_S), BF)],
         (
             normed, inner, outer, counts, atom_wq, atom_wk, atom_wv, initial, atom_wo, w_pool, token_single,
-            token_wq.T, token_wk.T,
+            token_wq.T, token_wk.T, token_wv.T, token_wo, w_back,
         ),
-        name="atom_mid", flops=1000,
+        name="atom_mid", flops=10**9,
     )
     flip = [
         ((y * NZ * NK + i) * NC + x, (x * NZ * NK + i) * NC + y)
@@ -477,13 +469,16 @@
     ]
     turned = lax.ppermute(token_normed, ("atom", "col"), flip)
     lines = [[(y * NZ + z) * NK + k for z in range(NZ)] for y in range(NY) for k in range(NK)]
-    turned, biases[0], weights = lax.optimization_barrier((turned, biases[0], weights))
-    queries = around(t_own, "col", NC)
+    turned, biases[0], t_own = lax.optimization_barrier((turned, biases[0], t_own))
     own = lax.all_to_all(
         jnp.broadcast_to(turned[None], (NZ, TOKS, C_S)), "atom", 0, 0, axis_index_groups=lines, tiled=True
     )
+    one = lax.ppermute(t_own, "col", [(i, (i + 1) % NC) for i in range(NC)])
+    three_on = lax.ppermute(t_own, "col", [(i, (i - 1) % NC) for i in range(NC)])
+    two = lax.ppermute(one, "col", [(i, (i + 1) % NC) for i in range(NC)])
     pair(1)
-    own, biases[1], queries = lax.optimization_barrier((own, biases[1], queries))
+    packed = [t_own, one, two, three_on]
+    own, biases[1], packed = lax.optimization_barrier((own, biases[1], packed))
     other = lax.ppermute(own, "atom", [(i, i ^ 1) for i in range(atoms)])
     for i in range(2, len(CHUNKS)):
         pair(i)
@@ -491,14 +486,14 @@
     msg, back = call(
         attention_kernel,
         [((TOKS, C_S + 128), BF), ((NC, GW, C_A), BF)],
-        (t_own, *queries, own, other, *weights, *biases),
-        name="attention", flops=1000,
+        (*packed, own, other, *biases),
+        name="attention", flops=3 * 10**9,
         scratch=[pltpu.VMEM((NZ, NK, TOKS, C_S), BF), pltpu.VMEM((NC, TOKS, GW), F32)],
     )
     msgs = [msg] + around(msg, "col", NC)
     (atom_out,) = call(
         final_kernel, [((ATOMS, C_A), BF)], (*msgs, token_in, state, counts, w_back, back),
-        name="final", flops=1000,
+        name="final", flops=10**8,
     )
     return (atom_out, pair_out)
 

time: 81.6 us -> 75.1 us (0.920)
  the two profiles are of different devices: /device:TPU:1 before, /device:TPU:112 now
where the time goes in v3:
time: 75.1 us; the launch traced here: 74.8 us
  Pallas kernels  31.2 us (42%)
  starting transfers between devices  22.2 us (30%)
  waiting for transfers between devices  16.9 us (23%)
  local copies, waits for them, and re-layouts  2.79 us (4%)
  between operations  1.6 us (2%)
    pallas_call x6, Pallas kernels, call(): pl.pallas_call(body, in_specs=[pl.BlockSpec(memory_space=pltpu.SMEM if i...  31.2 us
    all_to_all x1, starting transfers between devices, local(): lax.all_to_all(jnp.broadcast_to(turned[None], (NZ, TOKS, C_S)), 'atom', 0...  8.79 us
    ppermute x1, starting transfers between devices, local(): turned = lax.ppermute(token_normed, ('atom', 'col'), flip)  4.7 us
    ppermute x1, waiting for transfers between devices, local(): two = lax.ppermute(one, 'col', [(i, (i + 1) % NC) for i in range(NC)])  4.32 us
    ppermute x3, waiting for transfers between devices, around(): lax.ppermute(array, axis, [(i, (i + s) % size) for i in range(size)])  3.93 us
    ppermute x1, waiting for transfers between devices, local(): one = lax.ppermute(t_own, 'col', [(i, (i + 1) % NC) for i in range(NC)])  3.36 us
    ppermute x3, starting transfers between devices, around(): lax.ppermute(array, axis, [(i, (i + s) % size) for i in range(size)])  3.31 us
    ppermute x1, starting transfers between devices, local(): lax.ppermute(t_own, 'col', [(i, (i - 1) % NC) for i in range(NC)])  3.23 us
  transfers between devices with their start and end apart: 11, of which 7 were waited for; matrix products, arithmetic and copies ran while one was open for 1% of the time, Pallas kernels for 22%

profile of v3, /device:TPU:112, one launch (start us, length us, event | category | flops | bytes accessed | tf_op | source)
XLA Modules:
  0.0 74.8 jit_solution(3739805148124791497)
XLA Ops:
  1.3 2.3 %atom_in.1 = (f32[512,128]{1,0:T(8,128)}, bf16[512,128]{1,0:T(8,128)(2,1)}, bf16[48,256]{1,0:T(8,128)(2,1)}, bf16[48,256]{1,0:T(8,128)(2,1)}) custom-call(s32[1]{0:T(128)S(6)} %copy.24.refs_0_, f32[3,512]{1,0:T(4,128)} %refs_1_.3, f32[3,128]{1,0:T(4,128)} %refs_2_.3, bf16[512,128]{1,0:T(8,128)(2,1)} %refs_3_.1, s32[1,32]{1,0:T(1,128)} %bitcast.5), custom_call_target="tpu_custom_call" | custom-call | flops 100000000 | bytes 1024 | tf_op jit(solution)/shard_map/atom_in/pallas_call | solution.py:124
  3.6 0.1 collective-permute-start
  3.7 2.1 %collective-permute-start.1 = (bf16[48,256]{1,0:T(8,128)(2,1)}, bf16[48,256]{1,0:T(8,128)(2,1)S(1)}, u32[]{:S(2)}, u32[]{:S(2)}) collective-permute-start(bf16[48,256]{1,0:T(8,128)(2,1)} %get-tuple-element.27), channel_id=1, source_target_pairs={{4,8},{8,4},{12,16},{16,12},{20,24},{24,20},{28,32},{32,28},{36,40... | collective-permute-start | bytes 73736 | tf_op jit(solution)/shard_map/ppermute | solution.py:447
  5.8 3.2 %collective-permute-done.1.refs_2_ = bf16[48,256]{1,0:T(8,128)(2,1)S(1)} collective-permute-done((bf16[48,256]{1,0:T(8,128)(2,1)}, bf16[48,256]{1,0:T(8,128)(2,1)S(1)}, u32[]{:S(2)}, u32[]{:S(2)}) %collective-permute-start.1) | collective-permute-done | bytes 24608 | tf_op jit(solution)/shard_map/ppermute | solution.py:447
  9.0 0.6 copy-done.10
  9.6 5.3 %atom_mid.1 = (f32[512,128]{1,0:T(8,128)}, f32[32,768]{1,0:T(8,128)}, bf16[32,768]{1,0:T(8,128)(2,1)}, bf16[352,768]{1,0:T(8,128)(2,1)}) custom-call(bf16[512,128]{1,0:T(8,128)(2,1)} %get-tuple-element.25.refs_0_, bf16[48,256]{1,0:T(8,128)(2,1)} %copy-done.9, bf16[48,256]{1,0:T(8,128)(2,1)} %copy-done.10, s32[1,32]{1,0:T(1,128)} %bitcast.6, ...), custom_call_target="tpu_custom_call" | custom-call | flops 1000000000 | bytes 1024 | tf_op jit(solution)/shard_map/atom_mid/pallas_call | solution.py:124
  14.9 4.7 %collective-permute-start.2 = (bf16[32,768]{1,0:T(8,128)(2,1)}, bf16[32,768]{1,0:T(8,128)(2,1)S(1)}, u32[]{:S(2)}, u32[]{:S(2)}) collective-permute-start(bf16[32,768]{1,0:T(8,128)(2,1)} %get-tuple-element.29), channel_id=1, source_target_pairs={{0,0},{1,64},{2,128},{3,192},{4,4},{5,68},{6,132},{7,196},{8,8},{9... | collective-permute-start | bytes 147464 | tf_op jit(solution)/shard_map/ppermute | solution.py:470
  19.7 5.1 %pair.2 = (bf16[32,512,128]{2,1,0:T(8,128)(2,1)}, bf16[4,1,32,512]{3,2,1,0:T(8,128)(2,1)}) custom-call(bf16[32,512,128]{2,1,0:T(8,128)(2,1)} %refs_0_.4, bf16[128,512]{1,0:T(8,128)(2,1)} %refs_1_.5, bf16[256,128]{1,0:T(8,128)(2,1)} %refs_2_.5, bf16[16,128]{1,0:T(8,128)(2,1)} %bitcast.11), custom_call_target="tpu_custom_call" | custom-call | flops 3000000000 | bytes 1024 | tf_op jit(solution)/shard_map/pair/pallas_call | solution.py:124
  24.8 0.4 collective-permute-done.2
  25.1 3.2 %collective-permute-start.5 = (bf16[352,768]{1,0:T(8,128)(2,1)S(1)}, bf16[352,768]{1,0:T(8,128)(2,1)S(1)}, u32[]{:S(2)}, u32[]{:S(2)}) collective-permute-start(bf16[352,768]{1,0:T(8,128)(2,1)S(1)} %copy-done.4), channel_id=1, source_target_pairs={{0,3},{1,0},{2,1},{3,2},{4,7},{5,4},{6,5},{7,6},{8,11},{9,8},{10,9... | collective-permute-start | bytes 1622024 | tf_op jit(solution)/shard_map/ppermute | solution.py:477
  28.4 0.8 %broadcast_in_dim.2 = bf16[8,32,768]{2,1,0:T(8,128)(2,1)} broadcast(bf16[32,768]{1,0:T(8,128)(2,1)S(1)} %collective-permute-done.2), dimensions={1,2} | broadcast | bytes 442368 | tf_op jit(solution)/shard_map/broadcast_in_dim | solution.py:474
  29.2 8.8 %all-to-all-start = ((bf16[8,32,768]{2,1,0:T(8,128)(2,1)}), bf16[8,32,768]{2,1,0:T(8,128)(2,1)S(1)}, u32[]{:S(2)}, u32[]{:S(2)}) async-start(bf16[8,32,768]{2,1,0:T(8,128)(2,1)} %broadcast_in_dim.2), calls=%async_computation | async-start | bytes 786432 | tf_op jit(solution)/shard_map/all_to_all | solution.py:473
  38.0 3.4 %collective-permute-done.3.refs_1_ = bf16[352,768]{1,0:T(8,128)(2,1)S(1)} collective-permute-done((bf16[352,768]{1,0:T(8,128)(2,1)S(1)}, bf16[352,768]{1,0:T(8,128)(2,1)S(1)}, u32[]{:S(2)}, u32[]{:S(2)}) %collective-permute-start.3) | collective-permute-done | bytes 540704 | tf_op jit(solution)/shard_map/ppermute | solution.py:476
  41.3 11.3 %pair.3 = (bf16[32,512,128]{2,1,0:T(8,128)(2,1)}, bf16[4,3,32,512]{3,2,1,0:T(8,128)(2,1)}) custom-call(bf16[32,512,128]{2,1,0:T(8,128)(2,1)} %refs_0_.4, bf16[128,512]{1,0:T(8,128)(2,1)} %refs_1_.5, bf16[256,128]{1,0:T(8,128)(2,1)} %refs_2_.5, bf16[16,128]{1,0:T(8,128)(2,1)} %bitcast.12, ...), custom_call_target="tpu_custom_call", output_to_operand_aliasing={{0}: (4, {})} | custom-call | flops 8999999488 | bytes 1024 | tf_op jit(solution)/shard_map/pair/pallas_call | solution.py:124
  52.7 4.3 %collective-permute-done.4.refs_2_ = bf16[352,768]{1,0:T(8,128)(2,1)S(1)} collective-permute-done((bf16[352,768]{1,0:T(8,128)(2,1)S(1)}, bf16[352,768]{1,0:T(8,128)(2,1)S(1)}, u32[]{:S(2)}, u32[]{:S(2)}) %collective-permute-start.4) | collective-permute-done | bytes 540704 | tf_op jit(solution)/shard_map/ppermute | solution.py:478
  57.0 1.7 %collective-permute-done.6.refs_5_ = bf16[8,32,768]{2,1,0:T(8,128)(2,1)S(1)} collective-permute-done((bf16[8,32,768]{2,1,0:T(8,128)(2,1)S(1)}, bf16[8,32,768]{2,1,0:T(8,128)(2,1)S(1)}, u32[]{:S(2)}, u32[]{:S(2)}) %collective-permute-start.6) | collective-permute-done | bytes 393248 | tf_op jit(solution)/shard_map/ppermute | solution.py:482
  58.8 0.7 copy-done.8
  59.5 4.5 %attention.1 = (bf16[32,896]{1,0:T(8,128)(2,1)}, bf16[4,192,128]{2,1,0:T(8,128)(2,1)}) custom-call(bf16[352,768]{1,0:T(8,128)(2,1)} %get-tuple-element.36.refs_0_, bf16[352,768]{1,0:T(8,128)(2,1)} %copy-done.5, bf16[352,768]{1,0:T(8,128)(2,1)} %copy-done.7, bf16[352,768]{1,0:T(8,128)(2,1)} %copy-done.6, bf16[8,32,768]{2,1,0:T(8,128)(2,1)} %copy-done, ...), custom_call_target="tpu_custom_call" | custom-call | flops 3000000000 | bytes 1024 | tf_op jit(solution)/shard_map/attention/pallas_call | solution.py:124
  64.1 1.0 %collective-permute-start.8 = (bf16[32,896]{1,0:T(8,128)(2,1)}, bf16[32,896]{1,0:T(8,128)(2,1)S(1)}, u32[]{:S(2)}, u32[]{:S(2)}) collective-permute-start(bf16[32,896]{1,0:T(8,128)(2,1)} %get-tuple-element.43.refs_0_), channel_id=1, source_target_pairs={{0,2},{1,3},{2,0},{3,1},{4,6},{5,7},{6,4},{7,5},{8,10},{9,11},{10,... | collective-permute-start | bytes 172040 | tf_op jit(solution)/shard_map/ppermute | solution.py:432
  65.1 2.2 %collective-permute-start.9 = (bf16[32,896]{1,0:T(8,128)(2,1)}, bf16[32,896]{1,0:T(8,128)(2,1)S(1)}, u32[]{:S(2)}, u32[]{:S(2)}) collective-permute-start(bf16[32,896]{1,0:T(8,128)(2,1)} %get-tuple-element.43.refs_0_), channel_id=1, source_target_pairs={{0,3},{1,0},{2,1},{3,2},{4,7},{5,4},{6,5},{7,6},{8,11},{9,8},{10,9... | collective-permute-start | bytes 172040 | tf_op jit(solution)/shard_map/ppermute | solution.py:432
  67.4 3.4 %collective-permute-done.7.refs_1_ = bf16[32,896]{1,0:T(8,128)(2,1)S(1)} collective-permute-done((bf16[32,896]{1,0:T(8,128)(2,1)}, bf16[32,896]{1,0:T(8,128)(2,1)S(1)}, u32[]{:S(2)}, u32[]{:S(2)}) %collective-permute-start.7) | collective-permute-done | bytes 57376 | tf_op jit(solution)/shard_map/ppermute | solution.py:432
  70.7 0.6 collective-permute-done.9.refs_3_
  71.4 0.5 copy-done.3
  71.9 2.7 %final.1 = bf16[512,128]{1,0:T(8,128)(2,1)} custom-call(bf16[32,896]{1,0:T(8,128)(2,1)} %get-tuple-element.43.refs_0_, bf16[32,896]{1,0:T(8,128)(2,1)} %copy-done.1, bf16[32,896]{1,0:T(8,128)(2,1)} %copy-done.2, bf16[32,896]{1,0:T(8,128)(2,1)} %copy-done.3, f32[32,768]{1,0:T(8,128)} %get-tuple-element.44.refs_4_, f32[512,128]{1,0:T(8,128)} %get-tuple-element.45.refs_5_, ...), custom_call_target="tpu_custom_call" | custom-call | flops 100000000 | bytes 1024 | tf_op jit(solution)/shard_map/final/pallas_call | solution.py:124
  (27 shorter events, 0.2 us)
Async XLA Ops:
  3.6 2.2 %collective-permute-start = (bf16[48,256]{1,0:T(8,128)(2,1)}, bf16[48,256]{1,0:T(8,128)(2,1)S(1)}, u32[]{:S(2)}, u32[]{:S(2)}) collective-permute-start(bf16[48,256]{1,0:T(8,128)(2,1)} %get-tuple-element.26), channel_id=1, source_target_pairs={{0,4},{4,0},{8,12},{12,8},{16,20},{20,16},{24,28},{28,24},{32,36},... | collective-permute-start | bytes 73736 | tf_op jit(solution)/shard_map/ppermute | solution.py:448
  3.7 5.4 %collective-permute-start.1 = (bf16[48,256]{1,0:T(8,128)(2,1)}, bf16[48,256]{1,0:T(8,128)(2,1)S(1)}, u32[]{:S(2)}, u32[]{:S(2)}) collective-permute-start(bf16[48,256]{1,0:T(8,128)(2,1)} %get-tuple-element.27), channel_id=1, source_target_pairs={{4,8},{8,4},{12,16},{16,12},{20,24},{24,20},{28,32},{32,28},{36,40... | collective-permute-start | bytes 73736 | tf_op jit(solution)/shard_map/ppermute | solution.py:447
  5.8 3.2 %copy-start.9 = (bf16[48,256]{1,0:T(8,128)(2,1)}, bf16[48,256]{1,0:T(8,128)(2,1)S(1)}, u32[]{:S(2)}) copy-start(bf16[48,256]{1,0:T(8,128)(2,1)S(1)} %collective-permute-done.refs_1_) | copy-start | bytes 73732
  9.0 0.6 copy-start.10
  14.9 10.2 %collective-permute-start.2 = (bf16[32,768]{1,0:T(8,128)(2,1)}, bf16[32,768]{1,0:T(8,128)(2,1)S(1)}, u32[]{:S(2)}, u32[]{:S(2)}) collective-permute-start(bf16[32,768]{1,0:T(8,128)(2,1)} %get-tuple-element.29), channel_id=1, source_target_pairs={{0,0},{1,64},{2,128},{3,192},{4,4},{5,68},{6,132},{7,196},{8,8},{9... | collective-permute-start | bytes 147464 | tf_op jit(solution)/shard_map/ppermute | solution.py:470
  19.7 5.5 %copy-start.4 = (bf16[352,768]{1,0:T(8,128)(2,1)S(1)}, bf16[352,768]{1,0:T(8,128)(2,1)}, u32[]{:S(2)}) copy-start(bf16[352,768]{1,0:T(8,128)(2,1)} %get-tuple-element.36.refs_0_) | copy-start | bytes 1622020
  25.1 16.2 %collective-permute-start.3 = (bf16[352,768]{1,0:T(8,128)(2,1)S(1)}, bf16[352,768]{1,0:T(8,128)(2,1)S(1)}, u32[]{:S(2)}, u32[]{:S(2)}) collective-permute-start(bf16[352,768]{1,0:T(8,128)(2,1)S(1)} %copy-done.4), channel_id=1, source_target_pairs={{0,1},{1,2},{2,3},{3,0},{4,5},{5,6},{6,7},{7,4},{8,9},{9,10},{10,1... | collective-permute-start | bytes 1622024 | tf_op jit(solution)/shard_map/ppermute | solution.py:476
  25.1 27.5 %collective-permute-start.5 = (bf16[352,768]{1,0:T(8,128)(2,1)S(1)}, bf16[352,768]{1,0:T(8,128)(2,1)S(1)}, u32[]{:S(2)}, u32[]{:S(2)}) collective-permute-start(bf16[352,768]{1,0:T(8,128)(2,1)S(1)} %copy-done.4), channel_id=1, source_target_pairs={{0,3},{1,0},{2,1},{3,2},{4,7},{5,4},{6,5},{7,6},{8,11},{9,8},{10,9... | collective-permute-start | bytes 1622024 | tf_op jit(solution)/shard_map/ppermute | solution.py:477
  29.2 23.5 %all-to-all-start = ((bf16[8,32,768]{2,1,0:T(8,128)(2,1)}), bf16[8,32,768]{2,1,0:T(8,128)(2,1)S(1)}, u32[]{:S(2)}, u32[]{:S(2)}) async-start(bf16[8,32,768]{2,1,0:T(8,128)(2,1)} %broadcast_in_dim.2), calls=%async_computation | async-start | bytes 786432 | tf_op jit(solution)/shard_map/all_to_all | solution.py:473
  41.3 11.3 %copy-start.5 = (bf16[352,768]{1,0:T(8,128)(2,1)}, bf16[352,768]{1,0:T(8,128)(2,1)S(1)}, u32[]{:S(2)}) copy-start(bf16[352,768]{1,0:T(8,128)(2,1)S(1)} %collective-permute-done.3.refs_1_) | copy-start | bytes 1622020
  41.3 15.7 %collective-permute-start.4 = (bf16[352,768]{1,0:T(8,128)(2,1)S(1)}, bf16[352,768]{1,0:T(8,128)(2,1)S(1)}, u32[]{:S(2)}, u32[]{:S(2)}) collective-permute-start(bf16[352,768]{1,0:T(8,128)(2,1)S(1)} %collective-permute-done.3.refs_1_), channel_id=1, source_target_pairs={{0,1},{1,2},{2,3},{3,0},{4,5},{5,6},{6,7},{7,4},{8,9},{9,10},{10,1... | collective-permute-start | bytes 1622024 | tf_op jit(solution)/shard_map/ppermute | solution.py:478
  52.7 6.1 %copy-start.6 = (bf16[352,768]{1,0:T(8,128)(2,1)}, bf16[352,768]{1,0:T(8,128)(2,1)S(1)}, u32[]{:S(2)}) copy-start(bf16[352,768]{1,0:T(8,128)(2,1)S(1)} %collective-permute-done.5.refs_3_) | copy-start | bytes 1622020
  52.7 6.1 %copy-start = (bf16[8,32,768]{2,1,0:T(8,128)(2,1)}, bf16[8,32,768]{2,1,0:T(8,128)(2,1)S(1)}, u32[]{:S(2)}) copy-start(bf16[8,32,768]{2,1,0:T(8,128)(2,1)S(1)} %all-to-all-done.refs_4_) | copy-start | bytes 1179652
  57.0 1.7 %copy-start.7 = (bf16[352,768]{1,0:T(8,128)(2,1)}, bf16[352,768]{1,0:T(8,128)(2,1)S(1)}, u32[]{:S(2)}) copy-start(bf16[352,768]{1,0:T(8,128)(2,1)S(1)} %collective-permute-done.4.refs_2_) | copy-start | bytes 1622020
  57.0 1.7 %collective-permute-start.6 = (bf16[8,32,768]{2,1,0:T(8,128)(2,1)S(1)}, bf16[8,32,768]{2,1,0:T(8,128)(2,1)S(1)}, u32[]{:S(2)}, u32[]{:S(2)}) collective-permute-start(bf16[8,32,768]{2,1,0:T(8,128)(2,1)S(1)} %all-to-all-done.refs_4_), channel_id=1, source_target_pairs={{0,4},{4,0},{8,12},{12,8},{16,20},{20,16},{24,28},{28,24},{32,36},... | collective-permute-start | bytes 1179656 | tf_op jit(solution)/shard_map/ppermute | solution.py:482
  58.7 0.7 copy-start.8
  64.0 6.7 %collective-permute-start.7 = (bf16[32,896]{1,0:T(8,128)(2,1)}, bf16[32,896]{1,0:T(8,128)(2,1)S(1)}, u32[]{:S(2)}, u32[]{:S(2)}) collective-permute-start(bf16[32,896]{1,0:T(8,128)(2,1)} %get-tuple-element.43.refs_0_), channel_id=1, source_target_pairs={{0,1},{1,2},{2,3},{3,0},{4,5},{5,6},{6,7},{7,4},{8,9},{9,10},{10,1... | collective-permute-start | bytes 172040 | tf_op jit(solution)/shard_map/ppermute | solution.py:432
  64.1 6.6 %collective-permute-start.8 = (bf16[32,896]{1,0:T(8,128)(2,1)}, bf16[32,896]{1,0:T(8,128)(2,1)S(1)}, u32[]{:S(2)}, u32[]{:S(2)}) collective-permute-start(bf16[32,896]{1,0:T(8,128)(2,1)} %get-tuple-element.43.refs_0_), channel_id=1, source_target_pairs={{0,2},{1,3},{2,0},{3,1},{4,6},{5,7},{6,4},{7,5},{8,10},{9,11},{10,... | collective-permute-start | bytes 172040 | tf_op jit(solution)/shard_map/ppermute | solution.py:432
  65.1 6.2 %collective-permute-start.9 = (bf16[32,896]{1,0:T(8,128)(2,1)}, bf16[32,896]{1,0:T(8,128)(2,1)S(1)}, u32[]{:S(2)}, u32[]{:S(2)}) collective-permute-start(bf16[32,896]{1,0:T(8,128)(2,1)} %get-tuple-element.43.refs_0_), channel_id=1, source_target_pairs={{0,3},{1,0},{2,1},{3,2},{4,7},{5,4},{6,5},{7,6},{8,11},{9,8},{10,9... | collective-permute-start | bytes 172040 | tf_op jit(solution)/shard_map/ppermute | solution.py:432
  70.7 0.6 copy-start.1
  70.7 0.6 copy-start.2
  71.3 0.6 copy-start.3

commit v4 on v3

--- a/solution.py
+++ b/solution.py
@@ -478,7 +478,7 @@
     two = lax.ppermute(one, "col", [(i, (i + 1) % NC) for i in range(NC)])
     pair(1)
     packed = [t_own, one, two, three_on]
-    own, biases[1], packed = lax.optimization_barrier((own, biases[1], packed))
+    own, biases[1] = lax.optimization_barrier((own, biases[1]))
     other = lax.ppermute(own, "atom", [(i, i ^ 1) for i in range(atoms)])
     for i in range(2, len(CHUNKS)):
         pair(i)

time: 75.1 us -> 73.4 us (0.977)
  the two profiles are of different devices: /device:TPU:112 before, /device:TPU:1 now
where the time goes in v4:
time: 73.4 us; the launch traced here: 72.8 us
  Pallas kernels  31 us (42%)
  starting transfers between devices  28 us (38%)
  waiting for transfers between devices  8.7 us (12%)
  local copies, waits for them, and re-layouts  3.56 us (5%)
  between operations  1.55 us (2%)
    pallas_call x6, Pallas kernels, call(): pl.pallas_call(body, in_specs=[pl.BlockSpec(memory_space=pltpu.SMEM if i...  31 us
    all_to_all x1, starting transfers between devices, local(): lax.all_to_all(jnp.broadcast_to(turned[None], (NZ, TOKS, C_S)), 'atom', 0...  8.48 us
    ppermute x3, starting transfers between devices, around(): lax.ppermute(array, axis, [(i, (i + s) % size) for i in range(size)])  4.44 us
    ppermute x1, starting transfers between devices, local(): other = lax.ppermute(own, 'atom', [(i, i ^ 1) for i in range(atoms)])  3.88 us
    ppermute x1, waiting for transfers between devices, local(): lax.ppermute(outer, 'atom', [(i, i + (1 if i % 2 else -1)) for i in range...  3.41 us
    ppermute x1, starting transfers between devices, local(): inner = lax.ppermute(inner, 'atom', [(i, i ^ 1) for i in range(atoms)])  3.33 us
    ppermute x3, waiting for transfers between devices, around(): lax.ppermute(array, axis, [(i, (i + s) % size) for i in range(size)])  3.1 us
    unnamed x22, local copies, waits for them, and re-layouts  2.8 us
  transfers between devices with their start and end apart: 11, of which 7 were waited for; matrix products, arithmetic and copies ran while one was open for 1% of the time, Pallas kernels for 22%

profile of v4, /device:TPU:1, one launch (start us, length us, event | category | flops | bytes accessed | tf_op | source)
XLA Modules:
  0.0 72.8 jit_solution(17475930078586735248)
XLA Ops:
  1.3 2.3 %atom_in.1 = (f32[512,128]{1,0:T(8,128)}, bf16[512,128]{1,0:T(8,128)(2,1)}, bf16[48,256]{1,0:T(8,128)(2,1)}, bf16[48,256]{1,0:T(8,128)(2,1)}) custom-call(s32[1]{0:T(128)S(6)} %copy.24.refs_0_, f32[3,512]{1,0:T(4,128)} %refs_1_.3, f32[3,128]{1,0:T(4,128)} %refs_2_.3, bf16[512,128]{1,0:T(8,128)(2,1)} %refs_3_.1, s32[1,32]{1,0:T(1,128)} %bitcast.5), custom_call_target="tpu_custom_call" | custom-call | flops 100000000 | bytes 1024 | tf_op jit(solution)/shard_map/atom_in/pallas_call | solution.py:124
  3.6 3.3 %collective-permute-start = (bf16[48,256]{1,0:T(8,128)(2,1)}, bf16[48,256]{1,0:T(8,128)(2,1)S(1)}, u32[]{:S(2)}, u32[]{:S(2)}) collective-permute-start(bf16[48,256]{1,0:T(8,128)(2,1)} %get-tuple-element.22), channel_id=1, source_target_pairs={{0,4},{4,0},{8,12},{12,8},{16,20},{20,16},{24,28},{28,24},{32,36},... | collective-permute-start | bytes 73736 | tf_op jit(solution)/shard_map/ppermute | solution.py:448
  6.9 1.9 %collective-permute-start.1 = (bf16[48,256]{1,0:T(8,128)(2,1)}, bf16[48,256]{1,0:T(8,128)(2,1)S(1)}, u32[]{:S(2)}, u32[]{:S(2)}) collective-permute-start(bf16[48,256]{1,0:T(8,128)(2,1)} %get-tuple-element.23), channel_id=1, source_target_pairs={{4,8},{8,4},{12,16},{16,12},{20,24},{24,20},{28,32},{32,28},{36,40... | collective-permute-start | bytes 73736 | tf_op jit(solution)/shard_map/ppermute | solution.py:447
  8.8 3.4 %collective-permute-done.1.refs_2_ = bf16[48,256]{1,0:T(8,128)(2,1)S(1)} collective-permute-done((bf16[48,256]{1,0:T(8,128)(2,1)}, bf16[48,256]{1,0:T(8,128)(2,1)S(1)}, u32[]{:S(2)}, u32[]{:S(2)}) %collective-permute-start.1) | collective-permute-done | bytes 24608 | tf_op jit(solution)/shard_map/ppermute | solution.py:447
  12.3 0.6 copy-done.10
  12.9 5.3 %atom_mid.1 = (f32[512,128]{1,0:T(8,128)}, f32[32,768]{1,0:T(8,128)}, bf16[32,768]{1,0:T(8,128)(2,1)}, bf16[352,768]{1,0:T(8,128)(2,1)}) custom-call(bf16[512,128]{1,0:T(8,128)(2,1)} %get-tuple-element.21.refs_0_, bf16[48,256]{1,0:T(8,128)(2,1)} %copy-done.9, bf16[48,256]{1,0:T(8,128)(2,1)} %copy-done.10, s32[1,32]{1,0:T(1,128)} %bitcast.6, ...), custom_call_target="tpu_custom_call" | custom-call | flops 1000000000 | bytes 1024 | tf_op jit(solution)/shard_map/atom_mid/pallas_call | solution.py:124
  18.2 1.5 %collective-permute-start.2 = (bf16[32,768]{1,0:T(8,128)(2,1)}, bf16[32,768]{1,0:T(8,128)(2,1)S(1)}, u32[]{:S(2)}, u32[]{:S(2)}) collective-permute-start(bf16[32,768]{1,0:T(8,128)(2,1)} %get-tuple-element.25), channel_id=1, source_target_pairs={{0,0},{1,64},{2,128},{3,192},{4,4},{5,68},{6,132},{7,196},{8,8},{9... | collective-permute-start | bytes 147464 | tf_op jit(solution)/shard_map/ppermute | solution.py:470
  19.6 5.1 %pair.2 = (bf16[32,512,128]{2,1,0:T(8,128)(2,1)}, bf16[4,1,32,512]{3,2,1,0:T(8,128)(2,1)}) custom-call(bf16[32,512,128]{2,1,0:T(8,128)(2,1)} %refs_0_.4, bf16[128,512]{1,0:T(8,128)(2,1)} %refs_1_.5, bf16[256,128]{1,0:T(8,128)(2,1)} %refs_2_.5, bf16[16,128]{1,0:T(8,128)(2,1)} %bitcast.11), custom_call_target="tpu_custom_call" | custom-call | flops 3000000000 | bytes 1024 | tf_op jit(solution)/shard_map/pair/pallas_call | solution.py:124
  24.7 1.3 %collective-permute-start.3 = (bf16[352,768]{1,0:T(8,128)(2,1)S(1)}, bf16[352,768]{1,0:T(8,128)(2,1)S(1)}, u32[]{:S(2)}, u32[]{:S(2)}) collective-permute-start(bf16[352,768]{1,0:T(8,128)(2,1)S(1)} %copy-done.4), channel_id=1, source_target_pairs={{0,1},{1,2},{2,3},{3,0},{4,5},{5,6},{6,7},{7,4},{8,9},{9,10},{10,1... | collective-permute-start | bytes 1622024 | tf_op jit(solution)/shard_map/ppermute | solution.py:476
  26.0 2.7 %collective-permute-start.5 = (bf16[352,768]{1,0:T(8,128)(2,1)S(1)}, bf16[352,768]{1,0:T(8,128)(2,1)S(1)}, u32[]{:S(2)}, u32[]{:S(2)}) collective-permute-start(bf16[352,768]{1,0:T(8,128)(2,1)S(1)} %copy-done.4), channel_id=1, source_target_pairs={{0,3},{1,0},{2,1},{3,2},{4,7},{5,4},{6,5},{7,6},{8,11},{9,8},{10,9... | collective-permute-start | bytes 1622024 | tf_op jit(solution)/shard_map/ppermute | solution.py:477
  28.8 0.8 %broadcast_in_dim.2 = bf16[8,32,768]{2,1,0:T(8,128)(2,1)} broadcast(bf16[32,768]{1,0:T(8,128)(2,1)S(1)} %collective-permute-done.2), dimensions={1,2} | broadcast | bytes 442368 | tf_op jit(solution)/shard_map/broadcast_in_dim | solution.py:474
  29.5 8.5 %all-to-all-start = ((bf16[8,32,768]{2,1,0:T(8,128)(2,1)}), bf16[8,32,768]{2,1,0:T(8,128)(2,1)S(1)}, u32[]{:S(2)}, u32[]{:S(2)}) async-start(bf16[8,32,768]{2,1,0:T(8,128)(2,1)} %broadcast_in_dim.2), calls=%async_computation | async-start | bytes 786432 | tf_op jit(solution)/shard_map/all_to_all | solution.py:473
  38.8 11.1 %pair.3 = (bf16[32,512,128]{2,1,0:T(8,128)(2,1)}, bf16[4,3,32,512]{3,2,1,0:T(8,128)(2,1)}) custom-call(bf16[32,512,128]{2,1,0:T(8,128)(2,1)} %refs_0_.4, bf16[128,512]{1,0:T(8,128)(2,1)} %refs_1_.5, bf16[256,128]{1,0:T(8,128)(2,1)} %refs_2_.5, bf16[16,128]{1,0:T(8,128)(2,1)} %bitcast.12, ...), custom_call_target="tpu_custom_call", output_to_operand_aliasing={{0}: (4, {})} | custom-call | flops 8999999488 | bytes 1024 | tf_op jit(solution)/shard_map/pair/pallas_call | solution.py:124
  50.4 3.9 %collective-permute-start.6 = (bf16[8,32,768]{2,1,0:T(8,128)(2,1)S(1)}, bf16[8,32,768]{2,1,0:T(8,128)(2,1)S(1)}, u32[]{:S(2)}, u32[]{:S(2)}) collective-permute-start(bf16[8,32,768]{2,1,0:T(8,128)(2,1)S(1)} %all-to-all-done.refs_4_), channel_id=1, source_target_pairs={{0,4},{4,0},{8,12},{12,8},{16,20},{20,16},{24,28},{28,24},{32,36},... | collective-permute-start | bytes 1179656 | tf_op jit(solution)/shard_map/ppermute | solution.py:482
  54.3 1.3 %collective-permute-done.6.refs_5_ = bf16[8,32,768]{2,1,0:T(8,128)(2,1)S(1)} collective-permute-done((bf16[8,32,768]{2,1,0:T(8,128)(2,1)S(1)}, bf16[8,32,768]{2,1,0:T(8,128)(2,1)S(1)}, u32[]{:S(2)}, u32[]{:S(2)}) %collective-permute-start.6) | collective-permute-done | bytes 393248 | tf_op jit(solution)/shard_map/ppermute | solution.py:482
  55.6 0.7 %copy-done.8 = bf16[8,32,768]{2,1,0:T(8,128)(2,1)} copy-done((bf16[8,32,768]{2,1,0:T(8,128)(2,1)}, bf16[8,32,768]{2,1,0:T(8,128)(2,1)S(1)}, u32[]{:S(2)}) %copy-start.8) | copy-done | bytes 393240
  56.4 0.8 %copy-done.7 = bf16[352,768]{1,0:T(8,128)(2,1)} copy-done((bf16[352,768]{1,0:T(8,128)(2,1)}, bf16[352,768]{1,0:T(8,128)(2,1)S(1)}, u32[]{:S(2)}) %copy-start.7) | copy-done | bytes 540696
  57.2 4.5 %attention.1 = (bf16[32,896]{1,0:T(8,128)(2,1)}, bf16[4,192,128]{2,1,0:T(8,128)(2,1)}) custom-call(bf16[352,768]{1,0:T(8,128)(2,1)} %get-tuple-element.28.refs_0_, bf16[352,768]{1,0:T(8,128)(2,1)} %copy-done.5, bf16[352,768]{1,0:T(8,128)(2,1)} %copy-done.7, bf16[352,768]{1,0:T(8,128)(2,1)} %copy-done.6, bf16[8,32,768]{2,1,0:T(8,128)(2,1)} %copy-done, ...), custom_call_target="tpu_custom_call" | custom-call | flops 3000000000 | bytes 1024 | tf_op jit(solution)/shard_map/attention/pallas_call | solution.py:124
  61.7 0.9 %collective-permute-start.7 = (bf16[32,896]{1,0:T(8,128)(2,1)}, bf16[32,896]{1,0:T(8,128)(2,1)S(1)}, u32[]{:S(2)}, u32[]{:S(2)}) collective-permute-start(bf16[32,896]{1,0:T(8,128)(2,1)} %get-tuple-element.35.refs_0_), channel_id=1, source_target_pairs={{0,1},{1,2},{2,3},{3,0},{4,5},{5,6},{6,7},{7,4},{8,9},{9,10},{10,1... | collective-permute-start | bytes 172040 | tf_op jit(solution)/shard_map/ppermute | solution.py:432
  62.6 3.2 %collective-permute-start.8 = (bf16[32,896]{1,0:T(8,128)(2,1)}, bf16[32,896]{1,0:T(8,128)(2,1)S(1)}, u32[]{:S(2)}, u32[]{:S(2)}) collective-permute-start(bf16[32,896]{1,0:T(8,128)(2,1)} %get-tuple-element.35.refs_0_), channel_id=1, source_target_pairs={{0,2},{1,3},{2,0},{3,1},{4,6},{5,7},{6,4},{7,5},{8,10},{9,11},{10,... | collective-permute-start | bytes 172040 | tf_op jit(solution)/shard_map/ppermute | solution.py:432
  66.3 2.2 %collective-permute-done.8.refs_2_ = bf16[32,896]{1,0:T(8,128)(2,1)S(1)} collective-permute-done((bf16[32,896]{1,0:T(8,128)(2,1)}, bf16[32,896]{1,0:T(8,128)(2,1)S(1)}, u32[]{:S(2)}, u32[]{:S(2)}) %collective-permute-start.8) | collective-permute-done | bytes 57376 | tf_op jit(solution)/shard_map/ppermute | solution.py:432
  68.6 0.7 collective-permute-done.9.refs_3_
  69.3 0.6 copy-done.3
  69.9 2.7 %final.1 = bf16[512,128]{1,0:T(8,128)(2,1)} custom-call(bf16[32,896]{1,0:T(8,128)(2,1)} %get-tuple-element.35.refs_0_, bf16[32,896]{1,0:T(8,128)(2,1)} %copy-done.1, bf16[32,896]{1,0:T(8,128)(2,1)} %copy-done.2, bf16[32,896]{1,0:T(8,128)(2,1)} %copy-done.3, f32[32,768]{1,0:T(8,128)} %get-tuple-element.36.refs_4_, f32[512,128]{1,0:T(8,128)} %get-tuple-element.37.refs_5_, ...), custom_call_target="tpu_custom_call" | custom-call | flops 100000000 | bytes 1024 | tf_op jit(solution)/shard_map/final/pallas_call | solution.py:124
  (27 shorter events, 1.9 us)
Async XLA Ops:
  3.6 5.2 %collective-permute-start = (bf16[48,256]{1,0:T(8,128)(2,1)}, bf16[48,256]{1,0:T(8,128)(2,1)S(1)}, u32[]{:S(2)}, u32[]{:S(2)}) collective-permute-start(bf16[48,256]{1,0:T(8,128)(2,1)} %get-tuple-element.22), channel_id=1, source_target_pairs={{0,4},{4,0},{8,12},{12,8},{16,20},{20,16},{24,28},{28,24},{32,36},... | collective-permute-start | bytes 73736 | tf_op jit(solution)/shard_map/ppermute | solution.py:448
  6.9 5.3 %collective-permute-start.1 = (bf16[48,256]{1,0:T(8,128)(2,1)}, bf16[48,256]{1,0:T(8,128)(2,1)S(1)}, u32[]{:S(2)}, u32[]{:S(2)}) collective-permute-start(bf16[48,256]{1,0:T(8,128)(2,1)} %get-tuple-element.23), channel_id=1, source_target_pairs={{4,8},{8,4},{12,16},{16,12},{20,24},{24,20},{28,32},{32,28},{36,40... | collective-permute-start | bytes 73736 | tf_op jit(solution)/shard_map/ppermute | solution.py:447
  8.8 3.4 %copy-start.9 = (bf16[48,256]{1,0:T(8,128)(2,1)}, bf16[48,256]{1,0:T(8,128)(2,1)S(1)}, u32[]{:S(2)}) copy-start(bf16[48,256]{1,0:T(8,128)(2,1)S(1)} %collective-permute-done.refs_1_) | copy-start | bytes 73732
  12.3 0.6 copy-start.10
  18.2 6.5 %collective-permute-start.2 = (bf16[32,768]{1,0:T(8,128)(2,1)}, bf16[32,768]{1,0:T(8,128)(2,1)S(1)}, u32[]{:S(2)}, u32[]{:S(2)}) collective-permute-start(bf16[32,768]{1,0:T(8,128)(2,1)} %get-tuple-element.25), channel_id=1, source_target_pairs={{0,0},{1,64},{2,128},{3,192},{4,4},{5,68},{6,132},{7,196},{8,8},{9... | collective-permute-start | bytes 147464 | tf_op jit(solution)/shard_map/ppermute | solution.py:470
  19.6 5.1 %copy-start.4 = (bf16[352,768]{1,0:T(8,128)(2,1)S(1)}, bf16[352,768]{1,0:T(8,128)(2,1)}, u32[]{:S(2)}) copy-start(bf16[352,768]{1,0:T(8,128)(2,1)} %get-tuple-element.28.refs_0_) | copy-start | bytes 1622020
  24.7 13.7 %collective-permute-start.3 = (bf16[352,768]{1,0:T(8,128)(2,1)S(1)}, bf16[352,768]{1,0:T(8,128)(2,1)S(1)}, u32[]{:S(2)}, u32[]{:S(2)}) collective-permute-start(bf16[352,768]{1,0:T(8,128)(2,1)S(1)} %copy-done.4), channel_id=1, source_target_pairs={{0,1},{1,2},{2,3},{3,0},{4,5},{5,6},{6,7},{7,4},{8,9},{9,10},{10,1... | collective-permute-start | bytes 1622024 | tf_op jit(solution)/shard_map/ppermute | solution.py:476
  26.0 28.3 %collective-permute-start.5 = (bf16[352,768]{1,0:T(8,128)(2,1)S(1)}, bf16[352,768]{1,0:T(8,128)(2,1)S(1)}, u32[]{:S(2)}, u32[]{:S(2)}) collective-permute-start(bf16[352,768]{1,0:T(8,128)(2,1)S(1)} %copy-done.4), channel_id=1, source_target_pairs={{0,3},{1,0},{2,1},{3,2},{4,7},{5,4},{6,5},{7,6},{8,11},{9,8},{10,9... | collective-permute-start | bytes 1622024 | tf_op jit(solution)/shard_map/ppermute | solution.py:477
  29.5 20.9 %all-to-all-start = ((bf16[8,32,768]{2,1,0:T(8,128)(2,1)}), bf16[8,32,768]{2,1,0:T(8,128)(2,1)S(1)}, u32[]{:S(2)}, u32[]{:S(2)}) async-start(bf16[8,32,768]{2,1,0:T(8,128)(2,1)} %broadcast_in_dim.2), calls=%async_computation | async-start | bytes 786432 | tf_op jit(solution)/shard_map/all_to_all | solution.py:473
  38.4 11.5 %copy-start.5 = (bf16[352,768]{1,0:T(8,128)(2,1)}, bf16[352,768]{1,0:T(8,128)(2,1)S(1)}, u32[]{:S(2)}) copy-start(bf16[352,768]{1,0:T(8,128)(2,1)S(1)} %collective-permute-done.3.refs_1_) | copy-start | bytes 1622020
  38.4 17.2 %collective-permute-start.4 = (bf16[352,768]{1,0:T(8,128)(2,1)S(1)}, bf16[352,768]{1,0:T(8,128)(2,1)S(1)}, u32[]{:S(2)}, u32[]{:S(2)}) collective-permute-start(bf16[352,768]{1,0:T(8,128)(2,1)S(1)} %collective-permute-done.3.refs_1_), channel_id=1, source_target_pairs={{0,1},{1,2},{2,3},{3,0},{4,5},{5,6},{6,7},{7,4},{8,9},{9,10},{10,1... | collective-permute-start | bytes 1622024 | tf_op jit(solution)/shard_map/ppermute | solution.py:478
  50.4 5.2 %copy-start = (bf16[8,32,768]{2,1,0:T(8,128)(2,1)}, bf16[8,32,768]{2,1,0:T(8,128)(2,1)S(1)}, u32[]{:S(2)}) copy-start(bf16[8,32,768]{2,1,0:T(8,128)(2,1)S(1)} %all-to-all-done.refs_4_) | copy-start | bytes 1179652
  50.4 5.2 %collective-permute-start.6 = (bf16[8,32,768]{2,1,0:T(8,128)(2,1)S(1)}, bf16[8,32,768]{2,1,0:T(8,128)(2,1)S(1)}, u32[]{:S(2)}, u32[]{:S(2)}) collective-permute-start(bf16[8,32,768]{2,1,0:T(8,128)(2,1)S(1)} %all-to-all-done.refs_4_), channel_id=1, source_target_pairs={{0,4},{4,0},{8,12},{12,8},{16,20},{20,16},{24,28},{28,24},{32,36},... | collective-permute-start | bytes 1179656 | tf_op jit(solution)/shard_map/ppermute | solution.py:482
  54.3 1.4 %copy-start.6 = (bf16[352,768]{1,0:T(8,128)(2,1)}, bf16[352,768]{1,0:T(8,128)(2,1)S(1)}, u32[]{:S(2)}) copy-start(bf16[352,768]{1,0:T(8,128)(2,1)S(1)} %collective-permute-done.5.refs_3_) | copy-start | bytes 1622020
  55.6 0.7 %copy-start.8 = (bf16[8,32,768]{2,1,0:T(8,128)(2,1)}, bf16[8,32,768]{2,1,0:T(8,128)(2,1)S(1)}, u32[]{:S(2)}) copy-start(bf16[8,32,768]{2,1,0:T(8,128)(2,1)S(1)} %collective-permute-done.6.refs_5_) | copy-start | bytes 1179652
  56.4 0.8 %copy-start.7 = (bf16[352,768]{1,0:T(8,128)(2,1)}, bf16[352,768]{1,0:T(8,128)(2,1)S(1)}, u32[]{:S(2)}) copy-start(bf16[352,768]{1,0:T(8,128)(2,1)S(1)} %collective-permute-done.4.refs_2_) | copy-start | bytes 1622020
  61.7 4.6 %collective-permute-start.7 = (bf16[32,896]{1,0:T(8,128)(2,1)}, bf16[32,896]{1,0:T(8,128)(2,1)S(1)}, u32[]{:S(2)}, u32[]{:S(2)}) collective-permute-start(bf16[32,896]{1,0:T(8,128)(2,1)} %get-tuple-element.35.refs_0_), channel_id=1, source_target_pairs={{0,1},{1,2},{2,3},{3,0},{4,5},{5,6},{6,7},{7,4},{8,9},{9,10},{10,1... | collective-permute-start | bytes 172040 | tf_op jit(solution)/shard_map/ppermute | solution.py:432
  62.6 6.0 %collective-permute-start.8 = (bf16[32,896]{1,0:T(8,128)(2,1)}, bf16[32,896]{1,0:T(8,128)(2,1)S(1)}, u32[]{:S(2)}, u32[]{:S(2)}) collective-permute-start(bf16[32,896]{1,0:T(8,128)(2,1)} %get-tuple-element.35.refs_0_), channel_id=1, source_target_pairs={{0,2},{1,3},{2,0},{3,1},{4,6},{5,7},{6,4},{7,5},{8,10},{9,11},{10,... | collective-permute-start | bytes 172040 | tf_op jit(solution)/shard_map/ppermute | solution.py:432
  65.8 3.5 %collective-permute-start.9 = (bf16[32,896]{1,0:T(8,128)(2,1)}, bf16[32,896]{1,0:T(8,128)(2,1)S(1)}, u32[]{:S(2)}, u32[]{:S(2)}) collective-permute-start(bf16[32,896]{1,0:T(8,128)(2,1)} %get-tuple-element.35.refs_0_), channel_id=1, source_target_pairs={{0,3},{1,0},{2,1},{3,2},{4,7},{5,4},{6,5},{7,6},{8,11},{9,8},{10,9... | collective-permute-start | bytes 172040 | tf_op jit(solution)/shard_map/ppermute | solution.py:432
  66.3 2.9 %copy-start.1 = (bf16[32,896]{1,0:T(8,128)(2,1)}, bf16[32,896]{1,0:T(8,128)(2,1)S(1)}, u32[]{:S(2)}) copy-start(bf16[32,896]{1,0:T(8,128)(2,1)S(1)} %collective-permute-done.7.refs_1_) | copy-start | bytes 172036
  68.6 0.7 %copy-start.2 = (bf16[32,896]{1,0:T(8,128)(2,1)}, bf16[32,896]{1,0:T(8,128)(2,1)S(1)}, u32[]{:S(2)}) copy-start(bf16[32,896]{1,0:T(8,128)(2,1)S(1)} %collective-permute-done.8.refs_2_) | copy-start | bytes 172036
  69.3 0.6 copy-start.3
